TPU v7x, 512 devices: a whole 4x8x8 slice. The times are simulated.
512 devices in a mesh: ctx: 32 (over x, y), tp: 16 (over z, core).
Axes of the slice: x: 4, y: 8, z: 8, core: 2. Of those that a mesh axis runs over, the one named last changes fastest.
Arguments:
- prefix_x: bfloat16 [8192, 8192], P('ctx', 'tp'), may hold values from -6 to 6
- prefix_z: bfloat16 [8192, 8192], P('ctx', 'tp'), may hold values from -6 to 6
- prefix_bc: bfloat16 [8192, 256], P(('ctx', 'tp')), may hold values from -6 to 6
- prefix_dt: float32 [128, 8192], P('tp', 'ctx'), may hold values from -6 to 6
- branch_x: bfloat16 [8192, 8192], P('ctx', 'tp'), may hold values from -6 to 6
- branch_z: bfloat16 [8192, 8192], P('ctx', 'tp'), may hold values from -6 to 6
- branch_bc: bfloat16 [8192, 256], P(('ctx', 'tp')), may hold values from -6 to 6
- branch_dt: float32 [128, 8192], P('tp', 'ctx'), may hold values from -6 to 6
- conv_x: bfloat16 [4, 8192], P(None, 'tp'), may hold values from -3 to 3
- conv_bc: bfloat16 [4, 256], replicated, may hold values from -3 to 3
- decay_rate: float32 [128], P('tp'), may hold values from 2.4414063e-05 to 0.03
- skip: float32 [128], P('tp'), may hold values from 0.5 to 1.5
- norm_gain: float32 [8192], P('tp'), may hold values from 0.5 to 1.5
- bound_pos: int32 [8], replicated, may hold values from 0 to 8191
- branch_owner: int32 [64], replicated, may hold values from 0 to 31, as said below
- branch_parent: int32 [64], replicated, may hold values from 0 to 7
- branch_len: int32 [64], replicated, may hold values from 1 to 255, as said below
Outputs:
- prefix_out: bfloat16 [8192, 8192], P('ctx', 'tp')
- branch_out: bfloat16 [8192, 8192], P('ctx', 'tp')
Inputs may be any that keep to these rules, and one draw needn't show every extreme that they name: `branch_owner`: every block index 0 to 31 holds exactly 2 branches. `branch_len`: the branches of one block have lengths that sum to at most 256; in every draw some block's sum is exactly 256, and some branch has exactly 255 rows.
All inputs are finite; a program needn't handle non-finite values.
Results may differ from a plain program's by a relative error of at most 0.0034.
Values may be sent and summed in bfloat16 or wider, within the bound.
No kernel may reach another device: no remote copies, remote signals or barrier semaphores. Data moves between devices by JAX's collectives and lax.ppermute only.
A program may use at most 64 MiB of HBM per device.

v0:
```python
import jax
import jax.numpy as jnp
from jax import lax
from jax.sharding import PartitionSpec as P

NORM_GROUP = 8192
BR_PER = 2


EPSILON = 1e-05


def passed_along(value, axis, steps):
    count = lax.axis_size(axis)
    first, last = (max(0, -steps), min(count, count - steps))
    return lax.ppermute(value, axis, [(source, source + steps) for source in range(first, last)])


def conv_silu(lagged, weights):
    summed = weights[0].astype(jnp.float32)[None, :] * lagged[0].astype(jnp.float32)
    for tap_index in range(1, len(lagged)):
        summed = summed + weights[tap_index].astype(jnp.float32)[None, :] * lagged[
            tap_index
        ].astype(jnp.float32)
    return jax.nn.silu(summed).astype(jnp.bfloat16)


def split_conv(convolved, channels, head_count):
    length = convolved.shape[0]
    state_size = (convolved.shape[1] - channels) // 2
    values = convolved[:, :channels].reshape(length, head_count, channels // head_count)
    return (
        values,
        convolved[:, channels : channels + state_size],
        convolved[:, channels + state_size :],
    )


def decays(raw_steps, rates):
    step_size = jax.nn.softplus(raw_steps)
    log_decay = -rates[:, None] * step_size
    return (step_size, log_decay, jnp.cumsum(log_decay, axis=1))


def intra_block(values, b_rows, c_rows, step_size, cumulative, causal_mask):
    scores = jnp.dot(c_rows, b_rows.T, preferred_element_type=jnp.float32)
    exponent = jnp.where(causal_mask[None], cumulative[:, :, None] - cumulative[:, None, :], 0.0)
    mixing = jnp.where(
        causal_mask[None], scores[None] * jnp.exp(exponent) * step_size[:, None, :], 0.0
    ).astype(jnp.bfloat16)
    return jnp.einsum("hts,shp->thp", mixing, values, preferred_element_type=jnp.float32)


def local_states(values, b_rows, step_size, cumulative, positions):
    length = cumulative.shape[1]
    clipped = jnp.clip(positions, 0, length - 1)
    decay_end = jnp.take(cumulative, clipped, axis=1)
    row_index = jnp.arange(length, dtype=jnp.int32)
    inside = row_index[None, :] <= positions[:, None]
    exponent = jnp.where(inside[:, None, :], decay_end.T[:, :, None] - cumulative[None], 0.0)
    weight = jnp.where(inside[:, None, :], jnp.exp(exponent) * step_size[None], 0.0)
    weighted = (
        jnp.transpose(weight, (0, 2, 1))[:, :, :, None] * values[None].astype(jnp.float32)
    ).astype(jnp.bfloat16)
    return jnp.einsum("jshp,sn->jhpn", weighted, b_rows, preferred_element_type=jnp.float32)


def from_state(c_rows, state, weight):
    result = jnp.einsum(
        "tn,hpn->thp", c_rows.astype(jnp.float32), state, precision=lax.Precision.HIGHEST
    )
    return result * weight.T[:, :, None]


def finish(mixed_out, values, skip, gate_rows, gain):
    length = mixed_out.shape[0]
    mixed_out = mixed_out + skip[None, :, None] * values.astype(jnp.float32)
    gated = mixed_out.reshape(length, -1) * jax.nn.silu(gate_rows.astype(jnp.float32))
    partial_squares = jnp.sum(gated * gated, axis=1, keepdims=True)
    total_squares = lax.psum(partial_squares, "tp")
    factor = lax.rsqrt(total_squares / NORM_GROUP + EPSILON)
    return (gated * factor * gain[None, :]).astype(jnp.bfloat16)


def layout(owner_index, branch_owner, branch_parent, branch_len, length):
    owned = (branch_owner == owner_index).astype(jnp.int32)
    owned_rank = jnp.cumsum(owned) - 1
    owned_lengths = owned * branch_len
    starts = jnp.cumsum(owned_lengths) - owned_lengths
    branch_slot = jnp.arange(BR_PER, dtype=jnp.int32)
    chosen = owned[None, :] * (owned_rank[None, :] == branch_slot[:, None]).astype(jnp.int32)
    segment_length = jnp.sum(chosen * branch_len[None, :], axis=1)
    segment_start = jnp.sum(chosen * starts[None, :], axis=1)
    parents = jnp.sum(chosen * branch_parent[None, :], axis=1)
    row_index = jnp.arange(length, dtype=jnp.int32)
    inside = (
        (row_index[None, :] >= segment_start[:, None])
        & (row_index[None, :] < (segment_start + segment_length)[:, None])
    ).astype(jnp.int32)
    live_count = jnp.sum(inside, axis=0)
    segment = jnp.sum(inside * branch_slot[:, None], axis=0) + BR_PER * (1 - live_count)
    offset = row_index - jnp.sum(inside * segment_start[:, None], axis=0)
    return (segment, offset, live_count > 0, parents)


def branch_block(
    joined_rows,
    gate_rows,
    raw_steps,
    all_states,
    all_tails,
    weights,
    rates,
    skip,
    gain,
    owner_index,
    branch_owner,
    branch_parent,
    branch_len,
):
    length, row_width = joined_rows.shape
    channels = gate_rows.shape[1]
    head_count = rates.shape[0]
    tail_count = weights.shape[0] - 1
    segment, offset, live_rows, parents = layout(
        owner_index, branch_owner, branch_parent, branch_len, length
    )
    seed_states = jnp.take(all_states, parents, axis=0)
    tail_rows = jnp.take(all_tails, parents, axis=0).reshape(-1, row_width).astype(jnp.bfloat16)
    column = jnp.arange(tail_rows.shape[0], dtype=jnp.int32)
    column_segment = column // tail_count
    column_row = column % tail_count
    lagged = []
    for tap_index in range(tail_count + 1):
        shift_rows = tail_count - tap_index
        if shift_rows == 0:
            lagged.append(joined_rows)
        else:
            shifted = jnp.concatenate(
                [
                    jnp.zeros((shift_rows, row_width), jnp.bfloat16),
                    joined_rows[: length - shift_rows],
                ],
                axis=0,
            )
            local_rows = jnp.where(
                (offset >= shift_rows)[:, None], shifted, jnp.zeros_like(shifted)
            )
            picker = (
                (segment[:, None] == column_segment[None, :])
                & (offset[:, None] < shift_rows)
                & (column_row[None, :] == tail_count - shift_rows + offset[:, None])
            ).astype(jnp.bfloat16)
            tail_part = jnp.dot(picker, tail_rows, preferred_element_type=jnp.float32).astype(
                jnp.bfloat16
            )
            lagged.append(local_rows + tail_part)
    values, b_rows, c_rows = split_conv(conv_silu(lagged, weights), channels, head_count)
    step_size, log_decay, cumulative = decays(raw_steps, rates)
    row_index = jnp.arange(length, dtype=jnp.int32)
    causal_mask = (
        (segment[:, None] == segment[None, :])
        & live_rows[:, None]
        & (row_index[None, :] <= row_index[:, None])
    )
    mixed_out = intra_block(values, b_rows, c_rows, step_size, cumulative, causal_mask)
    first_rows = jnp.clip(row_index - offset, 0, length - 1)
    start_log = jnp.take(cumulative - log_decay, first_rows, axis=1)
    seed_weight = jnp.where(
        live_rows[None, :], jnp.exp(jnp.where(live_rows[None, :], cumulative - start_log, 0.0)), 0.0
    )
    for branch_slot in range(seed_states.shape[0]):
        portion = from_state(c_rows, seed_states[branch_slot], seed_weight)
        mixed_out = mixed_out + jnp.where((segment == branch_slot)[:, None, None], portion, 0.0)
    result = finish(mixed_out, values, skip, gate_rows, gain)
    return jnp.where(live_rows[:, None], result, jnp.zeros_like(result))


def body(
    prefix_x,
    prefix_z,
    prefix_bc,
    prefix_dt,
    branch_x,
    branch_z,
    branch_bc,
    branch_dt,
    conv_x,
    conv_bc,
    decay_rate,
    skip,
    norm_gain,
    bound_pos,
    branch_owner,
    branch_parent,
    branch_len,
):
    prefix_gathered, branch_gathered = (
        lax.all_gather(prefix_bc, "tp", axis=0, tiled=True),
        lax.all_gather(branch_bc, "tp", axis=0, tiled=True),
    )
    length = prefix_x.shape[0]
    channels = prefix_x.shape[1]
    head_count = decay_rate.shape[0]
    weights = jnp.concatenate([conv_x, conv_bc], axis=1)
    tail_count = weights.shape[0] - 1
    joined_rows = jnp.concatenate([prefix_x, prefix_gathered], axis=1)
    before = passed_along(joined_rows[length - tail_count :], "ctx", 1)
    extended = jnp.concatenate([before, joined_rows], axis=0)
    lagged = [extended[tap_index : tap_index + length] for tap_index in range(tail_count + 1)]
    values, b_rows, c_rows = split_conv(conv_silu(lagged, weights), channels, head_count)
    step_size, log_decay, cumulative = decays(prefix_dt, decay_rate)
    row_index = jnp.arange(length, dtype=jnp.int32)
    causal_mask = row_index[None, :] <= row_index[:, None]
    mixed_out = intra_block(values, b_rows, c_rows, step_size, cumulative, causal_mask)
    owner_index = lax.axis_index("ctx")
    local_at = jnp.where(bound_pos // length == owner_index, bound_pos - owner_index * length, -1)
    positions = jnp.concatenate([local_at, jnp.full((1,), length - 1, jnp.int32)])
    states = local_states(values, b_rows, step_size, cumulative, positions)
    bound_count = bound_pos.shape[0]
    end_state = states[bound_count]
    end_decay = jnp.exp(cumulative[:, -1])

    def carry_step(unused, state):
        return passed_along(end_decay[:, None, None] * state + end_state, "ctx", 1)

    entering = lax.fori_loop(0, lax.axis_size("ctx") - 1, carry_step, jnp.zeros_like(end_state))
    mixed_out = mixed_out + from_state(c_rows, entering, jnp.exp(cumulative))
    prefix_out = finish(mixed_out, values, skip, prefix_z, norm_gain)
    held_here = local_at >= 0
    decay_at = jnp.exp(jnp.take(cumulative, jnp.clip(local_at, 0, length - 1), axis=1))
    candidate = jnp.where(
        held_here[:, None, None, None],
        decay_at.T[:, :, None, None] * entering[None] + states[:bound_count],
        0.0,
    )
    tail_index = (local_at[:, None] + 1 + jnp.arange(tail_count, dtype=jnp.int32)[None, :]).reshape(
        -1
    )
    held_rows = jnp.repeat(held_here, tail_count)
    picker = (
        (jnp.arange(length + tail_count, dtype=jnp.int32)[None, :] == tail_index[:, None])
        & held_rows[:, None]
    ).astype(jnp.bfloat16)
    tail_rows = jnp.dot(picker, extended, preferred_element_type=jnp.float32).reshape(
        bound_count, tail_count, -1
    )
    all_states, all_tails = lax.psum((candidate, tail_rows), "ctx")
    branch_joined = jnp.concatenate([branch_x, branch_gathered], axis=1)
    branch_out = branch_block(
        branch_joined,
        branch_z,
        branch_dt,
        all_states,
        all_tails,
        weights,
        decay_rate,
        skip,
        norm_gain,
        owner_index,
        branch_owner,
        branch_parent,
        branch_len,
    )
    return (prefix_out, branch_out)


def solution(mesh):
    in_specs = (
        P("ctx", "tp"),
        P("ctx", "tp"),
        P(("ctx", "tp"), None),
        P("tp", "ctx"),
        P("ctx", "tp"),
        P("ctx", "tp"),
        P(("ctx", "tp"), None),
        P("tp", "ctx"),
        P(None, "tp"),
        P(),
        P("tp"),
        P("tp"),
        P("tp"),
        P(),
        P(),
        P(),
        P(),
    )
    out_specs = (P("ctx", "tp"), P("ctx", "tp"))
    return jax.shard_map(body, mesh=mesh, in_specs=in_specs, out_specs=out_specs, check_vma=False)
```

profile of v0, /device:TPU:1, one launch (start us, length us, event | category | flops | bytes accessed | tf_op | source)
XLA Modules:
  0.0 639.3 jit_solution(6690966973142288056)
XLA Ops:
  8.3 25.1 %all_gather.6 = bf16[256,256]{1,0:T(8,128)(2,1)S(1)} all-gather(bf16[16,256]{1,0:T(8,128)(2,1)} %param.21), channel_id=1, replica_groups=mesh['ctx'=32,'tp'=16] {'tp'}, dimensions={0}, use_global_device_ids=true | all-gather | bytes 139264 | tf_op jit(solution)/shard_map/all_gather | solution.py:199
  50.8 14.8 %all_gather.7 = bf16[256,256]{1,0:T(8,128)(2,1)S(1)} all-gather(bf16[16,256]{1,0:T(8,128)(2,1)S(1)} %copy-done.27), channel_id=1, replica_groups=mesh['ctx'=32,'tp'=16] {'tp'}, dimensions={0}, use_global_device_ids=true | all-gather | bytes 139264 | tf_op jit(solution)/shard_map/all_gather | solution.py:200
  74.3 305.5 %while.10 = (s32[]{:T(128)}, f32[8,64,128]{2,1,0:T(8,128)S(1)}, f32[8]{0:T(128)}, f32[8,64,128]{2,1,0:T(8,128)S(1)}, s32[]{:T(128)}) while((s32[]{:T(128)}, f32[8,64,128]{2,1,0:T(8,128)S(1)}, f32[8]{0:T(128)}, f32[8,64,128]{2,1,0:T(8,128)S(1)}, s32[]{:T(128)}) %tuple.49), condition=%wide.region_3.4_spmd, body=%wide.region_2.3_spmd.sunk | while | flops 131074 | bytes 1835141 | solution.py:227
  78.2 5.5 collective-permute-done
  84.4 4.1 collective-permute-start
  88.6 4.6 collective-permute-done
  93.9 4.1 collective-permute-start
  102.4 4.1 collective-permute-start
  110.5 3.8 collective-permute-start
  118.3 4.4 collective-permute-start
  126.8 5.3 collective-permute-start
  136.1 5.0 collective-permute-start
  145.1 5.0 collective-permute-start
  150.2 4.0 collective-permute-done
  154.9 5.5 collective-permute-start
  160.3 5.0 collective-permute-done
  166.1 5.9 collective-permute-start
  172.0 6.0 collective-permute-done
  178.7 5.4 collective-permute-start
  184.0 4.8 collective-permute-done
  189.5 5.1 collective-permute-start
  199.0 4.2 collective-permute-start
  207.2 5.3 collective-permute-start
  216.5 5.3 collective-permute-start
  225.8 5.5 collective-permute-start
  235.3 5.0 collective-permute-start
  244.3 5.2 collective-permute-start
  249.5 4.2 collective-permute-done
  254.5 5.3 collective-permute-start
  259.8 5.0 collective-permute-done
  265.5 4.3 collective-permute-start
  269.9 5.6 collective-permute-done
  276.2 4.1 collective-permute-start
  280.4 5.7 collective-permute-done
  286.7 5.1 collective-permute-start
  291.9 5.8 collective-permute-done
  298.4 6.9 %collective-permute-start = (f32[8,64,128]{2,1,0:T(8,128)S(1)}, f32[8,64,128]{2,1,0:T(8,128)S(1)}, u32[]{:S(2)}, u32[]{:S(2)}) collective-permute-start(f32[8,64,128]{2,1,0:T(8,128)S(1)} %multiply_add_fusion.4), channel_id=1, source_target_pairs={{0,16},{16,32},{32,48},{48,64},{64,80},{80,96},{96,112},{112,128},... | collective-permute-start | bytes 786440 | tf_op jit(solution)/shard_map/while/body/eval_jaxpr/ppermute | solution.py:16
  305.3 5.0 collective-permute-done
  311.0 6.1 collective-permute-start
  321.5 6.8 %collective-permute-start = (f32[8,64,128]{2,1,0:T(8,128)S(1)}, f32[8,64,128]{2,1,0:T(8,128)S(1)}, u32[]{:S(2)}, u32[]{:S(2)}) collective-permute-start(f32[8,64,128]{2,1,0:T(8,128)S(1)} %multiply_add_fusion.4), channel_id=1, source_target_pairs={{0,16},{16,32},{32,48},{48,64},{64,80},{80,96},{96,112},{112,128},... | collective-permute-start | bytes 786440 | tf_op jit(solution)/shard_map/while/body/eval_jaxpr/ppermute | solution.py:16
  332.3 5.0 collective-permute-start
  341.3 5.3 collective-permute-start
  350.6 5.0 collective-permute-start
  359.6 6.1 collective-permute-start
  369.7 6.2 collective-permute-start
  385.2 129.6 %psum.29 = bf16[8,3,768]{2,1,0:T(4,128)(2,1)S(1)} all-reduce(f32[8,3,768]{2,1,0:T(4,128)S(1)} %reshape.508), channel_id=1, replica_groups=mesh['ctx'=32,'tp'=16] {'ctx'}, use_global_device_ids=true, to_apply=%region_14.15 | all-reduce | flops 18432 | bytes 110592 | tf_op jit(solution)/shard_map/psum | solution.py:248
  520.6 75.2 %all-reduce.6.cloned.1.call-done = f32[8,8,64,128]{3,2,1,0:T(8,128)} async-done(((f32[8,8,64,128]{3,2,1,0:T(8,128)}), f32[8,8,64,128]{3,2,1,0:T(8,128)}) %all-reduce.6.cloned.1.call-update) | async-done | bytes 2097168 | tf_op jit(solution)/shard_map/psum | solution.py:248
  602.0 28.6 %all-reduce.3 = (f32[256,1]{0,1:T(1,128)S(1)}, f32[256,1]{0,1:T(1,128)S(1)}) all-reduce(f32[256,1]{0,1:T(1,128)S(1)} %bitcast.99, f32[256,1]{0,1:T(1,128)S(1)} %bitcast.102), channel_id=1, replica_groups=mesh['ctx'=32,'tp'=16] {'tp'}, use_global_device_ids=true, to_apply=%region_5.6 | all-reduce | flops 512 | bytes 4096 | tf_op jit(solution)/shard_map/psum | solution.py:80
  (287 shorter events, 134.2 us)
Async XLA Ops:
  7.2 588.5 %all-reduce.6.cloned.1.call-start = ((), (), s32[]{:S(2)}) async-start(), calls=%async_computation | async-start | bytes 4194304 | tf_op jit(solution)/shard_map/psum | solution.py:248
  33.5 38.7 %collective-permute-start.1 = (bf16[3,768]{1,0:T(4,128)(2,1)S(1)}, bf16[3,768]{1,0:T(4,128)(2,1)S(1)}, u32[]{:S(2)}, u32[]{:S(2)}) collective-permute-start(bf16[3,768]{1,0:T(4,128)(2,1)S(1)} %slice.119), channel_id=1, source_target_pairs={{0,16},{16,32},{32,48},{48,64},{64,80},{80,96},{96,112},{112,128},... | collective-permute-start | bytes 13832 | tf_op jit(solution)/shard_map/ppermute | solution.py:16
  75.0 8.8 %collective-permute-start = (f32[8,64,128]{2,1,0:T(8,128)S(1)}, f32[8,64,128]{2,1,0:T(8,128)S(1)}, u32[]{:S(2)}, u32[]{:S(2)}) collective-permute-start(f32[8,64,128]{2,1,0:T(8,128)S(1)} %multiply_add_fusion.4), channel_id=1, source_target_pairs={{0,16},{16,32},{32,48},{48,64},{64,80},{80,96},{96,112},{112,128},... | collective-permute-start | bytes 786440 | tf_op jit(solution)/shard_map/while/body/eval_jaxpr/ppermute | solution.py:16
  84.4 8.7 %collective-permute-start = (f32[8,64,128]{2,1,0:T(8,128)S(1)}, f32[8,64,128]{2,1,0:T(8,128)S(1)}, u32[]{:S(2)}, u32[]{:S(2)}) collective-permute-start(f32[8,64,128]{2,1,0:T(8,128)S(1)} %multiply_add_fusion.4), channel_id=1, source_target_pairs={{0,16},{16,32},{32,48},{48,64},{64,80},{80,96},{96,112},{112,128},... | collective-permute-start | bytes 786440 | tf_op jit(solution)/shard_map/while/body/eval_jaxpr/ppermute | solution.py:16
  93.9 7.8 %collective-permute-start = (f32[8,64,128]{2,1,0:T(8,128)S(1)}, f32[8,64,128]{2,1,0:T(8,128)S(1)}, u32[]{:S(2)}, u32[]{:S(2)}) collective-permute-start(f32[8,64,128]{2,1,0:T(8,128)S(1)} %multiply_add_fusion.4), channel_id=1, source_target_pairs={{0,16},{16,32},{32,48},{48,64},{64,80},{80,96},{96,112},{112,128},... | collective-permute-start | bytes 786440 | tf_op jit(solution)/shard_map/while/body/eval_jaxpr/ppermute | solution.py:16
  102.4 7.4 %collective-permute-start = (f32[8,64,128]{2,1,0:T(8,128)S(1)}, f32[8,64,128]{2,1,0:T(8,128)S(1)}, u32[]{:S(2)}, u32[]{:S(2)}) collective-permute-start(f32[8,64,128]{2,1,0:T(8,128)S(1)} %multiply_add_fusion.4), channel_id=1, source_target_pairs={{0,16},{16,32},{32,48},{48,64},{64,80},{80,96},{96,112},{112,128},... | collective-permute-start | bytes 786440 | tf_op jit(solution)/shard_map/while/body/eval_jaxpr/ppermute | solution.py:16
  110.5 7.1 %collective-permute-start = (f32[8,64,128]{2,1,0:T(8,128)S(1)}, f32[8,64,128]{2,1,0:T(8,128)S(1)}, u32[]{:S(2)}, u32[]{:S(2)}) collective-permute-start(f32[8,64,128]{2,1,0:T(8,128)S(1)} %multiply_add_fusion.4), channel_id=1, source_target_pairs={{0,16},{16,32},{32,48},{48,64},{64,80},{80,96},{96,112},{112,128},... | collective-permute-start | bytes 786440 | tf_op jit(solution)/shard_map/while/body/eval_jaxpr/ppermute | solution.py:16
  118.3 7.7 %collective-permute-start = (f32[8,64,128]{2,1,0:T(8,128)S(1)}, f32[8,64,128]{2,1,0:T(8,128)S(1)}, u32[]{:S(2)}, u32[]{:S(2)}) collective-permute-start(f32[8,64,128]{2,1,0:T(8,128)S(1)} %multiply_add_fusion.4), channel_id=1, source_target_pairs={{0,16},{16,32},{32,48},{48,64},{64,80},{80,96},{96,112},{112,128},... | collective-permute-start | bytes 786440 | tf_op jit(solution)/shard_map/while/body/eval_jaxpr/ppermute | solution.py:16
  126.8 8.6 %collective-permute-start = (f32[8,64,128]{2,1,0:T(8,128)S(1)}, f32[8,64,128]{2,1,0:T(8,128)S(1)}, u32[]{:S(2)}, u32[]{:S(2)}) collective-permute-start(f32[8,64,128]{2,1,0:T(8,128)S(1)} %multiply_add_fusion.4), channel_id=1, source_target_pairs={{0,16},{16,32},{32,48},{48,64},{64,80},{80,96},{96,112},{112,128},... | collective-permute-start | bytes 786440 | tf_op jit(solution)/shard_map/while/body/eval_jaxpr/ppermute | solution.py:16
  136.1 8.3 %collective-permute-start = (f32[8,64,128]{2,1,0:T(8,128)S(1)}, f32[8,64,128]{2,1,0:T(8,128)S(1)}, u32[]{:S(2)}, u32[]{:S(2)}) collective-permute-start(f32[8,64,128]{2,1,0:T(8,128)S(1)} %multiply_add_fusion.4), channel_id=1, source_target_pairs={{0,16},{16,32},{32,48},{48,64},{64,80},{80,96},{96,112},{112,128},... | collective-permute-start | bytes 786440 | tf_op jit(solution)/shard_map/while/body/eval_jaxpr/ppermute | solution.py:16
  145.1 9.1 %collective-permute-start = (f32[8,64,128]{2,1,0:T(8,128)S(1)}, f32[8,64,128]{2,1,0:T(8,128)S(1)}, u32[]{:S(2)}, u32[]{:S(2)}) collective-permute-start(f32[8,64,128]{2,1,0:T(8,128)S(1)} %multiply_add_fusion.4), channel_id=1, source_target_pairs={{0,16},{16,32},{32,48},{48,64},{64,80},{80,96},{96,112},{112,128},... | collective-permute-start | bytes 786440 | tf_op jit(solution)/shard_map/while/body/eval_jaxpr/ppermute | solution.py:16
  154.9 10.5 %collective-permute-start = (f32[8,64,128]{2,1,0:T(8,128)S(1)}, f32[8,64,128]{2,1,0:T(8,128)S(1)}, u32[]{:S(2)}, u32[]{:S(2)}) collective-permute-start(f32[8,64,128]{2,1,0:T(8,128)S(1)} %multiply_add_fusion.4), channel_id=1, source_target_pairs={{0,16},{16,32},{32,48},{48,64},{64,80},{80,96},{96,112},{112,128},... | collective-permute-start | bytes 786440 | tf_op jit(solution)/shard_map/while/body/eval_jaxpr/ppermute | solution.py:16
  166.1 11.9 %collective-permute-start = (f32[8,64,128]{2,1,0:T(8,128)S(1)}, f32[8,64,128]{2,1,0:T(8,128)S(1)}, u32[]{:S(2)}, u32[]{:S(2)}) collective-permute-start(f32[8,64,128]{2,1,0:T(8,128)S(1)} %multiply_add_fusion.4), channel_id=1, source_target_pairs={{0,16},{16,32},{32,48},{48,64},{64,80},{80,96},{96,112},{112,128},... | collective-permute-start | bytes 786440 | tf_op jit(solution)/shard_map/while/body/eval_jaxpr/ppermute | solution.py:16
  178.7 10.1 %collective-permute-start = (f32[8,64,128]{2,1,0:T(8,128)S(1)}, f32[8,64,128]{2,1,0:T(8,128)S(1)}, u32[]{:S(2)}, u32[]{:S(2)}) collective-permute-start(f32[8,64,128]{2,1,0:T(8,128)S(1)} %multiply_add_fusion.4), channel_id=1, source_target_pairs={{0,16},{16,32},{32,48},{48,64},{64,80},{80,96},{96,112},{112,128},... | collective-permute-start | bytes 786440 | tf_op jit(solution)/shard_map/while/body/eval_jaxpr/ppermute | solution.py:16
  189.5 8.8 %collective-permute-start = (f32[8,64,128]{2,1,0:T(8,128)S(1)}, f32[8,64,128]{2,1,0:T(8,128)S(1)}, u32[]{:S(2)}, u32[]{:S(2)}) collective-permute-start(f32[8,64,128]{2,1,0:T(8,128)S(1)} %multiply_add_fusion.4), channel_id=1, source_target_pairs={{0,16},{16,32},{32,48},{48,64},{64,80},{80,96},{96,112},{112,128},... | collective-permute-start | bytes 786440 | tf_op jit(solution)/shard_map/while/body/eval_jaxpr/ppermute | solution.py:16
  199.0 7.5 %collective-permute-start = (f32[8,64,128]{2,1,0:T(8,128)S(1)}, f32[8,64,128]{2,1,0:T(8,128)S(1)}, u32[]{:S(2)}, u32[]{:S(2)}) collective-permute-start(f32[8,64,128]{2,1,0:T(8,128)S(1)} %multiply_add_fusion.4), channel_id=1, source_target_pairs={{0,16},{16,32},{32,48},{48,64},{64,80},{80,96},{96,112},{112,128},... | collective-permute-start | bytes 786440 | tf_op jit(solution)/shard_map/while/body/eval_jaxpr/ppermute | solution.py:16
  207.2 8.6 %collective-permute-start = (f32[8,64,128]{2,1,0:T(8,128)S(1)}, f32[8,64,128]{2,1,0:T(8,128)S(1)}, u32[]{:S(2)}, u32[]{:S(2)}) collective-permute-start(f32[8,64,128]{2,1,0:T(8,128)S(1)} %multiply_add_fusion.4), channel_id=1, source_target_pairs={{0,16},{16,32},{32,48},{48,64},{64,80},{80,96},{96,112},{112,128},... | collective-permute-start | bytes 786440 | tf_op jit(solution)/shard_map/while/body/eval_jaxpr/ppermute | solution.py:16
  216.5 8.6 %collective-permute-start = (f32[8,64,128]{2,1,0:T(8,128)S(1)}, f32[8,64,128]{2,1,0:T(8,128)S(1)}, u32[]{:S(2)}, u32[]{:S(2)}) collective-permute-start(f32[8,64,128]{2,1,0:T(8,128)S(1)} %multiply_add_fusion.4), channel_id=1, source_target_pairs={{0,16},{16,32},{32,48},{48,64},{64,80},{80,96},{96,112},{112,128},... | collective-permute-start | bytes 786440 | tf_op jit(solution)/shard_map/while/body/eval_jaxpr/ppermute | solution.py:16
  225.8 8.8 %collective-permute-start = (f32[8,64,128]{2,1,0:T(8,128)S(1)}, f32[8,64,128]{2,1,0:T(8,128)S(1)}, u32[]{:S(2)}, u32[]{:S(2)}) collective-permute-start(f32[8,64,128]{2,1,0:T(8,128)S(1)} %multiply_add_fusion.4), channel_id=1, source_target_pairs={{0,16},{16,32},{32,48},{48,64},{64,80},{80,96},{96,112},{112,128},... | collective-permute-start | bytes 786440 | tf_op jit(solution)/shard_map/while/body/eval_jaxpr/ppermute | solution.py:16
  235.3 8.3 %collective-permute-start = (f32[8,64,128]{2,1,0:T(8,128)S(1)}, f32[8,64,128]{2,1,0:T(8,128)S(1)}, u32[]{:S(2)}, u32[]{:S(2)}) collective-permute-start(f32[8,64,128]{2,1,0:T(8,128)S(1)} %multiply_add_fusion.4), channel_id=1, source_target_pairs={{0,16},{16,32},{32,48},{48,64},{64,80},{80,96},{96,112},{112,128},... | collective-permute-start | bytes 786440 | tf_op jit(solution)/shard_map/while/body/eval_jaxpr/ppermute | solution.py:16
  244.3 9.4 %collective-permute-start = (f32[8,64,128]{2,1,0:T(8,128)S(1)}, f32[8,64,128]{2,1,0:T(8,128)S(1)}, u32[]{:S(2)}, u32[]{:S(2)}) collective-permute-start(f32[8,64,128]{2,1,0:T(8,128)S(1)} %multiply_add_fusion.4), channel_id=1, source_target_pairs={{0,16},{16,32},{32,48},{48,64},{64,80},{80,96},{96,112},{112,128},... | collective-permute-start | bytes 786440 | tf_op jit(solution)/shard_map/while/body/eval_jaxpr/ppermute | solution.py:16
  254.5 10.4 %collective-permute-start = (f32[8,64,128]{2,1,0:T(8,128)S(1)}, f32[8,64,128]{2,1,0:T(8,128)S(1)}, u32[]{:S(2)}, u32[]{:S(2)}) collective-permute-start(f32[8,64,128]{2,1,0:T(8,128)S(1)} %multiply_add_fusion.4), channel_id=1, source_target_pairs={{0,16},{16,32},{32,48},{48,64},{64,80},{80,96},{96,112},{112,128},... | collective-permute-start | bytes 786440 | tf_op jit(solution)/shard_map/while/body/eval_jaxpr/ppermute | solution.py:16
  265.5 10.0 %collective-permute-start = (f32[8,64,128]{2,1,0:T(8,128)S(1)}, f32[8,64,128]{2,1,0:T(8,128)S(1)}, u32[]{:S(2)}, u32[]{:S(2)}) collective-permute-start(f32[8,64,128]{2,1,0:T(8,128)S(1)} %multiply_add_fusion.4), channel_id=1, source_target_pairs={{0,16},{16,32},{32,48},{48,64},{64,80},{80,96},{96,112},{112,128},... | collective-permute-start | bytes 786440 | tf_op jit(solution)/shard_map/while/body/eval_jaxpr/ppermute | solution.py:16
  276.2 9.8 %collective-permute-start = (f32[8,64,128]{2,1,0:T(8,128)S(1)}, f32[8,64,128]{2,1,0:T(8,128)S(1)}, u32[]{:S(2)}, u32[]{:S(2)}) collective-permute-start(f32[8,64,128]{2,1,0:T(8,128)S(1)} %multiply_add_fusion.4), channel_id=1, source_target_pairs={{0,16},{16,32},{32,48},{48,64},{64,80},{80,96},{96,112},{112,128},... | collective-permute-start | bytes 786440 | tf_op jit(solution)/shard_map/while/body/eval_jaxpr/ppermute | solution.py:16
  286.7 11.0 %collective-permute-start = (f32[8,64,128]{2,1,0:T(8,128)S(1)}, f32[8,64,128]{2,1,0:T(8,128)S(1)}, u32[]{:S(2)}, u32[]{:S(2)}) collective-permute-start(f32[8,64,128]{2,1,0:T(8,128)S(1)} %multiply_add_fusion.4), channel_id=1, source_target_pairs={{0,16},{16,32},{32,48},{48,64},{64,80},{80,96},{96,112},{112,128},... | collective-permute-start | bytes 786440 | tf_op jit(solution)/shard_map/while/body/eval_jaxpr/ppermute | solution.py:16
  298.4 11.9 %collective-permute-start = (f32[8,64,128]{2,1,0:T(8,128)S(1)}, f32[8,64,128]{2,1,0:T(8,128)S(1)}, u32[]{:S(2)}, u32[]{:S(2)}) collective-permute-start(f32[8,64,128]{2,1,0:T(8,128)S(1)} %multiply_add_fusion.4), channel_id=1, source_target_pairs={{0,16},{16,32},{32,48},{48,64},{64,80},{80,96},{96,112},{112,128},... | collective-permute-start | bytes 786440 | tf_op jit(solution)/shard_map/while/body/eval_jaxpr/ppermute | solution.py:16
  311.0 9.8 %collective-permute-start = (f32[8,64,128]{2,1,0:T(8,128)S(1)}, f32[8,64,128]{2,1,0:T(8,128)S(1)}, u32[]{:S(2)}, u32[]{:S(2)}) collective-permute-start(f32[8,64,128]{2,1,0:T(8,128)S(1)} %multiply_add_fusion.4), channel_id=1, source_target_pairs={{0,16},{16,32},{32,48},{48,64},{64,80},{80,96},{96,112},{112,128},... | collective-permute-start | bytes 786440 | tf_op jit(solution)/shard_map/while/body/eval_jaxpr/ppermute | solution.py:16
  321.5 10.1 %collective-permute-start = (f32[8,64,128]{2,1,0:T(8,128)S(1)}, f32[8,64,128]{2,1,0:T(8,128)S(1)}, u32[]{:S(2)}, u32[]{:S(2)}) collective-permute-start(f32[8,64,128]{2,1,0:T(8,128)S(1)} %multiply_add_fusion.4), channel_id=1, source_target_pairs={{0,16},{16,32},{32,48},{48,64},{64,80},{80,96},{96,112},{112,128},... | collective-permute-start | bytes 786440 | tf_op jit(solution)/shard_map/while/body/eval_jaxpr/ppermute | solution.py:16
  332.3 8.2 %collective-permute-start = (f32[8,64,128]{2,1,0:T(8,128)S(1)}, f32[8,64,128]{2,1,0:T(8,128)S(1)}, u32[]{:S(2)}, u32[]{:S(2)}) collective-permute-start(f32[8,64,128]{2,1,0:T(8,128)S(1)} %multiply_add_fusion.4), channel_id=1, source_target_pairs={{0,16},{16,32},{32,48},{48,64},{64,80},{80,96},{96,112},{112,128},... | collective-permute-start | bytes 786440 | tf_op jit(solution)/shard_map/while/body/eval_jaxpr/ppermute | solution.py:16
  341.3 8.6 %collective-permute-start = (f32[8,64,128]{2,1,0:T(8,128)S(1)}, f32[8,64,128]{2,1,0:T(8,128)S(1)}, u32[]{:S(2)}, u32[]{:S(2)}) collective-permute-start(f32[8,64,128]{2,1,0:T(8,128)S(1)} %multiply_add_fusion.4), channel_id=1, source_target_pairs={{0,16},{16,32},{32,48},{48,64},{64,80},{80,96},{96,112},{112,128},... | collective-permute-start | bytes 786440 | tf_op jit(solution)/shard_map/while/body/eval_jaxpr/ppermute | solution.py:16
  350.6 8.3 %collective-permute-start = (f32[8,64,128]{2,1,0:T(8,128)S(1)}, f32[8,64,128]{2,1,0:T(8,128)S(1)}, u32[]{:S(2)}, u32[]{:S(2)}) collective-permute-start(f32[8,64,128]{2,1,0:T(8,128)S(1)} %multiply_add_fusion.4), channel_id=1, source_target_pairs={{0,16},{16,32},{32,48},{48,64},{64,80},{80,96},{96,112},{112,128},... | collective-permute-start | bytes 786440 | tf_op jit(solution)/shard_map/while/body/eval_jaxpr/ppermute | solution.py:16
  359.6 9.4 %collective-permute-start = (f32[8,64,128]{2,1,0:T(8,128)S(1)}, f32[8,64,128]{2,1,0:T(8,128)S(1)}, u32[]{:S(2)}, u32[]{:S(2)}) collective-permute-start(f32[8,64,128]{2,1,0:T(8,128)S(1)} %multiply_add_fusion.4), channel_id=1, source_target_pairs={{0,16},{16,32},{32,48},{48,64},{64,80},{80,96},{96,112},{112,128},... | collective-permute-start | bytes 786440 | tf_op jit(solution)/shard_map/while/body/eval_jaxpr/ppermute | solution.py:16
  369.7 10.0 %collective-permute-start = (f32[8,64,128]{2,1,0:T(8,128)S(1)}, f32[8,64,128]{2,1,0:T(8,128)S(1)}, u32[]{:S(2)}, u32[]{:S(2)}) collective-permute-start(f32[8,64,128]{2,1,0:T(8,128)S(1)} %multiply_add_fusion.4), channel_id=1, source_target_pairs={{0,16},{16,32},{32,48},{48,64},{64,80},{80,96},{96,112},{112,128},... | collective-permute-start | bytes 786440 | tf_op jit(solution)/shard_map/while/body/eval_jaxpr/ppermute | solution.py:16
  383.7 131.8 %copy-start.14 = (f32[768]{0:T(1024)S(1)}, f32[768]{0:T(1024)}, u32[]{:S(2)}) copy-start(f32[768]{0:T(1024)} %copy-done.13) | copy-start | bytes 9220
  383.7 131.8 %copy-start.19 = (s32[256]{0:T(256)S(1)}, s32[256]{0:T(256)}, u32[]{:S(2)}) copy-start(s32[256]{0:T(256)} %copy-done.18) | copy-start | bytes 3076
  383.7 131.8 %copy-start.35 = (s32[256]{0:T(256)S(1)}, s32[256]{0:T(256)}, u32[]{:S(2)}) copy-start(s32[256]{0:T(256)} %get-tuple-element.66) | copy-start | bytes 3076
  383.8 131.8 %copy-start.36 = (s32[6]{0:T(128)S(1)}, s32[6]{0:T(128)}, u32[]{:S(2)}) copy-start(s32[6]{0:T(128)} %get-tuple-element.73) | copy-start | bytes 76
  383.8 131.8 %copy-start.37 = (s32[6]{0:T(128)S(1)}, s32[6]{0:T(128)}, u32[]{:S(2)}) copy-start(s32[6]{0:T(128)} %get-tuple-element.74) | copy-start | bytes 76
  383.8 131.8 %copy-start.38 = (pred[6]{0:T(512)(128)(4,1)S(1)}, pred[6]{0:T(512)(128)(4,1)}, u32[]{:S(2)}) copy-start(pred[6]{0:T(512)(128)(4,1)} %broadcast_in_dim.287) | copy-start | bytes 22
  383.8 131.8 %copy-start.41 = (pred[256]{0:T(512)(128)(4,1)S(1)}, pred[256]{0:T(512)(128)(4,1)}, u32[]{:S(2)}) copy-start(pred[256]{0:T(512)(128)(4,1)} %get-tuple-element.61) | copy-start | bytes 772
  383.8 131.8 %copy-start.42 = (pred[256]{0:T(512)(128)(4,1)S(1)}, pred[256]{0:T(512)(128)(4,1)}, u32[]{:S(2)}) copy-start(pred[256]{0:T(512)(128)(4,1)} %get-tuple-element.62) | copy-start | bytes 772
  384.6 131.5 %copy-start.12 = (f32[768]{0:T(1024)S(1)}, f32[768]{0:T(1024)}, u32[]{:S(2)}) copy-start(f32[768]{0:T(1024)} %copy-done.11) | copy-start | bytes 9220
  384.6 131.5 %copy-start.34 = (s32[256]{0:T(256)S(1)}, s32[256]{0:T(256)}, u32[]{:S(2)}) copy-start(s32[256]{0:T(256)} %get-tuple-element.65) | copy-start | bytes 3076
  384.6 131.9 %copy-start.21 = (f32[768]{0:T(1024)S(1)}, f32[768]{0:T(1024)}, u32[]{:S(2)}) copy-start(f32[768]{0:T(1024)} %copy-done.20) | copy-start | bytes 9220
  384.6 131.9 %copy-start.23 = (f32[768]{0:T(1024)S(1)}, f32[768]{0:T(1024)}, u32[]{:S(2)}) copy-start(f32[768]{0:T(1024)} %copy-done.22) | copy-start | bytes 9220
  384.6 131.9 %copy-start.47 = (s32[256]{0:T(256)S(1)}, s32[256]{0:T(256)}, u32[]{:S(2)}) copy-start(s32[256]{0:T(256)} %get-tuple-element.64) | copy-start | bytes 3076
  384.7 131.9 %copy-start.52 = (pred[256]{0:T(512)(128)(4,1)S(1)}, pred[256]{0:T(512)(128)(4,1)}, u32[]{:S(2)}) copy-start(pred[256]{0:T(512)(128)(4,1)} %get-tuple-element.57) | copy-start | bytes 772
  384.7 131.9 %copy-start.53 = (pred[256]{0:T(512)(128)(4,1)S(1)}, pred[256]{0:T(512)(128)(4,1)}, u32[]{:S(2)}) copy-start(pred[256]{0:T(512)(128)(4,1)} %get-tuple-element.58) | copy-start | bytes 772
  (43 other events, 1378.7 us)
Sparse Core Ops, SparseCore 0:
  382.3 213.4 all-reduce.5
where the time goes:
time: 641 us; the launch traced here: 639 us
  waiting for transfers between devices  201 us (31%)
  blocking collectives  198 us (31%)
  starting transfers between devices  161 us (25%)
  other arithmetic  38.4 us (6%)
  local copies, waits for them, and re-layouts  16.2 us (3%)
  between operations  15.2 us (2%)
  matrix products  9.01 us (1%)
    ppermute x32, starting transfers between devices, passed_along(): lax.ppermute(value, axis, [(source, source + steps) for source in range(f...  161 us
    psum x1, blocking collectives, body(): all_states, all_tails = lax.psum((candidate, tail_rows), 'ctx')  130 us
    ppermute x32, waiting for transfers between devices, passed_along(): lax.ppermute(value, axis, [(source, source + steps) for source in range(f...  125 us
    psum x1, waiting for transfers between devices, body(): all_states, all_tails = lax.psum((candidate, tail_rows), 'ctx')  75.2 us
    psum x1, blocking collectives, finish(): total_squares = lax.psum(partial_squares, 'tp')  28.6 us
    all_gather x1, blocking collectives, body(): lax.all_gather(prefix_bc, 'tp', axis=0, tiled=True)  25.1 us
    add x31, other arithmetic, carry_step(): return passed_along(end_decay[:, None, None] * state + end_state, 'ctx', 1)  21.6 us
    all_gather x1, blocking collectives, body(): lax.all_gather(branch_bc, 'tp', axis=0, tiled=True)  14.8 us
  transfers between devices with their start and end apart: 33, of which 32 were waited for; matrix products, arithmetic and copies ran while one was open for 4% of the time, Pallas kernels for 0%

commit v1 on v0

v1 whole, which is shorter than its diff:
```python
import jax
import jax.numpy as jnp
from jax import lax
from jax.sharding import PartitionSpec as P

BR_PER = 2
EPSILON = 1e-05
SLOTS = 8
BF = jnp.bfloat16
F32 = jnp.float32
HIGH = lax.Precision.HIGHEST


def conv_silu(lagged, weights):
    summed = weights[0].astype(F32)[None, :] * lagged[0].astype(F32)
    for tap in range(1, len(lagged)):
        summed = summed + weights[tap].astype(F32)[None, :] * lagged[tap].astype(F32)
    return jax.nn.silu(summed).astype(BF)


def split_conv(convolved, channels, heads):
    length = convolved.shape[0]
    state = (convolved.shape[1] - channels) // 2
    values = convolved[:, :channels].reshape(length, heads, channels // heads)
    return values, convolved[:, channels : channels + state], convolved[:, channels + state :]


def decays(raw_steps, rates):
    length = raw_steps.shape[1]
    step = jax.nn.softplus(raw_steps)
    log_decay = -rates[:, None] * step
    index = jnp.arange(length, dtype=jnp.int32)
    upper = (index[:, None] <= index[None, :]).astype(F32)
    return step, log_decay, jnp.dot(log_decay, upper, precision=HIGH)


def intra(values, b_rows, c_rows, step, cumulative, mask):
    scores = jnp.dot(c_rows, b_rows.T, preferred_element_type=F32)
    exponent = jnp.where(mask[None], cumulative[:, :, None] - cumulative[:, None, :], 0.0)
    mixing = jnp.where(mask[None], scores[None] * jnp.exp(exponent) * step[:, None, :], 0.0)
    return jnp.einsum("hts,shp->thp", mixing.astype(BF), values, preferred_element_type=F32)


def pick(array, positions):
    index = jnp.arange(array.shape[1], dtype=jnp.int32)
    hit = index[None, None, :] == positions[:, None, None]
    return jnp.sum(jnp.where(hit, array[None], 0.0), axis=2)


def local_states(values, b_rows, step, cumulative, positions):
    length = cumulative.shape[1]
    ends = pick(cumulative, positions)
    row = jnp.arange(length, dtype=jnp.int32)
    inside = (row[None, :] <= positions[:, None])[:, None, :]
    exponent = jnp.where(inside, ends[:, :, None] - cumulative[None], 0.0)
    weight = jnp.where(inside, jnp.exp(exponent) * step[None], 0.0)
    weighted = (jnp.transpose(weight, (0, 2, 1))[:, :, :, None] * values[None].astype(F32)).astype(BF)
    states = jnp.einsum("jshp,sn->jhpn", weighted, b_rows, preferred_element_type=F32)
    return states, ends


def from_state(c_rows, state, weight):
    result = jnp.einsum("tn,hpn->thp", c_rows, state, preferred_element_type=F32)
    return result * weight.T[:, :, None]


def parts_of(value, count):
    found = []
    for _ in range(count):
        part = lax.reduce_precision(value, 8, 7)
        found.append(part.astype(BF))
        value = value - part
    return found


def body(
    prefix_x, prefix_z, prefix_bc, prefix_dt, branch_x, branch_z, branch_bc, branch_dt,
    conv_x, conv_bc, decay_rate, skip, norm_gain, bound_pos, branch_owner, branch_parent, branch_len,
):
    n_ctx = lax.axis_size("ctx")
    me = lax.axis_index("ctx")
    length, channels = prefix_x.shape
    heads = decay_rate.shape[0]
    width = prefix_bc.shape[1]
    n_state = width // 2
    bounds = bound_pos.shape[0]
    branches = branch_owner.shape[0]
    weights = jnp.concatenate([conv_x, conv_bc], axis=1)
    taps = weights.shape[0]
    tail = taps - 1
    row_width = channels + width

    gathered = lax.all_gather(jnp.concatenate([prefix_bc, branch_bc], axis=1), "tp", axis=0, tiled=True)
    joined = jnp.concatenate([prefix_x, gathered[:, :width]], axis=1)
    before = lax.ppermute(joined[length - tail :], "ctx", [(i, i + 1) for i in range(n_ctx - 1)])
    extended = jnp.concatenate([before, joined], axis=0)
    lagged = [extended[tap : tap + length] for tap in range(taps)]
    values, b_rows, c_rows = split_conv(conv_silu(lagged, weights), channels, heads)
    step, _, cumulative = decays(prefix_dt, decay_rate)

    block_of = bound_pos // length
    at = bound_pos - block_of * length
    order = jnp.arange(bounds, dtype=jnp.int32)
    slot_of = jnp.sum(
        ((block_of[:, None] == block_of[None, :]) & (order[None, :] < order[:, None])).astype(jnp.int32), axis=1
    )
    border = jnp.arange(branches, dtype=jnp.int32)
    same = branch_owner[:, None] == branch_owner[None, :]
    earlier = same & (border[None, :] < border[:, None])
    rank = jnp.sum(earlier.astype(jnp.int32), axis=1)
    start = jnp.sum(jnp.where(earlier, branch_len[None, :], 0), axis=1)
    place = jnp.arange(n_ctx * BR_PER, dtype=jnp.int32)
    chosen = place[:, None] == (branch_owner * BR_PER + rank)[None, :]
    parent_of = jnp.sum(jnp.where(chosen, branch_parent[None, :], 0), axis=1)
    mine = (me * BR_PER + jnp.arange(BR_PER, dtype=jnp.int32))[:, None] == (branch_owner * BR_PER + rank)[None, :]
    my_len = jnp.sum(jnp.where(mine, branch_len[None, :], 0), axis=1)
    my_start = jnp.sum(jnp.where(mine, start[None, :], 0), axis=1)

    slot_here = (block_of == me)[None, :] & (slot_of[None, :] == jnp.arange(SLOTS, dtype=jnp.int32)[:, None])
    positions = jnp.sum(jnp.where(slot_here, at[None, :] + 1, 0), axis=1) - 1
    positions = jnp.concatenate([jnp.full((1,), length - 1, jnp.int32), positions])
    states, ends = local_states(values, b_rows, step, cumulative, positions)
    slices = states.reshape(SLOTS + 1, n_ctx, -1, n_state)
    rows = slices.shape[2]
    end_hi, end_lo = parts_of(slices[0], 2)
    partial = jnp.transpose(slices[1:].astype(BF), (1, 0, 2, 3)).reshape(n_ctx, SLOTS * rows, n_state)
    per_head = jnp.repeat(jnp.pad(ends.T, ((0, 0), (0, n_state - SLOTS - 1))), n_ctx // heads, axis=0)
    logs = jnp.stack(parts_of(per_head, 3), axis=1)
    parent_hit = parent_of[:, None] == order[None, :]
    parent_at = jnp.sum(jnp.where(parent_hit, at[None, :], 0), axis=1)
    parent_block = jnp.sum(jnp.where(parent_hit, block_of[None, :], 0), axis=1)
    wanted = parent_at[:, None] + 1 + jnp.arange(tail, dtype=jnp.int32)[None, :]
    wanted = jnp.where((parent_block == me)[:, None], wanted, -1).reshape(-1)
    picker = (wanted[:, None] == jnp.arange(length + tail, dtype=jnp.int32)[None, :]).astype(BF)
    tails = jnp.dot(picker, extended, preferred_element_type=F32).astype(BF)
    tails = tails.reshape(n_ctx, BR_PER * tail * row_width // n_state, n_state)
    pieces = [end_hi, end_lo, partial, tails, logs]
    sent = jnp.concatenate(pieces, axis=1)
    sent = jnp.pad(sent, ((0, 0), (0, -sent.shape[1] % 16), (0, 0)))
    got = lax.all_to_all(sent, "ctx", 0, 0, tiled=True)

    edges = [0]
    for piece in pieces:
        edges.append(edges[-1] + piece.shape[1])
    end_hi, end_lo, partial, tails, logs = [
        got[:, first:last].astype(F32) for first, last in zip(edges[:-1], edges[1:], strict=True)
    ]
    ends = jnp.sum(logs, axis=1)[:, : SLOTS + 1]
    block = jnp.arange(n_ctx, dtype=jnp.int32)
    totals = jnp.sum(jnp.where(block[None, :] <= block[:, None], ends[:, 0][None, :], 0.0), axis=1)
    gap = (totals - ends[:, 0])[:, None] - totals[None, :]
    earlier_block = block[None, :] < block[:, None]
    carry = jnp.where(earlier_block, jnp.exp(jnp.where(earlier_block, gap, 0.0)), 0.0)
    entering = jnp.dot(carry, (end_hi + end_lo).reshape(n_ctx, -1), precision=HIGH)
    held = block[None, :] == block_of[:, None]
    bound_end = jnp.sum(
        jnp.where(
            held[:, :, None] & (slot_of[:, None, None] == jnp.arange(SLOTS, dtype=jnp.int32)[None, None, :]),
            ends[None, :, 1:],
            0.0,
        ),
        axis=(1, 2),
    )
    choose = jnp.where(held, jnp.exp(bound_end)[:, None], 0.0)
    slot_pick = (
        held[:, :, None] & (slot_of[:, None, None] == jnp.arange(SLOTS, dtype=jnp.int32)[None, None, :])
    ).reshape(bounds, -1)
    bound_state = jnp.dot(choose, entering, precision=HIGH) + jnp.dot(
        slot_pick.astype(BF), partial.astype(BF).reshape(n_ctx * SLOTS, -1), preferred_element_type=F32
    )
    seeds = jnp.dot(parent_hit.astype(F32), bound_state, precision=HIGH).reshape(n_ctx, BR_PER * rows, n_state)
    back = jnp.concatenate([entering.reshape(n_ctx, rows, n_state), seeds], axis=1).astype(BF)
    back = lax.all_to_all(back, "ctx", 0, 0, tiled=True)

    row = jnp.arange(length, dtype=jnp.int32)
    mixed = intra(values, b_rows, c_rows, step, cumulative, row[None, :] <= row[:, None])

    inside = (row[None, :] >= my_start[:, None]) & (row[None, :] < (my_start + my_len)[:, None])
    live = inside[0] | inside[1]
    segment = jnp.where(inside[0], 0, jnp.where(inside[1], 1, BR_PER))
    offset = row - jnp.sum(jnp.where(inside, my_start[:, None], 0), axis=0)
    tail_rows = jnp.sum(tails, axis=0).astype(BF).reshape(BR_PER * tail, row_width)
    branch_joined = jnp.concatenate([branch_x, gathered[:, width:]], axis=1)
    column = jnp.arange(BR_PER * tail, dtype=jnp.int32)
    lagged = []
    for shift in range(tail, 0, -1):
        shifted = jnp.concatenate(
            [jnp.zeros((shift, row_width), BF), branch_joined[: length - shift]], axis=0
        )
        local = jnp.where((offset >= shift)[:, None], shifted, jnp.zeros_like(shifted))
        picker = (
            (segment[:, None] == (column // tail)[None, :])
            & (offset[:, None] < shift)
            & ((column % tail)[None, :] == tail - shift + offset[:, None])
        ).astype(BF)
        lagged.append(local + jnp.dot(picker, tail_rows, preferred_element_type=F32).astype(BF))
    lagged.append(branch_joined)
    b_values, b_b, b_c = split_conv(conv_silu(lagged, weights), channels, heads)
    b_step, b_log, b_cum = decays(branch_dt, decay_rate)
    mask = (segment[:, None] == segment[None, :]) & live[:, None] & (row[None, :] <= row[:, None])
    b_mixed = intra(b_values, b_b, b_c, b_step, b_cum, mask)
    starts = pick(b_cum - b_log, my_start)
    gap = b_cum - jnp.where(inside[0][None, :], starts[0][:, None], starts[1][:, None])
    seed_weight = jnp.where(live[None, :], jnp.exp(jnp.where(live[None, :], gap, 0.0)), 0.0)

    shape = (heads, channels // heads, n_state)
    mixed = mixed + from_state(c_rows, back[:, :rows].reshape(shape), jnp.exp(cumulative))
    for slot in range(BR_PER):
        seed = back[:, (slot + 1) * rows : (slot + 2) * rows].reshape(shape)
        b_mixed = b_mixed + from_state(b_c, seed, jnp.where(inside[slot][None, :], seed_weight, 0.0))

    def gate(mixed, values, z):
        mixed = mixed + skip[None, :, None] * values.astype(F32)
        gated = mixed.reshape(length, -1) * jax.nn.silu(z.astype(F32))
        return gated, jnp.sum(gated * gated, axis=1)

    gated, squares = gate(mixed, values, prefix_z)
    b_gated, b_squares = gate(b_mixed, b_values, branch_z)
    every = lax.all_gather(jnp.stack([squares, b_squares])[None], "tp", axis=0, tiled=True)
    factor = lax.rsqrt(jnp.sum(every, axis=0) / (channels * lax.axis_size("tp")) + EPSILON)
    prefix_out = (gated * factor[0][:, None] * norm_gain[None, :]).astype(BF)
    branch_out = (b_gated * factor[1][:, None] * norm_gain[None, :]).astype(BF)
    return prefix_out, jnp.where(live[:, None], branch_out, jnp.zeros_like(branch_out))


def solution(mesh):
    both = P(("ctx", "tp"), None)
    in_specs = (
        P("ctx", "tp"), P("ctx", "tp"), both, P("tp", "ctx"),
        P("ctx", "tp"), P("ctx", "tp"), both, P("tp", "ctx"),
        P(None, "tp"), P(), P("tp"), P("tp"), P("tp"), P(), P(), P(), P(),
    )
    out_specs = (P("ctx", "tp"), P("ctx", "tp"))
    return jax.shard_map(body, mesh=mesh, in_specs=in_specs, out_specs=out_specs, check_vma=False)
```

time: 641 us -> 160 us (0.25)
  waiting for transfers between devices: 201 us -> 36.3 us
  blocking collectives: 198 us -> 43.9 us
  starting transfers between devices: 161 us -> 19.6 us
  between operations: 15.2 us -> 1.58 us
  other arithmetic: 38.4 us -> 25.4 us
    psum x2 -> x0, blocking collectives: 158 us -> none  [the longest x1 130 us: body(): all_states, all_tails = lax.psum((candidate, tail_rows), 'ctx')]
    ppermute x32 -> x1, starting transfers between devices: 161 us -> 3.19 us  [body(): lax.ppermute(joined[length - tail:], 'ctx', [(i, i + 1) for i in range(n_...]
    ppermute x32 -> x1, waiting for transfers between devices: 125 us -> 0.01 us  [body(): lax.ppermute(joined[length - tail:], 'ctx', [(i, i + 1) for i in range(n_...]
    psum x1 -> x0, waiting for transfers between devices: 75.2 us -> none  [body(): all_states, all_tails = lax.psum((candidate, tail_rows), 'ctx')]
    all_to_all x0 -> x2, waiting for transfers between devices: none -> 36.3 us  [the longest x1 31 us: body(): got = lax.all_to_all(sent, 'ctx', 0, 0, tiled=True)]
    add x34 -> x6, other arithmetic: 21.7 us -> 1.37 us  [the longest x1 0.66 us: body(): positions = jnp.sum(jnp.where(slot_here, at[None, :] + 1, 0), axis=1) - 1]
    all_to_all x0 -> x2, starting transfers between devices: none -> 16.4 us  [the longest x1 8.92 us: body(): got = lax.all_to_all(sent, 'ctx', 0, 0, tiled=True)]
    dot_general x12 -> x18, matrix products: 9.01 us -> 13.9 us  [the longest x3 3.24 us: body(): jnp.dot(picker, tail_rows, preferred_element_type=F32).astype(BF)]
  transfers between devices with their start and end apart: 33 -> 3, of which waited for: 32 -> 2; matrix products, arithmetic and copies ran while one was open for 4% -> 17% of each run, Pallas kernels for 0% -> 0%
where the time goes in v1:
time: 160 us; the launch traced here: 158 us
  blocking collectives  43.9 us (27%)
  waiting for transfers between devices  36.3 us (23%)
  other arithmetic  25.4 us (16%)
  starting transfers between devices  19.6 us (12%)
  local copies, waits for them, and re-layouts  17.9 us (11%)
  matrix products  13.9 us (9%)
    all_to_all x1, waiting for transfers between devices, body(): got = lax.all_to_all(sent, 'ctx', 0, 0, tiled=True)  31 us
    all_gather x1, blocking collectives, body(): lax.all_gather(jnp.concatenate([prefix_bc, branch_bc], axis=1), 'tp', axi...  25.2 us
    all_gather x1, blocking collectives, body(): lax.all_gather(jnp.stack([squares, b_squares])[None], 'tp', axis=0, tiled...  18.7 us
    all_to_all x1, starting transfers between devices, body(): got = lax.all_to_all(sent, 'ctx', 0, 0, tiled=True)  8.92 us
    all_to_all x1, starting transfers between devices, body(): back = lax.all_to_all(back, 'ctx', 0, 0, tiled=True)  7.45 us
    all_to_all x1, waiting for transfers between devices, body(): back = lax.all_to_all(back, 'ctx', 0, 0, tiled=True)  5.25 us
    concatenate x1, local copies, waits for them, and re-layouts, body(): sent = jnp.concatenate(pieces, axis=1)  3.65 us
    dot_general x3, matrix products, body(): jnp.dot(picker, tail_rows, preferred_element_type=F32).astype(BF)  3.24 us
  transfers between devices with their start and end apart: 3, of which 2 were waited for; matrix products, arithmetic and copies ran while one was open for 17% of the time, Pallas kernels for 0%

profile of v1, /device:TPU:1, one launch (start us, length us, event | category | flops | bytes accessed | tf_op | source)
XLA Modules:
  0.0 158.5 jit_solution(17156961118969503318)
XLA Ops:
  0.6 0.8 pad_maximum_fusion.3
  1.4 25.2 %all_gather.6 = bf16[256,512]{1,0:T(8,128)(2,1)S(1)} all-gather(bf16[16,512]{1,0:T(8,128)(2,1)S(1)} %pad_maximum_fusion.3), channel_id=1, replica_groups=mesh['ctx'=32,'tp'=16] {'tp'}, dimensions={0}, use_global_device_ids=true | all-gather | bytes 278528 | tf_op jit(solution)/shard_map/all_gather | solution.py:93
  26.6 0.7 fusion.90
  27.3 3.2 %collective-permute-start = (bf16[3,768]{1,0:T(4,128)(2,1)S(1)}, bf16[3,768]{1,0:T(4,128)(2,1)S(1)}, u32[]{:S(2)}, u32[]{:S(2)}) collective-permute-start(bf16[3,768]{1,0:T(4,128)(2,1)S(1)} %fusion.90), channel_id=1, source_target_pairs={{0,16},{16,32},{32,48},{48,64},{64,80},{80,96},{96,112},{112,128},... | collective-permute-start | bytes 13832 | tf_op jit(solution)/shard_map/ppermute | solution.py:95
  33.1 1.3 compare_select_fusion.1
  34.4 1.5 bitcast_exponential_fusion
  36.0 0.7 constant_dynamic-update-slice_fusion.1
  36.7 1.4 select_reduce_fusion.2
  38.8 0.8 select_reduce_fusion.3
  40.1 0.7 constant_dynamic-update-slice_fusion
  40.9 0.7 broadcast_and_fusion
  43.1 1.0 maximum_maximum_fusion
  45.0 0.8 fusion
  46.0 0.7 fusion.44
  47.7 3.7 %concatenate.39 = bf16[32,199,128]{2,1,0:T(8,128)(2,1)S(1)} concatenate(bf16[32,16,128]{2,1,0:T(8,128)(2,1)} %get-tuple-element.25, bf16[32,16,128]{2,1,0:T(8,128)(2,1)} %get-tuple-element.24, bf16[32,128,128]{2,1,0:T(8,128)(2,1)S(1)} %bitcast.88, bf16[32,36,128]{2,1,0:T(8,128)(2,1)S(1)} %reshape.471, bf16[32,1,128]{2,1,0:T(2,128)(2,1)S(1)} %copy.56, bf16[32,1,128]{2,1,0:T(2,128)(2,1)} %copy.57, ...), dimensions={1} | concatenate | bytes 3260416 | tf_op jit(solution)/shard_map/concatenate | solution.py:138
  51.4 1.3 pad.12
  52.7 8.9 %all-to-all-start = ((bf16[32,208,128]{2,1,0:T(8,128)(2,1)}), bf16[32,208,128]{2,1,0:T(8,128)(2,1)S(1)}, u32[]{:S(2)}, u32[]{:S(2)}) async-start(bf16[32,208,128]{2,1,0:T(8,128)(2,1)} %pad.12), calls=%async_computation | async-start | bytes 3407872 | tf_op jit(solution)/shard_map/all_to_all | solution.py:140
  61.7 0.7 and.137
  64.8 0.8 fusion.41
  65.5 0.8 fusion.42
  66.3 0.8 fusion.40
  68.3 0.7 fusion.92
  69.0 0.8 and_and_fusion
  69.7 0.9 fusion.59
  70.6 31.0 %all-to-all-done = bf16[32,208,128]{2,1,0:T(8,128)(2,1)S(1)} async-done(((bf16[32,208,128]{2,1,0:T(8,128)(2,1)}), bf16[32,208,128]{2,1,0:T(8,128)(2,1)S(1)}, u32[]{:S(2)}, u32[]{:S(2)}) %all-to-all-start) | async-done | bytes 1703968 | tf_op jit(solution)/shard_map/all_to_all | solution.py:140
  103.0 1.1 slice.184
  104.1 1.5 reshape.475
  105.7 1.4 select_reduce_fusion.5
  107.0 1.4 copy.59
  108.4 0.8 subtract_reduce_fusion
  109.2 0.9 select_reduce_fusion
  110.2 1.1 fusion.46
  112.0 0.9 fusion.99
  112.9 0.9 convolution_add_fusion
  114.4 0.9 copy.66
  115.3 0.8 pad_maximum_fusion.2
  116.1 7.5 %all-to-all-start.1 = ((bf16[32,48,128]{2,1,0:T(8,128)(2,1)}), bf16[32,48,128]{2,1,0:T(8,128)(2,1)S(1)}, u32[]{:S(2)}, u32[]{:S(2)}) async-start(bf16[32,48,128]{2,1,0:T(8,128)(2,1)} %pad_maximum_fusion.2), calls=%async_computation.1 | async-start | bytes 786432 | tf_op jit(solution)/shard_map/all_to_all | solution.py:173
  123.7 1.5 fusion.16
  125.2 1.1 fusion.19
  126.4 0.7 multiply_convert_fusion.2
  127.2 0.8 copy.61
  128.0 0.9 fusion.52
  128.9 5.3 %all-to-all-done.1 = bf16[32,48,128]{2,1,0:T(8,128)(2,1)S(1)} async-done(((bf16[32,48,128]{2,1,0:T(8,128)(2,1)}), bf16[32,48,128]{2,1,0:T(8,128)(2,1)S(1)}, u32[]{:S(2)}, u32[]{:S(2)}) %all-to-all-start.1) | async-done | bytes 393248 | tf_op jit(solution)/shard_map/all_to_all | solution.py:173
  134.5 0.8 fusion.6
  136.4 0.8 fusion.7
  137.9 18.7 %all-gather.1 = f32[16,2,256]{2,1,0:T(2,128)S(1)} all-gather(f32[1,2,256]{2,1,0:T(2,128)S(1)} %maximum_bitcast_fusion), channel_id=2, replica_groups=mesh['ctx'=32,'tp'=16] {'tp'}, dimensions={0}, use_global_device_ids=true | all-gather | bytes 34816 | tf_op jit(solution)/shard_map/all_gather | solution.py:219
  156.7 0.9 fusion.45
  157.6 0.9 multiply_convert_fusion.5
  (184 shorter events, 15.6 us)
Async XLA Ops:
  0.6 43.6 %copy-start.1 = (bf16[256,512]{1,0:T(8,128)(2,1)S(1)}, bf16[256,512]{1,0:T(8,128)(2,1)}, u32[]{:S(2)}) copy-start(bf16[256,512]{1,0:T(8,128)(2,1)} %param.17) | copy-start | bytes 786436
  27.3 15.8 %collective-permute-start = (bf16[3,768]{1,0:T(4,128)(2,1)S(1)}, bf16[3,768]{1,0:T(4,128)(2,1)S(1)}, u32[]{:S(2)}, u32[]{:S(2)}) collective-permute-start(bf16[3,768]{1,0:T(4,128)(2,1)S(1)} %fusion.90), channel_id=1, source_target_pairs={{0,16},{16,32},{32,48},{48,64},{64,80},{80,96},{96,112},{112,128},... | collective-permute-start | bytes 13832 | tf_op jit(solution)/shard_map/ppermute | solution.py:95
  31.2 8.6 %copy-start.30 = (s32[8]{0:T(128)}, s32[8]{0:T(128)S(1)}, u32[]{:S(2)}) copy-start(s32[8]{0:T(128)S(1)} %get-tuple-element.16) | copy-start | bytes 100
  32.1 12.1 %copy-start.34 = (pred[8,32]{1,0:T(8,128)(4,1)}, pred[8,32]{1,0:T(8,128)(4,1)S(1)}, u32[]{:S(2)}) copy-start(pred[8,32]{1,0:T(8,128)(4,1)S(1)} %iota_compare_fusion.14) | copy-start | bytes 772
  32.2 12.0 %copy-start.35 = (pred[8,8]{1,0:T(8,128)(4,1)}, pred[8,8]{1,0:T(8,128)(4,1)S(1)}, u32[]{:S(2)}) copy-start(pred[8,8]{1,0:T(8,128)(4,1)S(1)} %iota_compare_fusion.13) | copy-start | bytes 196
  33.1 2.8 %copy-start.51 = (f32[8]{0:T(128)}, f32[8]{0:T(128)S(1)}, u32[]{:S(2)}) copy-start(f32[8]{0:T(128)S(1)} %neg.27) | copy-start | bytes 100
  36.0 8.7 %copy-start.20 = (f32[8,256]{1,0:T(8,128)}, f32[8,256]{1,0:T(8,128)S(1)}, u32[]{:S(2)}) copy-start(f32[8,256]{1,0:T(8,128)S(1)} %get-tuple-element.54) | copy-start | bytes 24580
  41.7 3.0 %copy-start.14 = (f32[768]{0:T(1024)}, f32[768]{0:T(1024)S(1)}, u32[]{:S(2)}) copy-start(f32[768]{0:T(1024)S(1)} %get-tuple-element.4) | copy-start | bytes 9220
  41.7 3.0 %copy-start.16 = (f32[768]{0:T(1024)}, f32[768]{0:T(1024)S(1)}, u32[]{:S(2)}) copy-start(f32[768]{0:T(1024)S(1)} %get-tuple-element.5) | copy-start | bytes 9220
  41.7 3.0 %copy-start.24 = (f32[768]{0:T(1024)}, f32[768]{0:T(1024)S(1)}, u32[]{:S(2)}) copy-start(f32[768]{0:T(1024)S(1)} %get-tuple-element.2) | copy-start | bytes 9220
  41.7 3.0 %copy-start.26 = (f32[768]{0:T(1024)}, f32[768]{0:T(1024)S(1)}, u32[]{:S(2)}) copy-start(f32[768]{0:T(1024)S(1)} %get-tuple-element.3) | copy-start | bytes 9220
  52.7 9.0 %copy-start.11 = (pred[8,32,8]{2,1,0:T(8,128)(4,1)S(1)}, pred[8,32,8]{2,1,0:T(8,128)(4,1)}, u32[]{:S(2)}) copy-start(pred[8,32,8]{2,1,0:T(8,128)(4,1)} %broadcast_and_fusion) | copy-start | bytes 6148
  52.7 9.7 %copy-start.42 = (s32[64]{0:T(128)S(1)}, s32[64]{0:T(128)}, u32[]{:S(2)}) copy-start(s32[64]{0:T(128)} %param.33) | copy-start | bytes 772
  52.7 9.7 %copy-start.43 = (s32[64]{0:T(128)S(1)}, s32[64]{0:T(128)}, u32[]{:S(2)}) copy-start(s32[64]{0:T(128)} %get-tuple-element.11) | copy-start | bytes 772
  52.7 9.7 %copy-start.46 = (s32[64]{0:T(128)S(1)}, s32[64]{0:T(128)}, u32[]{:S(2)}) copy-start(s32[64]{0:T(128)} %copy-done.45) | copy-start | bytes 772
  52.7 10.6 %copy-start.49 = (f32[8,256]{1,0:T(8,128)S(1)}, f32[8,256]{1,0:T(8,128)}, u32[]{:S(2)}) copy-start(f32[8,256]{1,0:T(8,128)} %param.24) | copy-start | bytes 24580
  52.7 10.6 %copy-start.52 = (f32[8]{0:T(128)S(1)}, f32[8]{0:T(128)}, u32[]{:S(2)}) copy-start(f32[8]{0:T(128)} %copy-done.51) | copy-start | bytes 100
  52.7 12.0 %copy-start = (bf16[256,512]{1,0:T(8,128)(2,1)S(1)}, bf16[256,512]{1,0:T(8,128)(2,1)}, u32[]{:S(2)}) copy-start(bf16[256,512]{1,0:T(8,128)(2,1)} %param.21) | copy-start | bytes 786436
  52.7 48.9 %all-to-all-start = ((bf16[32,208,128]{2,1,0:T(8,128)(2,1)}), bf16[32,208,128]{2,1,0:T(8,128)(2,1)S(1)}, u32[]{:S(2)}, u32[]{:S(2)}) async-start(bf16[32,208,128]{2,1,0:T(8,128)(2,1)} %pad.12), calls=%async_computation | async-start | bytes 3407872 | tf_op jit(solution)/shard_map/all_to_all | solution.py:140
  62.7 40.3 %copy-start.36 = (pred[256]{0:T(512)(128)(4,1)}, pred[256]{0:T(512)(128)(4,1)S(1)}, u32[]{:S(2)}) copy-start(pred[256]{0:T(512)(128)(4,1)S(1)} %or.10) | copy-start | bytes 772
  64.0 39.1 %copy-start.32 = (f32[8,256]{1,0:T(8,128)}, f32[8,256]{1,0:T(8,128)S(1)}, u32[]{:S(2)}) copy-start(f32[8,256]{1,0:T(8,128)S(1)} %get-tuple-element.52) | copy-start | bytes 24580
  67.1 35.9 %copy-start.22 = (s32[256]{0:T(256)}, s32[256]{0:T(256)S(1)}, u32[]{:S(2)}) copy-start(s32[256]{0:T(256)S(1)} %select_select_fusion.1) | copy-start | bytes 3076
  108.4 5.4 %copy-start.41 = (s32[64]{0:T(128)S(1)}, s32[64]{0:T(128)}, u32[]{:S(2)}) copy-start(s32[64]{0:T(128)} %copy-done.40) | copy-start | bytes 772
  112.9 10.8 %copy-start.17 = (f32[768]{0:T(1024)S(1)}, f32[768]{0:T(1024)}, u32[]{:S(2)}) copy-start(f32[768]{0:T(1024)} %copy-done.16) | copy-start | bytes 9220
  112.9 10.8 %copy-start.23 = (s32[256]{0:T(256)S(1)}, s32[256]{0:T(256)}, u32[]{:S(2)}) copy-start(s32[256]{0:T(256)} %copy-done.22) | copy-start | bytes 3076
  113.8 11.4 %copy-start.2 = (bf16[255,768]{1,0:T(8,128)(2,1)S(1)}, bf16[255,768]{1,0:T(8,128)(2,1)}, u32[]{:S(2)}) copy-start(bf16[255,768]{1,0:T(8,128)(2,1)} %fusion.42) | copy-start | bytes 1175044
  113.8 11.4 %copy-start.15 = (f32[768]{0:T(1024)S(1)}, f32[768]{0:T(1024)}, u32[]{:S(2)}) copy-start(f32[768]{0:T(1024)} %copy-done.14) | copy-start | bytes 9220
  115.3 11.0 %copy-start.25 = (f32[768]{0:T(1024)S(1)}, f32[768]{0:T(1024)}, u32[]{:S(2)}) copy-start(f32[768]{0:T(1024)} %copy-done.24) | copy-start | bytes 9220
  116.1 10.2 %copy-start.27 = (f32[768]{0:T(1024)S(1)}, f32[768]{0:T(1024)}, u32[]{:S(2)}) copy-start(f32[768]{0:T(1024)} %copy-done.26) | copy-start | bytes 9220
  116.1 10.2 %copy-start.38 = (s32[6]{0:T(128)S(1)}, s32[6]{0:T(128)}, u32[]{:S(2)}) copy-start(s32[6]{0:T(128)} %get-tuple-element.55) | copy-start | bytes 76
  116.1 10.2 %copy-start.39 = (s32[6]{0:T(128)S(1)}, s32[6]{0:T(128)}, u32[]{:S(2)}) copy-start(s32[6]{0:T(128)} %get-tuple-element.56) | copy-start | bytes 76
  116.1 10.2 %copy-start.44 = (s32[256]{0:T(256)S(1)}, s32[256]{0:T(256)}, u32[]{:S(2)}) copy-start(s32[256]{0:T(256)} %get-tuple-element.43) | copy-start | bytes 3076
  116.1 10.2 %copy-start.47 = (pred[256]{0:T(512)(128)(4,1)S(1)}, pred[256]{0:T(512)(128)(4,1)}, u32[]{:S(2)}) copy-start(pred[256]{0:T(512)(128)(4,1)} %get-tuple-element.37) | copy-start | bytes 772
  116.1 10.2 %copy-start.48 = (pred[256]{0:T(512)(128)(4,1)S(1)}, pred[256]{0:T(512)(128)(4,1)}, u32[]{:S(2)}) copy-start(pred[256]{0:T(512)(128)(4,1)} %get-tuple-element.38) | copy-start | bytes 772
  116.1 18.0 %all-to-all-start.1 = ((bf16[32,48,128]{2,1,0:T(8,128)(2,1)}), bf16[32,48,128]{2,1,0:T(8,128)(2,1)S(1)}, u32[]{:S(2)}, u32[]{:S(2)}) async-start(bf16[32,48,128]{2,1,0:T(8,128)(2,1)} %pad_maximum_fusion.2), calls=%async_computation.1 | async-start | bytes 786432 | tf_op jit(solution)/shard_map/all_to_all | solution.py:173
  123.7 2.7 %copy-start.7 = (bf16[253,768]{1,0:T(8,128)(2,1)S(1)}, bf16[253,768]{1,0:T(8,128)(2,1)}, u32[]{:S(2)}) copy-start(bf16[253,768]{1,0:T(8,128)(2,1)} %fusion.40) | copy-start | bytes 1165828
  127.1 7.1 %copy-start.28 = (f32[256,8]{0,1:T(8,128)S(1)}, f32[256,8]{0,1:T(8,128)}, u32[]{:S(2)}) copy-start(f32[256,8]{0,1:T(8,128)} %get-tuple-element.53) | copy-start | bytes 24580
  127.1 7.4 %copy-start.6 = (bf16[256,512]{0,1:T(8,128)(2,1)S(1)}, bf16[256,512]{0,1:T(8,128)(2,1)}, u32[]{:S(2)}) copy-start(bf16[256,512]{0,1:T(8,128)(2,1)} %copy-done.5) | copy-start | bytes 786436
  127.1 7.4 %copy-start.8 = (f32[256,256]{1,0:T(8,128)S(1)}, f32[256,256]{1,0:T(8,128)}, u32[]{:S(2)}) copy-start(f32[256,256]{1,0:T(8,128)} %fusion.59) | copy-start | bytes 786436
  127.1 7.4 %copy-start.12 = (pred[256,256]{1,0:T(8,128)(4,1)S(1)}, pred[256,256]{1,0:T(8,128)(4,1)}, u32[]{:S(2)}) copy-start(pred[256,256]{1,0:T(8,128)(4,1)} %iota_compare_fusion.5) | copy-start | bytes 196612
  127.1 7.4 %copy-start.21 = (f32[8,256]{1,0:T(8,128)S(1)}, f32[8,256]{1,0:T(8,128)}, u32[]{:S(2)}) copy-start(f32[8,256]{1,0:T(8,128)} %copy-done.20) | copy-start | bytes 24580
  127.1 7.4 %copy-start.31 = (f32[8,256]{1,0:T(8,128)S(1)}, f32[8,256]{1,0:T(8,128)}, u32[]{:S(2)}) copy-start(f32[8,256]{1,0:T(8,128)} %get-tuple-element.31) | copy-start | bytes 24580
  127.1 7.4 %copy-start.50 = (f32[8]{0:T(128)S(1)}, f32[8]{0:T(128)}, u32[]{:S(2)}) copy-start(f32[8]{0:T(128)} %param.28) | copy-start | bytes 100
  134.5 1.1 copy-start.19
  134.5 1.3 copy-start.18
  136.3 1.3 copy-start.3
  137.2 19.5 %copy-start.29 = (f32[512]{0:T(512)S(1)}, f32[512]{0:T(512)}, u32[]{:S(2)}) copy-start(f32[512]{0:T(512)} %param.29) | copy-start | bytes 6148
  137.2 19.5 %copy-start.37 = (pred[256]{0:T(512)(128)(4,1)S(1)}, pred[256]{0:T(512)(128)(4,1)}, u32[]{:S(2)}) copy-start(pred[256]{0:T(512)(128)(4,1)} %copy-done.36) | copy-start | bytes 772
  (9 other events, 8.2 us)

commit v2 on v1

v2 whole, which is shorter than its diff:
```python
import functools

import jax
import jax.numpy as jnp
from jax import lax
from jax.experimental import pallas as pl
from jax.experimental.pallas import tpu as pltpu
from jax.sharding import PartitionSpec as P

BR_PER = 2
EPSILON = 1e-05
SLOTS = 2
MISC = 48
HALO = 16
BF = jnp.bfloat16
F32 = jnp.float32
I32 = jnp.int32
HIGH = lax.Precision.HIGHEST
FAR = -1e30


def iota(shape, axis):
    return lax.broadcasted_iota(I32, shape, axis)


def log_row(value, part):
    at = 3 * value + part
    return (at // 2) * 8 + 6 + at % 2


def parts_of(value, count):
    found = []
    for _ in range(count):
        part = value.astype(BF)
        found.append(part)
        value = value - part.astype(F32)
    return found


def expand(columns, head_size):
    rows, heads = columns.shape
    low = iota((rows, 2 * head_size), 1) < head_size
    pairs = [
        jnp.where(low, columns[:, h : h + 1], columns[:, h + 1 : h + 2]) for h in range(0, heads, 2)
    ]
    return jnp.concatenate(pairs, axis=1)


def step_and_logs(raw, rates):
    step = jnp.maximum(raw, 0.0) + jnp.log1p(jnp.exp(-jnp.abs(raw)))
    log_decay = -rates * step
    length = raw.shape[1]
    upper = (iota((length, length), 0) <= iota((length, length), 1)).astype(F32)
    cumulative = jnp.dot(log_decay, upper, precision=HIGH, preferred_element_type=F32)
    return step, log_decay, cumulative


def silu(value):
    return value * jax.nn.sigmoid(value)


def mixed_rows(values, scores, step, cumulative, mask, out_ref, extra):
    length, channels = values.shape
    heads = step.shape[0]
    size = channels // heads
    columns = cumulative.T
    half = length // 2
    low = iota((half, 2 * size), 1) < size
    for first, width in ((0, half), (half, length)):
        rows = slice(first, first + half)
        kept = mask[rows, :width]
        score = scores[rows, :width]
        for h in range(0, heads, 2):
            lanes = slice(h * size, (h + 2) * size)
            sums = []
            for one in (h, h + 1):
                gap = columns[rows, one : one + 1] - cumulative[one : one + 1, :width]
                mixing = score * jnp.exp(jnp.where(kept, gap, FAR)) * step[one : one + 1, :width]
                sums.append(jnp.dot(mixing.astype(BF), values[:width, lanes], preferred_element_type=F32))
            out_ref[rows, lanes] = jnp.where(low, sums[0], sums[1]) + extra[rows, lanes]


def prefix_x_kernel(x_ref, halo_ref, dt_ref, rate_ref, taps_ref, xc_ref, cum_ref, step_ref, ext_ref):
    length = x_ref.shape[0]
    ext_ref[:HALO] = halo_ref[...].astype(F32)
    ext_ref[HALO:] = x_ref[...].astype(F32)
    taps = taps_ref[...].astype(F32)
    count = taps.shape[0]
    total = taps[0:1] * ext_ref[HALO - count + 1 : HALO - count + 1 + length]
    for i in range(1, count):
        first = HALO - count + 1 + i
        total = total + taps[i : i + 1] * ext_ref[first : first + length]
    xc_ref[...] = silu(total).astype(BF)
    step, _, cumulative = step_and_logs(dt_ref[...], rate_ref[...])
    cum_ref[...] = cumulative
    step_ref[...] = step


def prefix_state_kernel(
    meta_ref, wanted_ref, x_ref, halo_ref, bc_ref, bchalo_ref, taps_ref, xc_ref, cum_ref, step_ref,
    sent_ref, b_ref, c_ref, ext_ref, all_ref, *, base,
):
    length, channels = x_ref.shape
    width = bchalo_ref.shape[1]
    n_state = width // 2
    n_ctx = sent_ref.shape[0]
    heads = cum_ref.shape[0]
    bc = bc_ref[:, :width]
    ext_ref[:HALO] = bchalo_ref[...].astype(F32)
    ext_ref[HALO:] = bc.astype(F32)
    taps = taps_ref[...].astype(F32)
    count = taps.shape[0]
    total = taps[0:1] * ext_ref[HALO - count + 1 : HALO - count + 1 + length]
    for i in range(1, count):
        first = HALO - count + 1 + i
        total = total + taps[i : i + 1] * ext_ref[first : first + length]
    convolved = silu(total).astype(BF)
    b_rows = convolved[:, :n_state]
    b_ref[...] = b_rows
    c_ref[...] = convolved[:, n_state:]
    cumulative = cum_ref[...]
    step = step_ref[...]
    values = xc_ref[...].astype(F32)
    lane = iota((heads, length), 1)
    size = channels // heads

    def state(weight):
        weighted = (values * expand(weight.T, size)).astype(BF)
        return lax.dot_general(
            weighted, b_rows, (((0,), (0,)), ((), ())), preferred_element_type=F32
        )

    ends = [cumulative[:, length - 1 :]]
    local = state(jnp.exp(ends[0] - cumulative) * step)
    rows = channels // n_ctx
    for i, part in enumerate(parts_of(local, 2)):
        first = MISC + i * rows
        sent_ref[:, first : first + rows, :] = part.reshape(n_ctx, rows, n_state)
    for slot in range(SLOTS):
        position = meta_ref[base + slot]
        first = MISC + (2 + slot) * rows
        end = jnp.sum(jnp.where(lane == position, cumulative, 0.0), axis=1, keepdims=True)
        ends.append(end)

        @pl.when(position >= 0)
        def _():
            weight = jnp.exp(jnp.where(lane <= position, end - cumulative, FAR)) * step
            sent_ref[:, first : first + rows, :] = state(weight).astype(BF).reshape(n_ctx, rows, n_state)

        @pl.when(position < 0)
        def _():
            sent_ref[:, first : first + rows, :] = jnp.zeros((n_ctx, rows, n_state), BF)

    parts = [part for end in ends for part in parts_of(end, 3)]
    blank = jnp.zeros((heads, n_state), BF)
    groups = (channels + width) // n_state
    for g in range(groups):
        for k in range(2):
            at = 2 * g + k
            block = blank
            if at < len(parts):
                block = jnp.broadcast_to(parts[at].astype(F32), (heads, n_state)).astype(BF)
            first = HALO + length + k * heads
            all_ref[first : first + heads, g * n_state : (g + 1) * n_state] = block.astype(F32)
    all_ref[:HALO, :channels] = halo_ref[...].astype(F32)
    all_ref[:HALO, channels:] = bchalo_ref[...].astype(F32)
    all_ref[HALO : HALO + length, :channels] = x_ref[...].astype(F32)
    all_ref[HALO : HALO + length, channels:] = bc.astype(F32)
    depth = all_ref.shape[0]
    column = iota((n_ctx * 8, depth), 1)
    picker = (column == wanted_ref[...]).astype(BF)
    placed = jnp.dot(picker, all_ref[...].astype(BF), preferred_element_type=F32)
    for g in range(0, groups, 2):
        pair = [
            placed[:, (g + k) * n_state : (g + k + 1) * n_state].reshape(n_ctx, 8, n_state) for k in range(2)
        ]
        sent_ref[:, g * 8 : g * 8 + 16, :] = jnp.concatenate(pair, axis=1).astype(BF)


def prefix_mix_kernel(xc_ref, b_ref, c_ref, cum_ref, step_ref, skip_ref, y_ref):
    length = xc_ref.shape[0]
    scores = lax.dot_general(
        c_ref[...], b_ref[...], (((1,), (1,)), ((), ())), preferred_element_type=F32
    )
    mask = iota((length, length), 1) <= iota((length, length), 0)
    values = xc_ref[...]
    extra = values.astype(F32) * skip_ref[...]
    mixed_rows(values, scores, step_ref[...], cum_ref[...], mask, y_ref, extra)


def scan_kernel(meta_ref, got_ref, *rest, n_branch, bounds):
    extra_ref = rest[0] if len(rest) == 4 else None
    back_ref, entering_ref, bound_ref = rest[-3:]
    n_ctx, _, n_state = got_ref.shape
    rows = entering_ref.shape[1]

    def log_of(misc, value):
        found = [misc[r : r + 1] for r in (log_row(value, k) for k in range(3))]
        return found[0] + found[1] + found[2]

    state = jnp.zeros((rows, n_state), F32)
    for i in range(n_ctx):
        entering_ref[i] = state
        back_ref[i, :rows, :] = state.astype(BF)
        if i < n_ctx - 1:
            misc = got_ref[i, :16, :].astype(F32)
            local = got_ref[i, MISC : MISC + rows, :].astype(F32)
            local = local + got_ref[i, MISC + rows : MISC + 2 * rows, :].astype(F32)
            state = jnp.exp(log_of(misc, 0)) * state + local
    for j in range(bounds):
        block = meta_ref[n_branch + j]
        slot = meta_ref[n_branch + bounds + j]
        misc = got_ref[block, :MISC, :].astype(F32)
        log, part = log_of(misc, 1), got_ref[block, MISC + 2 * rows : MISC + 3 * rows, :].astype(F32)
        for other in range(1, SLOTS):
            first = MISC + (2 + other) * rows
            log = jnp.where(slot == other, log_of(misc, 1 + other), log)
            part = jnp.where(slot == other, got_ref[block, first : first + rows, :].astype(F32), part)
        if extra_ref is not None:
            tail = extra_ref[block, (bounds - SLOTS) * rows :, :].astype(F32)
            for more in range(bounds - SLOTS):
                here = slot == SLOTS + more
                three = tail[3 * more : 3 * more + 1] + tail[3 * more + 1 : 3 * more + 2] + tail[3 * more + 2 : 3 * more + 3]
                log = jnp.where(here, three, log)
                part = jnp.where(here, extra_ref[block, more * rows : (more + 1) * rows, :].astype(F32), part)
        bound_ref[j] = jnp.exp(log) * entering_ref[block] + part
    for o in range(n_ctx):
        for k in range(BR_PER):
            first = (1 + k) * rows
            back_ref[o, first : first + rows, :] = bound_ref[meta_ref[o * BR_PER + k]].astype(BF)


def segments(meta_ref, base, shape, axis):
    row = iota(shape, axis)
    segment = jnp.full(shape, BR_PER, I32)
    offset = row
    for k in range(BR_PER):
        start, size = meta_ref[base + k], meta_ref[base + BR_PER + k]
        inside = (row >= start) & (row < start + size)
        segment = jnp.where(inside, k, segment)
        offset = jnp.where(inside, row - start, offset)
    return segment, offset


def branch_kernel(
    meta_ref, x_ref, bc_ref, got_ref, dt_ref, rate_ref, xtaps_ref, taps_ref, skip_ref,
    y_ref, c_ref, seed_ref, ext_ref, *, base,
):
    length, channels = x_ref.shape
    n_ctx, _, n_state = got_ref.shape
    width = taps_ref.shape[1]
    ext_ref[:HALO] = jnp.zeros((HALO, channels + width), F32)
    ext_ref[HALO:, :channels] = x_ref[...].astype(F32)
    ext_ref[HALO:, channels:] = bc_ref[:, width:].astype(F32)
    misc = got_ref[0].astype(F32)
    for i in range(1, n_ctx):
        misc = misc + got_ref[i].astype(F32)
    groups = (channels + width) // n_state
    tails = jnp.concatenate([misc[g * 8 : (g + 1) * 8] for g in range(groups)], axis=1)
    tails = jnp.concatenate([tails, jnp.zeros_like(tails)], axis=0).astype(BF)
    taps = jnp.concatenate([xtaps_ref[...].astype(F32), taps_ref[...].astype(F32)], axis=1)
    count = taps.shape[0]
    tail = count - 1
    segment, offset = segments(meta_ref, base, (length, 1), 0)
    place = iota((length, 16), 1)
    total = None
    for i in range(count):
        shift = tail - i
        rows = ext_ref[HALO - shift : HALO - shift + length]
        if shift:
            ahead = (offset < shift) & (segment < BR_PER)
            picker = ahead & (place == segment * tail + tail - shift + offset)
            early = jnp.dot(picker.astype(BF), tails, preferred_element_type=F32)
            rows = jnp.where(offset >= shift, rows, 0.0) + early
        term = taps[i : i + 1] * rows
        total = term if total is None else total + term
    convolved = silu(total).astype(BF)
    values = convolved[:, :channels]
    b_rows = convolved[:, channels : channels + n_state]
    c_rows = convolved[:, channels + n_state :]
    c_ref[...] = c_rows
    step, log_decay, cumulative = step_and_logs(dt_ref[...], rate_ref[...])
    across, _ = segments(meta_ref, base, (1, length), 1)
    lane = iota(cumulative.shape, 1)
    before = cumulative - log_decay
    seed = jnp.zeros_like(cumulative)
    for k in range(BR_PER):
        first = jnp.sum(jnp.where(lane == meta_ref[base + k], before, 0.0), axis=1, keepdims=True)
        seed = jnp.where(across == k, jnp.exp(jnp.where(across == k, cumulative - first, 0.0)), seed)
    seed_ref[...] = seed
    scores = lax.dot_general(c_rows, b_rows, (((1,), (1,)), ((), ())), preferred_element_type=F32)
    mask = (segment == across) & (segment < BR_PER)
    mask = mask & (iota((length, length), 1) <= iota((length, length), 0))
    extra = values.astype(F32) * skip_ref[...]
    mixed_rows(values, scores, step, cumulative, mask, y_ref, extra)


def gate_kernel(
    meta_ref, y_ref, c_ref, cum_ref, z_ref, by_ref, bc_ref, seed_ref, bz_ref, back_ref,
    g_ref, bg_ref, sq_ref, *, base,
):
    length, channels = y_ref.shape
    heads = cum_ref.shape[0]
    size = channels // heads
    n_ctx, _, n_state = back_ref.shape
    rows = channels // n_ctx

    def from_state(c_rows, which):
        state = back_ref[:, which * rows : (which + 1) * rows, :].reshape(channels, n_state)
        return lax.dot_general(c_rows, state, (((1,), (1,)), ((), ())), preferred_element_type=F32)

    def squares(gated):
        ones = jnp.ones((8, channels), F32)
        return lax.dot_general(
            ones, gated * gated, (((1,), (1,)), ((), ())), precision=HIGH, preferred_element_type=F32
        )

    y = y_ref[...] + expand(jnp.exp(cum_ref[...]).T, size) * from_state(c_ref[...], 0)
    gated = y * silu(z_ref[...].astype(F32))
    g_ref[...] = gated
    sums = squares(gated)
    segment, _ = segments(meta_ref, base, (length, 1), 0)
    c_rows = bc_ref[...]
    seeded = from_state(c_rows, BR_PER)
    for k in range(BR_PER - 1):
        seeded = jnp.where(segment == k, from_state(c_rows, 1 + k), seeded)
    y = by_ref[...] + expand(seed_ref[...].T, size) * seeded
    gated = y * silu(bz_ref[...].astype(F32))
    bg_ref[...] = gated
    more = squares(gated)
    half = length // 2
    row = iota((8, half), 0)
    packed = jnp.where(
        row == 0,
        sums[:, :half],
        jnp.where(row == 1, sums[:, half:], jnp.where(row == 2, more[:, :half], more[:, half:])),
    )
    for i in range(sq_ref.shape[0]):
        sq_ref[i] = packed


def norm_kernel(meta_ref, sq_ref, g_ref, bg_ref, gain_ref, out_ref, bout_ref, *, base):
    length, channels = g_ref.shape
    n_tp = sq_ref.shape[0]
    total = sq_ref[0]
    for i in range(1, n_tp):
        total = total + sq_ref[i]
    factor = lax.rsqrt(total / (channels * n_tp) + EPSILON).T
    gain = gain_ref[...]
    half = length // 2
    segment, _ = segments(meta_ref, base, (length, 1), 0)
    for k in range(2):
        rows = slice(k * half, (k + 1) * half)
        out_ref[rows] = (g_ref[rows] * factor[:, k : k + 1] * gain).astype(BF)
        scaled = bg_ref[rows] * factor[:, 2 + k : 3 + k] * gain
        bout_ref[rows] = jnp.where(segment[rows] < BR_PER, scaled, 0.0).astype(BF)


def call(kernel, outs, scratch, args, smem=0, blocks=None):
    blocks = blocks or {}
    specs = []
    for i in range(len(args)):
        if i < smem:
            specs.append(pl.BlockSpec(memory_space=pltpu.SMEM))
        elif i in blocks:
            specs.append(pl.BlockSpec(blocks[i], lambda _, n=len(blocks[i]): (0,) * n))
        else:
            specs.append(pl.BlockSpec(args[i].shape, lambda _, n=args[i].ndim: (0,) * n))
    return pl.pallas_call(
        kernel,
        grid=(1,),
        in_specs=specs,
        out_specs=[pl.BlockSpec(s, lambda _, n=len(s): (0,) * n) for s, _ in outs],
        out_shape=[jax.ShapeDtypeStruct(s, t) for s, t in outs],
        scratch_shapes=[pltpu.VMEM(s, t) for s, t in scratch],
        compiler_params=pltpu.CompilerParams(vmem_limit_bytes=48 * 2**20),
        cost_estimate=pl.CostEstimate(flops=2 * 10**9, bytes_accessed=4 * 10**6, transcendentals=10**6),
    )(*args)


def more_states(xc, b_rows, step, cumulative, positions, n_ctx):
    length, channels = xc.shape
    heads = step.shape[0]
    n_state = b_rows.shape[1]
    row = jnp.arange(length, dtype=I32)
    hit = row[None, None, :] == positions[:, None, None]
    ends = jnp.sum(jnp.where(hit, cumulative[None], 0.0), axis=2)
    inside = (row[None, :] <= positions[:, None])[:, None, :]
    weight = jnp.exp(jnp.where(inside, ends[:, :, None] - cumulative[None], FAR)) * step[None]
    values = xc.reshape(length, heads, -1).astype(F32)
    weighted = (jnp.transpose(weight, (0, 2, 1))[:, :, :, None] * values[None]).astype(BF)
    states = jnp.einsum("jshp,sn->jhpn", weighted, b_rows, preferred_element_type=F32).astype(BF)
    rows = channels // n_ctx
    count = positions.shape[0]
    states = jnp.transpose(states.reshape(count, n_ctx, rows, n_state), (1, 0, 2, 3))
    parts = []
    rest = ends
    for _ in range(3):
        part = lax.reduce_precision(rest, 8, 7)
        parts.append(part)
        rest = rest - part
    logs = jnp.stack(parts, axis=1).reshape(3 * count, heads).T
    logs = jnp.repeat(logs, n_ctx // heads, axis=0)
    logs = jnp.broadcast_to(logs[:, :, None], (n_ctx, 3 * count, n_state)).astype(BF)
    sent = jnp.concatenate([states.reshape(n_ctx, count * rows, n_state), logs], axis=1)
    return jnp.pad(sent, ((0, 0), (0, -sent.shape[1] % 16), (0, 0)))


def body(
    prefix_x, prefix_z, prefix_bc, prefix_dt, branch_x, branch_z, branch_bc, branch_dt,
    conv_x, conv_bc, decay_rate, skip, norm_gain, bound_pos, branch_owner, branch_parent, branch_len,
):
    n_ctx = lax.axis_size("ctx")
    n_tp = lax.axis_size("tp")
    me = lax.axis_index("ctx")
    length, channels = prefix_x.shape
    heads = decay_rate.shape[0]
    width = prefix_bc.shape[1]
    n_state = width // 2
    rows = channels // n_ctx
    bounds = bound_pos.shape[0]
    branches = branch_owner.shape[0]
    tail = conv_x.shape[0] - 1
    onward = [(i, i + 1) for i in range(n_ctx - 1)]

    own = jnp.concatenate([prefix_bc, branch_bc], axis=1)
    gathered = lax.all_to_all(
        jnp.broadcast_to(own[None], (n_tp, *own.shape)), "tp", 0, 0, tiled=True
    ).reshape(length, 2 * width)
    halo = lax.ppermute(prefix_x[length - HALO :], "ctx", onward)
    bc_halo = lax.ppermute(gathered[length - HALO :, :width], "ctx", onward)
    rates = decay_rate[:, None]
    skips = jnp.repeat(skip, channels // heads)[None]
    gain = norm_gain[None]

    block_of = bound_pos // length
    at = bound_pos - block_of * length
    order = jnp.arange(bounds, dtype=I32)
    slot_of = jnp.sum(
        ((block_of[:, None] == block_of[None, :]) & (order[None, :] < order[:, None])).astype(I32), axis=1
    )
    border = jnp.arange(branches, dtype=I32)
    earlier = (branch_owner[:, None] == branch_owner[None, :]) & (border[None, :] < border[:, None])
    key = branch_owner * BR_PER + jnp.sum(earlier.astype(I32), axis=1)
    start = jnp.sum(jnp.where(earlier, branch_len[None, :], 0), axis=1)
    place = jnp.arange(n_ctx * BR_PER, dtype=I32)
    chosen = place[:, None] == key[None, :]
    parent_of = jnp.sum(jnp.where(chosen, branch_parent[None, :], 0), axis=1)
    mine = (me * BR_PER + jnp.arange(BR_PER, dtype=I32))[:, None] == key[None, :]
    my_len = jnp.sum(jnp.where(mine, branch_len[None, :], 0), axis=1)
    my_start = jnp.sum(jnp.where(mine, start[None, :], 0), axis=1)
    slot_here = (block_of == me)[None, :] & (slot_of[None, :] == order[:, None])
    positions = jnp.sum(jnp.where(slot_here, at[None, :] + 1, 0), axis=1) - 1
    meta = jnp.concatenate([parent_of, block_of, slot_of, positions, my_start, my_len])
    at_positions = branches + 2 * bounds
    at_mine = at_positions + bounds
    local_at = jnp.where(block_of == me, at + HALO - tail + 1, -HALO * length)
    parent_at = jnp.sum(jnp.where(parent_of[:, None] == order[None, :], local_at[None, :], 0), axis=1)
    k = jnp.arange(8, dtype=I32)
    tail_at = jnp.where(k[None, :] < tail, parent_at[0::2, None], parent_at[1::2, None]) + (k % tail)[None, :]
    head_of = jnp.arange(n_ctx, dtype=I32) // (n_ctx // heads)
    log_at = HALO + length + (k[None, :] - 2 * tail) * heads + head_of[:, None]
    wanted = jnp.where(k[None, :] < 2 * tail, tail_at, log_at).reshape(-1, 1)

    xc, cumulative, step = call(
        prefix_x_kernel,
        [((length, channels), BF), ((heads, length), F32), ((heads, length), F32)],
        [((HALO + length, channels), F32)],
        [prefix_x, halo, prefix_dt, rates, conv_x],
    )
    sent, b_rows, c_rows = call(
        functools.partial(prefix_state_kernel, base=at_positions),
        [((n_ctx, MISC + (2 + SLOTS) * rows, n_state), BF), ((length, n_state), BF), ((length, n_state), BF)],
        [((HALO + length, width), F32), ((HALO + length + 2 * heads, channels + width), F32)],
        [meta, wanted, prefix_x, halo, gathered, bc_halo, conv_bc, xc, cumulative, step],
        smem=1,
    )
    got = lax.all_to_all(sent, "ctx", 0, 0, tiled=True)
    [y] = call(
        prefix_mix_kernel,
        [((length, channels), F32)],
        [],
        [xc, b_rows, c_rows, cumulative, step, skips],
    )

    scan = functools.partial(scan_kernel, n_branch=branches, bounds=bounds)
    scan_out = [((n_ctx, (1 + BR_PER) * rows, n_state), BF)]
    scan_scratch = [((n_ctx, rows, n_state), F32), ((bounds, rows, n_state), F32)]

    def usual():
        return call(scan, scan_out, scan_scratch, [meta, got], smem=1)[0]

    def crowded():
        extra = more_states(xc, b_rows, step, cumulative, positions[SLOTS:], n_ctx)
        extra = lax.all_to_all(extra, "ctx", 0, 0, tiled=True)
        return call(scan, scan_out, scan_scratch, [meta, got, extra], smem=1)[0]

    back = lax.cond(jnp.max(slot_of) >= SLOTS, crowded, usual)
    back = lax.all_to_all(back, "ctx", 0, 0, tiled=True)

    branch_y, branch_c, seed = call(
        functools.partial(branch_kernel, base=at_mine),
        [((length, channels), F32), ((length, n_state), BF), ((heads, length), F32)],
        [((HALO + length, channels + width), F32)],
        [meta, branch_x, gathered, got, branch_dt, rates, conv_x, conv_bc, skips],
        smem=1,
        blocks={3: (n_ctx, MISC, n_state)},
    )
    gated, branch_gated, squares = call(
        functools.partial(gate_kernel, base=at_mine),
        [((length, channels), F32), ((length, channels), F32), ((n_tp, 8, length // 2), F32)],
        [],
        [meta, y, c_rows, cumulative, prefix_z, branch_y, branch_c, seed, branch_z, back],
        smem=1,
    )
    squares = lax.all_to_all(squares, "tp", 0, 0, tiled=True)
    return tuple(
        call(
            functools.partial(norm_kernel, base=at_mine),
            [((length, channels), BF), ((length, channels), BF)],
            [],
            [meta, squares, gated, branch_gated, gain],
            smem=1,
        )
    )


def solution(mesh):
    both = P(("ctx", "tp"), None)
    in_specs = (
        P("ctx", "tp"), P("ctx", "tp"), both, P("tp", "ctx"),
        P("ctx", "tp"), P("ctx", "tp"), both, P("tp", "ctx"),
        P(None, "tp"), P(), P("tp"), P("tp"), P("tp"), P(), P(), P(), P(),
    )
    out_specs = (P("ctx", "tp"), P("ctx", "tp"))
    return jax.shard_map(body, mesh=mesh, in_specs=in_specs, out_specs=out_specs, check_vma=False)
```

time: 160 us -> 110 us (0.69)
  blocking collectives: 43.9 us -> 14.9 us
  other arithmetic: 25.4 us -> 6.38 us
  starting transfers between devices: 19.6 us -> 37.2 us
  local copies, waits for them, and re-layouts: 17.9 us -> 2.37 us
  matrix products: 13.9 us -> 0 us
  Pallas kernels: 0 us -> 12.9 us
  waiting for transfers between devices: 36.3 us -> 34.4 us
    all_gather x2 -> x0, blocking collectives: 43.9 us -> none  [the longest x1 25.2 us: body(): lax.all_gather(jnp.concatenate([prefix_bc, branch_bc], axis=1), 'tp', axi...]
    all_to_all x0 -> x1, blocking collectives: none -> 14.9 us  [body(): squares = lax.all_to_all(squares, 'tp', 0, 0, tiled=True)]
    dot_general x18 -> x0, matrix products: 13.9 us -> none  [the longest x3 3.24 us: body(): jnp.dot(picker, tail_rows, preferred_element_type=F32).astype(BF)]
    pallas_call x0 -> x7, Pallas kernels: none -> 12.9 us  [call(): pl.pallas_call(kernel, grid=(1,), in_specs=specs, out_specs=[pl.BlockSpec...]
    all_to_all x0 -> x1, starting transfers between devices: none -> 11.3 us  [body(): lax.all_to_all(jnp.broadcast_to(own[None], (n_tp, *own.shape)), 'tp', 0,...]
    all_to_all x1, waiting for transfers between devices: 31 us -> 20.9 us  [body(): got = lax.all_to_all(sent, 'ctx', 0, 0, tiled=True)]
    all_to_all x0 -> x1, waiting for transfers between devices: none -> 6.13 us  [body(): lax.all_to_all(jnp.broadcast_to(own[None], (n_tp, *own.shape)), 'tp', 0,...]
    concatenate x8 -> x1, other arithmetic: 5.69 us -> 0.72 us  [body(): own = jnp.concatenate([prefix_bc, branch_bc], axis=1)]
  transfers between devices with their start and end apart: 3 -> 5, of which waited for: 2 -> 3; matrix products, arithmetic and copies ran while one was open for 17% -> 7% of each run, Pallas kernels for 0% -> 4%
where the time goes in v2:
time: 110 us
  starting transfers between devices  37.2 us (34%)
  waiting for transfers between devices  34.4 us (31%)
  blocking collectives  14.9 us (14%)
  Pallas kernels  12.9 us (12%)
  other arithmetic  6.38 us (6%)
  local copies, waits for them, and re-layouts  2.37 us (2%)
  between operations  1.47 us (1%)
    all_to_all x1, waiting for transfers between devices, body(): got = lax.all_to_all(sent, 'ctx', 0, 0, tiled=True)  20.9 us
    all_to_all x1, blocking collectives, body(): squares = lax.all_to_all(squares, 'tp', 0, 0, tiled=True)  14.9 us
    pallas_call x7, Pallas kernels, call(): pl.pallas_call(kernel, grid=(1,), in_specs=specs, out_specs=[pl.BlockSpec...  12.9 us
    all_to_all x1, starting transfers between devices, body(): lax.all_to_all(jnp.broadcast_to(own[None], (n_tp, *own.shape)), 'tp', 0,...  11.3 us
    all_to_all x1, starting transfers between devices, body(): got = lax.all_to_all(sent, 'ctx', 0, 0, tiled=True)  10.4 us
    all_to_all x1, starting transfers between devices, body(): back = lax.all_to_all(back, 'ctx', 0, 0, tiled=True)  8.19 us
    all_to_all x1, waiting for transfers between devices, body(): back = lax.all_to_all(back, 'ctx', 0, 0, tiled=True)  7.28 us
    all_to_all x1, waiting for transfers between devices, body(): lax.all_to_all(jnp.broadcast_to(own[None], (n_tp, *own.shape)), 'tp', 0,...  6.13 us
  transfers between devices with their start and end apart: 5, of which 3 were waited for; matrix products, arithmetic and copies ran while one was open for 7% of the time, Pallas kernels for 4%

profile of v2, /device:TPU:1, one launch (start us, length us, event | category | flops | bytes accessed | tf_op | source)
XLA Modules:
  0.0 109.6 jit_solution(6634804040858284480)
XLA Ops:
  0.6 0.0 copy-start
  0.6 0.0 copy-start.10
  0.7 0.8 slice.15
  1.4 4.0 %collective-permute-start = (bf16[16,512]{1,0:T(8,128)(2,1)S(1)}, bf16[16,512]{1,0:T(8,128)(2,1)S(1)}, u32[]{:S(2)}, u32[]{:S(2)}) collective-permute-start(bf16[16,512]{1,0:T(8,128)(2,1)S(1)} %slice.15), channel_id=1, source_target_pairs={{0,16},{16,32},{32,48},{48,64},{64,80},{80,96},{96,112},{112,128},... | collective-permute-start | bytes 49160 | tf_op jit(solution)/shard_map/ppermute | solution.py:430
  5.5 0.7 pad_maximum_fusion.1
  6.2 0.7 broadcast_in_dim.212
  6.9 11.3 %all-to-all-start.1 = ((bf16[16,16,512]{2,1,0:T(8,128)(2,1)}), bf16[16,16,512]{2,1,0:T(8,128)(2,1)S(1)}, u32[]{:S(2)}, u32[]{:S(2)}) async-start(bf16[16,16,512]{2,1,0:T(8,128)(2,1)} %broadcast_in_dim.212), calls=%async_computation.1 | async-start | bytes 524288 | tf_op jit(solution)/shard_map/all_to_all | solution.py:427
  18.2 0.7 add_select_fusion.1
  18.9 0.2 convert_reduce_fusion.1
  19.0 0.7 broadcast_add_fusion.1
  19.7 0.1 select_reduce_fusion.4
  19.8 0.9 select_reduce_fusion.1
  20.7 0.7 multiply_add_fusion.1
  21.4 0.8 select_reduce_fusion.2
  22.2 0.1 select_reduce_fusion.3
  22.3 0.1 slice.16
  22.4 0.1 slice.17
  22.5 0.1 add_select_fusion
  22.6 0.9 fusion.14
  23.5 0.1 select_n.103.wanted_ref
  23.6 0.0 copy-done.10
  23.6 0.1 copy.33.rate_ref
  23.7 0.1 concatenate.9.meta_ref
  23.8 6.1 %all-to-all-done.1 = bf16[16,16,512]{2,1,0:T(8,128)(2,1)S(1)} async-done(((bf16[16,16,512]{2,1,0:T(8,128)(2,1)}), bf16[16,16,512]{2,1,0:T(8,128)(2,1)S(1)}, u32[]{:S(2)}, u32[]{:S(2)}) %all-to-all-start.1) | async-done | bytes 262176 | tf_op jit(solution)/shard_map/all_to_all | solution.py:427
  29.9 3.3 %collective-permute-start.1 = (bf16[16,256]{1,0:T(8,128)(2,1)S(1)}, bf16[16,256]{1,0:T(8,128)(2,1)S(1)}, u32[]{:S(2)}, u32[]{:S(2)}) collective-permute-start(bf16[16,256]{1,0:T(8,128)(2,1)S(1)} %slice.19), channel_id=1, source_target_pairs={{0,16},{16,32},{32,48},{48,64},{64,80},{80,96},{96,112},{112,128},... | collective-permute-start | bytes 24584 | tf_op jit(solution)/shard_map/ppermute | solution.py:431
  33.2 0.0 collective-permute-done.halo_ref
  33.3 0.8 shard_map.176
  34.0 0.0 collective-permute-done.1.bchalo_ref
  34.0 0.0 copy-done.7
  34.1 3.7 %shard_map.177 = (bf16[32,112,128]{2,1,0:T(8,128)(2,1)}, bf16[256,128]{1,0:T(8,128)(2,1)S(1)}, bf16[256,128]{1,0:T(8,128)(2,1)S(1)}) custom-call(s32[92]{0:T(128)S(1)} %concatenate.9.meta_ref, s32[256,1]{1,0:T(8,128)S(1)} %select_n.103.wanted_ref, bf16[256,512]{1,0:T(8,128)(2,1)S(1)} %copy-done, bf16[16,512]{1,0:T(8,128)(2,1)S(1)} %collective-permute-done.halo_ref, ...), custom_call_target="tpu_custom_call" | custom-call | flops 2000000000 | bytes 4000000 | tf_op jit(solution)/shard_map/pallas_call | solution.py:369
  37.7 10.4 %all-to-all-start.2 = ((bf16[32,112,128]{2,1,0:T(8,128)(2,1)}), bf16[32,112,128]{2,1,0:T(8,128)(2,1)S(1)}, u32[]{:S(2)}, u32[]{:S(2)}) async-start(bf16[32,112,128]{2,1,0:T(8,128)(2,1)} %get-tuple-element.49), calls=%async_computation.2 | async-start | bytes 1835008 | tf_op jit(solution)/shard_map/all_to_all | solution.py:478
  48.2 0.6 reduce_max.9
  49.5 20.9 %all-to-all-done.2.got_ref = bf16[32,112,128]{2,1,0:T(8,128)(2,1)S(1)} async-done(((bf16[32,112,128]{2,1,0:T(8,128)(2,1)}), bf16[32,112,128]{2,1,0:T(8,128)(2,1)S(1)}, u32[]{:S(2)}, u32[]{:S(2)}) %all-to-all-start.2) | async-done | bytes 917536 | tf_op jit(solution)/shard_map/all_to_all | solution.py:478
  70.4 1.5 %conditional.1 = (bf16[32,48,128]{2,1,0:T(8,128)(2,1)}) conditional(s32[]{:T(128)} %convert_element_type.41, (s32[92]{0:T(128)S(1)}, bf16[32,112,128]{2,1,0:T(8,128)(2,1)S(1)}) %tuple.13, (s32[8]{0:T(128)S(1)}, f32[8,256]{1,0:T(8,128)S(1)}, f32[8,256]{1,0:T(8,128)S(1)}, bf16[256,512]{1,0:T(8,128)(2,1)S(1)}, bf16[256,128]{1,0:T(8,128)(2,1)S(1)}, ...), branch_computations={%region_9.10_spmd, %region_10.12_spmd} | conditional | flops 2207158784 | bytes 12621776 | solution.py:498
  70.4 1.5 %branch_0_fun.1 = bf16[32,48,128]{2,1,0:T(8,128)(2,1)} custom-call(s32[92]{0:T(128)S(1)} %get-tuple-element.10.meta_ref, bf16[32,112,128]{2,1,0:T(8,128)(2,1)S(1)} %get-tuple-element.22.got_ref), custom_call_target="tpu_custom_call" | custom-call | flops 2000000000 | bytes 4000000 | tf_op jit(solution)/shard_map/cond/branch_0_fun/pallas_call | solution.py:369
  71.9 8.2 %all-to-all-start.3 = ((bf16[32,48,128]{2,1,0:T(8,128)(2,1)}), bf16[32,48,128]{2,1,0:T(8,128)(2,1)S(1)}, u32[]{:S(2)}, u32[]{:S(2)}) async-start(bf16[32,48,128]{2,1,0:T(8,128)(2,1)} %get-tuple-element.93), calls=%async_computation.3 | async-start | bytes 786432 | tf_op jit(solution)/shard_map/all_to_all | solution.py:499
  80.1 0.1 broadcast_in_dim.213
  80.1 0.1 broadcast_in_dim_reshape.3.skip_ref
  80.2 0.8 shard_map.178.y_ref
  81.0 0.2 copy-done.1
  81.2 0.0 copy-done.5
  81.2 2.4 %shard_map.179 = (f32[256,512]{1,0:T(8,128)S(1)}, bf16[256,128]{1,0:T(8,128)(2,1)S(1)}, f32[8,256]{1,0:T(8,128)S(1)}) custom-call(s32[92]{0:T(128)S(1)} %concatenate.9.meta_ref, bf16[256,512]{1,0:T(8,128)(2,1)S(1)} %copy-done.1, bf16[256,512]{1,0:T(8,128)(2,1)S(1)} %bitcast.27, bf16[32,112,128]{2,1,0:T(8,128)(2,1)S(1)} %all-to-all-done.2.got_ref, ...), custom_call_target="tpu_custom_call" | custom-call | flops 2000000000 | bytes 4000000 | tf_op jit(solution)/shard_map/pallas_call | solution.py:369
  83.6 7.3 %all-to-all-done.3.back_ref = bf16[32,48,128]{2,1,0:T(8,128)(2,1)S(1)} async-done(((bf16[32,48,128]{2,1,0:T(8,128)(2,1)}), bf16[32,48,128]{2,1,0:T(8,128)(2,1)S(1)}, u32[]{:S(2)}, u32[]{:S(2)}) %all-to-all-start.3) | async-done | bytes 393248 | tf_op jit(solution)/shard_map/all_to_all | solution.py:499
  90.9 0.0 copy-done.2
  90.9 2.2 %shard_map.180 = (f32[256,512]{1,0:T(8,128)S(1)}, f32[256,512]{1,0:T(8,128)S(1)}, f32[16,8,128]{2,1,0:T(8,128)S(1)}) custom-call(s32[92]{0:T(128)S(1)} %concatenate.9.meta_ref, f32[256,512]{1,0:T(8,128)S(1)} %shard_map.178.y_ref, bf16[256,128]{1,0:T(8,128)(2,1)S(1)} %get-tuple-element.48.c_ref, f32[8,256]{1,0:T(8,128)} %copy-done.9, ...), custom_call_target="tpu_custom_call" | custom-call | flops 2000000000 | bytes 4000000 | tf_op jit(solution)/shard_map/pallas_call | solution.py:369
  93.1 14.9 %all_to_all.25.sq_ref = f32[16,8,128]{2,1,0:T(8,128)S(1)} all-to-all(f32[16,8,128]{2,1,0:T(8,128)S(1)} %get-tuple-element.53), channel_id=1, replica_groups=mesh['ctx'=32,'tp'=16] {'tp'}, dimensions={0} | all-to-all | bytes 131072 | tf_op jit(solution)/shard_map/all_to_all | solution.py:516
  108.0 0.0 copy-done.8
  108.0 1.6 %shard_map.181 = (bf16[256,512]{1,0:T(8,128)(2,1)}, bf16[256,512]{1,0:T(8,128)(2,1)}) custom-call(s32[92]{0:T(128)S(1)} %concatenate.9.meta_ref, f32[16,8,128]{2,1,0:T(8,128)S(1)} %all_to_all.25.sq_ref, f32[256,512]{1,0:T(8,128)S(1)} %get-tuple-element.54.g_ref, f32[256,512]{1,0:T(8,128)S(1)} %get-tuple-element.55.bg_ref, f32[1,512]{1,0:T(1,128)S(1)} %bitcast.28), custom_call_target="tpu_custom_call" | custom-call | flops 2000000000 | bytes 4000000 | tf_op jit(solution)/shard_map/pallas_call | solution.py:369
  (22 shorter events, 0.1 us)
Async XLA Ops:
  0.6 32.6 %copy-start = (bf16[256,512]{1,0:T(8,128)(2,1)S(1)}, bf16[256,512]{1,0:T(8,128)(2,1)}, u32[]{:S(2)}) copy-start(bf16[256,512]{1,0:T(8,128)(2,1)} %x_ref.4) | copy-start | bytes 786436
  0.6 23.0 %copy-start.10 = (f32[8]{0:T(128)S(1)}, f32[8]{0:T(128)}, u32[]{:S(2)}) copy-start(f32[8]{0:T(128)} %param.29) | copy-start | bytes 100
  0.7 32.6 %copy-start.4 = (f32[8,256]{1,0:T(8,128)S(1)}, f32[8,256]{1,0:T(8,128)}, u32[]{:S(2)}) copy-start(f32[8,256]{1,0:T(8,128)} %dt_ref.2) | copy-start | bytes 24580
  0.7 32.6 %copy-start.6 = (bf16[4,512]{1,0:T(4,128)(2,1)S(1)}, bf16[4,512]{1,0:T(4,128)(2,1)}, u32[]{:S(2)}) copy-start(bf16[4,512]{1,0:T(4,128)(2,1)} %xtaps_ref.1) | copy-start | bytes 12292
  1.4 31.8 %collective-permute-start = (bf16[16,512]{1,0:T(8,128)(2,1)S(1)}, bf16[16,512]{1,0:T(8,128)(2,1)S(1)}, u32[]{:S(2)}, u32[]{:S(2)}) collective-permute-start(bf16[16,512]{1,0:T(8,128)(2,1)S(1)} %slice.15), channel_id=1, source_target_pairs={{0,16},{16,32},{32,48},{48,64},{64,80},{80,96},{96,112},{112,128},... | collective-permute-start | bytes 49160 | tf_op jit(solution)/shard_map/ppermute | solution.py:430
  6.9 23.0 %all-to-all-start.1 = ((bf16[16,16,512]{2,1,0:T(8,128)(2,1)}), bf16[16,16,512]{2,1,0:T(8,128)(2,1)S(1)}, u32[]{:S(2)}, u32[]{:S(2)}) async-start(bf16[16,16,512]{2,1,0:T(8,128)(2,1)} %broadcast_in_dim.212), calls=%async_computation.1 | async-start | bytes 524288 | tf_op jit(solution)/shard_map/all_to_all | solution.py:427
  29.9 4.2 %copy-start.7 = (bf16[4,256]{1,0:T(4,128)(2,1)S(1)}, bf16[4,256]{1,0:T(4,128)(2,1)}, u32[]{:S(2)}) copy-start(bf16[4,256]{1,0:T(4,128)(2,1)} %taps_ref.5) | copy-start | bytes 6148
  29.9 4.1 %collective-permute-start.1 = (bf16[16,256]{1,0:T(8,128)(2,1)S(1)}, bf16[16,256]{1,0:T(8,128)(2,1)S(1)}, u32[]{:S(2)}, u32[]{:S(2)}) collective-permute-start(bf16[16,256]{1,0:T(8,128)(2,1)S(1)} %slice.19), channel_id=1, source_target_pairs={{0,16},{16,32},{32,48},{48,64},{64,80},{80,96},{96,112},{112,128},... | collective-permute-start | bytes 24584 | tf_op jit(solution)/shard_map/ppermute | solution.py:431
  34.0 46.2 %copy-start.9 = (f32[8,256]{1,0:T(8,128)}, f32[8,256]{1,0:T(8,128)S(1)}, u32[]{:S(2)}) copy-start(f32[8,256]{1,0:T(8,128)S(1)} %get-tuple-element.45.cum_ref) | copy-start | bytes 24580
  37.7 32.7 %all-to-all-start.2 = ((bf16[32,112,128]{2,1,0:T(8,128)(2,1)}), bf16[32,112,128]{2,1,0:T(8,128)(2,1)S(1)}, u32[]{:S(2)}, u32[]{:S(2)}) async-start(bf16[32,112,128]{2,1,0:T(8,128)(2,1)} %get-tuple-element.49), calls=%async_computation.2 | async-start | bytes 1835008 | tf_op jit(solution)/shard_map/all_to_all | solution.py:478
  70.4 9.7 %copy-start.11 = (f32[8]{0:T(128)S(1)}, f32[8]{0:T(128)}, u32[]{:S(2)}) copy-start(f32[8]{0:T(128)} %param.30) | copy-start | bytes 100
  71.9 19.0 %all-to-all-start.3 = ((bf16[32,48,128]{2,1,0:T(8,128)(2,1)}), bf16[32,48,128]{2,1,0:T(8,128)(2,1)S(1)}, u32[]{:S(2)}, u32[]{:S(2)}) async-start(bf16[32,48,128]{2,1,0:T(8,128)(2,1)} %get-tuple-element.93), calls=%async_computation.3 | async-start | bytes 786432 | tf_op jit(solution)/shard_map/all_to_all | solution.py:499
  80.2 1.0 copy-start.1
  80.2 1.0 copy-start.5
  81.2 9.7 %copy-start.2 = (bf16[256,512]{1,0:T(8,128)(2,1)S(1)}, bf16[256,512]{1,0:T(8,128)(2,1)}, u32[]{:S(2)}) copy-start(bf16[256,512]{1,0:T(8,128)(2,1)} %z_ref.1) | copy-start | bytes 786436
  81.2 9.7 %copy-start.3 = (bf16[256,512]{1,0:T(8,128)(2,1)S(1)}, bf16[256,512]{1,0:T(8,128)(2,1)}, u32[]{:S(2)}) copy-start(bf16[256,512]{1,0:T(8,128)(2,1)} %bz_ref.1) | copy-start | bytes 786436
  90.9 17.1 %copy-start.8 = (f32[512]{0:T(512)S(1)}, f32[512]{0:T(512)}, u32[]{:S(2)}) copy-start(f32[512]{0:T(512)} %param.31) | copy-start | bytes 6148

commit v3 on v2

--- a/solution.py
+++ b/solution.py
@@ -10,8 +10,10 @@
 BR_PER = 2
 EPSILON = 1e-05
 SLOTS = 2
-MISC = 48
+MISC = 16
+LOGS = 3
 HALO = 16
+EARLY = 2
 BF = jnp.bfloat16
 F32 = jnp.float32
 I32 = jnp.int32
@@ -21,11 +23,6 @@
 
 def iota(shape, axis):
     return lax.broadcasted_iota(I32, shape, axis)
-
-
-def log_row(value, part):
-    at = 3 * value + part
-    return (at // 2) * 8 + 6 + at % 2
 
 
 def parts_of(value, count):
@@ -96,11 +93,82 @@
     step_ref[...] = step
 
 
+def tail_tiles(meta_ref, base, bounds, height, rows):
+    row = iota((bounds * height, 1), 0)
+    wanted = jnp.full(row.shape, -1, I32)
+    for j in range(bounds):
+        wanted = jnp.where(row // height == j, meta_ref[base + j] + row % 4, wanted)
+    wanted = jnp.where(row % 4 < 3, wanted, -1)
+    picker = (iota((bounds * height, rows.shape[0]), 1) == wanted).astype(BF)
+    return jnp.dot(picker, rows, preferred_element_type=F32)
+
+
+def index_kernel(
+    me_ref, bound_ref, owner_ref, parent_ref, len_ref, x_ref,
+    meta_ref, tails_ref, last_ref, count_ref, start_ref, size_ref, *, n_ctx,
+):
+    me = me_ref[0]
+    length = x_ref.shape[0]
+    bounds = bound_ref.shape[0]
+    branches = owner_ref.shape[0]
+
+    def clear(o, _):
+        count_ref[o] = 0
+        count_ref[n_ctx + o] = 0
+        return 0
+
+    lax.fori_loop(0, n_ctx, clear, 0)
+
+    def place(b, _):
+        owner = owner_ref[b]
+        rank = count_ref[owner]
+        start = count_ref[n_ctx + owner]
+        size = len_ref[b]
+        count_ref[owner] = rank + 1
+        count_ref[n_ctx + owner] = start + size
+        at = owner * BR_PER + rank
+        meta_ref[at] = parent_ref[b]
+        start_ref[at] = start
+        size_ref[at] = size
+        return 0
+
+    lax.fori_loop(0, branches, place, 0)
+    blocks = [lax.div(bound_ref[j], length) for j in range(bounds)]
+    at = branches
+    for k in range(SLOTS):
+        meta_ref[at + 3 * bounds + k] = -1
+    for j in range(bounds):
+        slot = jnp.int32(0)
+        for i in range(j):
+            slot = slot + (blocks[i] == blocks[j]).astype(I32)
+        meta_ref[at + j] = blocks[j]
+        meta_ref[at + bounds + j] = slot
+        meta_ref[at + 2 * bounds + j] = bound_ref[j] - me * length - 2
+
+        @pl.when((blocks[j] == me) & (slot < SLOTS))
+        def _():
+            meta_ref[at + 3 * bounds + slot] = bound_ref[j] - me * length
+
+    for k in range(BR_PER):
+        meta_ref[at + 3 * bounds + SLOTS + k] = start_ref[me * BR_PER + k]
+        meta_ref[at + 3 * bounds + SLOTS + BR_PER + k] = size_ref[me * BR_PER + k]
+        meta_ref[at + 3 * bounds + SLOTS + 2 * BR_PER + k] = meta_ref[me * BR_PER + k]
+    last_ref[...] = x_ref[length - HALO :, :]
+    tails_ref[...] = tail_tiles(meta_ref, at + 2 * bounds, bounds, 4, x_ref[...]).astype(BF)
+
+
+def spread_kernel(prefix_ref, branch_ref, out_ref):
+    width = prefix_ref.shape[1]
+    for i in range(out_ref.shape[0]):
+        out_ref[i, :, :width] = prefix_ref[...]
+        out_ref[i, :, width:] = branch_ref[...]
+
+
 def prefix_state_kernel(
-    meta_ref, wanted_ref, x_ref, halo_ref, bc_ref, bchalo_ref, taps_ref, xc_ref, cum_ref, step_ref,
-    sent_ref, b_ref, c_ref, ext_ref, all_ref, *, base,
+    meta_ref, bc_ref, bchalo_ref, taps_ref, xc_ref, cum_ref, step_ref,
+    sent_ref, b_ref, c_ref, ext_ref, tile_ref, *, base, tail_base,
 ):
-    length, channels = x_ref.shape
+    length, channels = xc_ref.shape
     width = bchalo_ref.shape[1]
     n_state = width // 2
     n_ctx = sent_ref.shape[0]
@@ -123,58 +191,48 @@
     values = xc_ref[...].astype(F32)
     lane = iota((heads, length), 1)
     size = channels // heads
-
-    def state(weight):
+    rows = channels // n_ctx
+
+    def send(first, weight):
         weighted = (values * expand(weight.T, size)).astype(BF)
-        return lax.dot_general(
+        state = lax.dot_general(
             weighted, b_rows, (((0,), (0,)), ((), ())), preferred_element_type=F32
         )
+        sent_ref[:, first : first + rows, :] = state.astype(BF).reshape(n_ctx, rows, n_state)
 
     ends = [cumulative[:, length - 1 :]]
-    local = state(jnp.exp(ends[0] - cumulative) * step)
-    rows = channels // n_ctx
-    for i, part in enumerate(parts_of(local, 2)):
-        first = MISC + i * rows
-        sent_ref[:, first : first + rows, :] = part.reshape(n_ctx, rows, n_state)
+    send(MISC, jnp.exp(ends[0] - cumulative) * step)
     for slot in range(SLOTS):
         position = meta_ref[base + slot]
-        first = MISC + (2 + slot) * rows
+        first = MISC + (1 + slot) * rows
         end = jnp.sum(jnp.where(lane == position, cumulative, 0.0), axis=1, keepdims=True)
         ends.append(end)
 
         @pl.when(position >= 0)
         def _():
-            weight = jnp.exp(jnp.where(lane <= position, end - cumulative, FAR)) * step
-            sent_ref[:, first : first + rows, :] = state(weight).astype(BF).reshape(n_ctx, rows, n_state)
+            send(first, jnp.exp(jnp.where(lane <= position, end - cumulative, FAR)) * step)
 
         @pl.when(position < 0)
         def _():
             sent_ref[:, first : first + rows, :] = jnp.zeros((n_ctx, rows, n_state), BF)
 
-    parts = [part for end in ends for part in parts_of(end, 3)]
-    blank = jnp.zeros((heads, n_state), BF)
-    groups = (channels + width) // n_state
-    for g in range(groups):
-        for k in range(2):
-            at = 2 * g + k
-            block = blank
-            if at < len(parts):
-                block = jnp.broadcast_to(parts[at].astype(F32), (heads, n_state)).astype(BF)
-            first = HALO + length + k * heads
-            all_ref[first : first + heads, g * n_state : (g + 1) * n_state] = block.astype(F32)
-    all_ref[:HALO, :channels] = halo_ref[...].astype(F32)
-    all_ref[:HALO, channels:] = bchalo_ref[...].astype(F32)
-    all_ref[HALO : HALO + length, :channels] = x_ref[...].astype(F32)
-    all_ref[HALO : HALO + length, channels:] = bc.astype(F32)
-    depth = all_ref.shape[0]
-    column = iota((n_ctx * 8, depth), 1)
-    picker = (column == wanted_ref[...]).astype(BF)
-    placed = jnp.dot(picker, all_ref[...].astype(BF), preferred_element_type=F32)
-    for g in range(0, groups, 2):
-        pair = [
-            placed[:, (g + k) * n_state : (g + k + 1) * n_state].reshape(n_ctx, 8, n_state) for k in range(2)
+    spot = iota((heads, n_state), 1)
+    logs = jnp.zeros((heads, n_state), F32)
+    for at, part in enumerate(part for end in ends for part in parts_of(end, 3)):
+        logs = jnp.where(spot == at, part.astype(F32), logs)
+    bounds = tile_ref.shape[0]
+    tile_ref[...] = tail_tiles(meta_ref, tail_base, bounds, 8, bc).reshape(bounds, 8, width)
+    row = iota((8, n_state), 0)
+    per_head = n_ctx // heads
+    for o in range(n_ctx):
+        pair = [tile_ref[meta_ref[o * BR_PER + k]] for k in range(BR_PER)]
+        tails = [
+            jnp.where(row < 4, pair[0][:, g * n_state : (g + 1) * n_state], pair[1][:, g * n_state : (g + 1) * n_state])
+            for g in range(2)
         ]
-        sent_ref[:, g * 8 : g * 8 + 16, :] = jnp.concatenate(pair, axis=1).astype(BF)
+        h = o // per_head
+        tails[0] = jnp.where(row == LOGS, logs[h : h + 1], tails[0])
+        sent_ref[o, :MISC, :] = jnp.concatenate(tails, axis=0).astype(BF)
 
 
 def prefix_mix_kernel(xc_ref, b_ref, c_ref, cum_ref, step_ref, skip_ref, y_ref):
@@ -189,32 +247,29 @@
 
 
 def scan_kernel(meta_ref, got_ref, *rest, n_branch, bounds):
-    extra_ref = rest[0] if len(rest) == 4 else None
-    back_ref, entering_ref, bound_ref = rest[-3:]
+    extra_ref = rest[0] if len(rest) == 5 else None
+    back_ref, entering_ref, bound_ref, log_ref = rest[-4:]
     n_ctx, _, n_state = got_ref.shape
     rows = entering_ref.shape[1]
-
-    def log_of(misc, value):
-        found = [misc[r : r + 1] for r in (log_row(value, k) for k in range(3))]
-        return found[0] + found[1] + found[2]
-
+    parts = got_ref[:, :MISC, :].astype(F32)[:, LOGS, :]
+    for v in range(1 + SLOTS):
+        log = parts[:, 3 * v : 3 * v + 1] + parts[:, 3 * v + 1 : 3 * v + 2] + parts[:, 3 * v + 2 : 3 * v + 3]
+        log_ref[v] = jnp.broadcast_to(log, (n_ctx, n_state))
     state = jnp.zeros((rows, n_state), F32)
     for i in range(n_ctx):
         entering_ref[i] = state
         back_ref[i, :rows, :] = state.astype(BF)
         if i < n_ctx - 1:
-            misc = got_ref[i, :16, :].astype(F32)
             local = got_ref[i, MISC : MISC + rows, :].astype(F32)
-            local = local + got_ref[i, MISC + rows : MISC + 2 * rows, :].astype(F32)
-            state = jnp.exp(log_of(misc, 0)) * state + local
+            state = jnp.exp(log_ref[0, i : i + 1]) * state + local
     for j in range(bounds):
         block = meta_ref[n_branch + j]
         slot = meta_ref[n_branch + bounds + j]
-        misc = got_ref[block, :MISC, :].astype(F32)
-        log, part = log_of(misc, 1), got_ref[block, MISC + 2 * rows : MISC + 3 * rows, :].astype(F32)
+        log = log_ref[1, pl.ds(block, 1)]
+        part = got_ref[block, MISC + rows : MISC + 2 * rows, :].astype(F32)
         for other in range(1, SLOTS):
-            first = MISC + (2 + other) * rows
-            log = jnp.where(slot == other, log_of(misc, 1 + other), log)
+            first = MISC + (1 + other) * rows
+            log = jnp.where(slot == other, log_ref[1 + other, pl.ds(block, 1)], log)
             part = jnp.where(slot == other, got_ref[block, first : first + rows, :].astype(F32), part)
         if extra_ref is not None:
             tail = extra_ref[block, (bounds - SLOTS) * rows :, :].astype(F32)
@@ -243,7 +298,7 @@
 
 
 def branch_kernel(
-    meta_ref, x_ref, bc_ref, got_ref, dt_ref, rate_ref, xtaps_ref, taps_ref, skip_ref,
+    meta_ref, x_ref, bc_ref, xtails_ref, got_ref, dt_ref, rate_ref, xtaps_ref, taps_ref, skip_ref,
     y_ref, c_ref, seed_ref, ext_ref, *, base,
 ):
     length, channels = x_ref.shape
@@ -255,8 +310,13 @@
     misc = got_ref[0].astype(F32)
     for i in range(1, n_ctx):
         misc = misc + got_ref[i].astype(F32)
-    groups = (channels + width) // n_state
-    tails = jnp.concatenate([misc[g * 8 : (g + 1) * 8] for g in range(groups)], axis=1)
+    row = iota((8, 1), 0)
+    parents = [meta_ref[base + 2 * BR_PER + k] for k in range(BR_PER)]
+    wanted = jnp.where(row < 4, parents[0], parents[1]) * 4 + row % 4
+    picker = (iota((8, xtails_ref.shape[0]), 1) == wanted).astype(BF)
+    tails = jnp.dot(picker, xtails_ref[...], preferred_element_type=F32)
+    tails = jnp.concatenate([tails, misc[:8], misc[8:]], axis=1)
+    tails = jnp.where(iota(tails.shape, 0) % 4 == LOGS, 0.0, tails)
     tails = jnp.concatenate([tails, jnp.zeros_like(tails)], axis=0).astype(BF)
     taps = jnp.concatenate([xtaps_ref[...].astype(F32), taps_ref[...].astype(F32)], axis=1)
     count = taps.shape[0]
@@ -269,7 +329,7 @@
         rows = ext_ref[HALO - shift : HALO - shift + length]
         if shift:
             ahead = (offset < shift) & (segment < BR_PER)
-            picker = ahead & (place == segment * tail + tail - shift + offset)
+            picker = ahead & (place == segment * 4 + tail - shift + offset)
             early = jnp.dot(picker.astype(BF), tails, preferred_element_type=F32)
             rows = jnp.where(offset >= shift, rows, 0.0) + early
         term = taps[i : i + 1] * rows
@@ -356,7 +416,7 @@
         bout_ref[rows] = jnp.where(segment[rows] < BR_PER, scaled, 0.0).astype(BF)
 
 
-def call(kernel, outs, scratch, args, smem=0, blocks=None):
+def call(kernel, outs, scratch, args, smem=0, blocks=None, smem_out=False):
     blocks = blocks or {}
     specs = []
     for i in range(len(args)):
@@ -370,9 +430,14 @@
         kernel,
         grid=(1,),
         in_specs=specs,
-        out_specs=[pl.BlockSpec(s, lambda _, n=len(s): (0,) * n) for s, _ in outs],
+        out_specs=[
+            pl.BlockSpec(memory_space=pltpu.SMEM)
+            if smem_out and i == 0
+            else pl.BlockSpec(s, lambda _, n=len(s): (0,) * n)
+            for i, (s, _) in enumerate(outs)
+        ],
         out_shape=[jax.ShapeDtypeStruct(s, t) for s, t in outs],
-        scratch_shapes=[pltpu.VMEM(s, t) for s, t in scratch],
+        scratch_shapes=[(pltpu.SMEM if len(s) == 1 else pltpu.VMEM)(s, t) for s, t in scratch],
         compiler_params=pltpu.CompilerParams(vmem_limit_bytes=48 * 2**20),
         cost_estimate=pl.CostEstimate(flops=2 * 10**9, bytes_accessed=4 * 10**6, transcendentals=10**6),
     )(*args)
@@ -423,45 +488,39 @@
     tail = conv_x.shape[0] - 1
     onward = [(i, i + 1) for i in range(n_ctx - 1)]
 
-    own = jnp.concatenate([prefix_bc, branch_bc], axis=1)
-    gathered = lax.all_to_all(
-        jnp.broadcast_to(own[None], (n_tp, *own.shape)), "tp", 0, 0, tiled=True
-    ).reshape(length, 2 * width)
-    halo = lax.ppermute(prefix_x[length - HALO :], "ctx", onward)
-    bc_halo = lax.ppermute(gathered[length - HALO :, :width], "ctx", onward)
+    [spread] = call(spread_kernel, [((n_tp, length // n_tp, 2 * width), BF)], [], [prefix_bc, branch_bc])
+    gathered = lax.all_to_all(spread, "tp", 0, 0, tiled=True).reshape(length, 2 * width)
     rates = decay_rate[:, None]
     skips = jnp.repeat(skip, channels // heads)[None]
     gain = norm_gain[None]
-
+    order = jnp.arange(bounds, dtype=I32)
     block_of = bound_pos // length
-    at = bound_pos - block_of * length
-    order = jnp.arange(bounds, dtype=I32)
     slot_of = jnp.sum(
         ((block_of[:, None] == block_of[None, :]) & (order[None, :] < order[:, None])).astype(I32), axis=1
     )
-    border = jnp.arange(branches, dtype=I32)
-    earlier = (branch_owner[:, None] == branch_owner[None, :]) & (border[None, :] < border[:, None])
-    key = branch_owner * BR_PER + jnp.sum(earlier.astype(I32), axis=1)
-    start = jnp.sum(jnp.where(earlier, branch_len[None, :], 0), axis=1)
-    place = jnp.arange(n_ctx * BR_PER, dtype=I32)
-    chosen = place[:, None] == key[None, :]
-    parent_of = jnp.sum(jnp.where(chosen, branch_parent[None, :], 0), axis=1)
-    mine = (me * BR_PER + jnp.arange(BR_PER, dtype=I32))[:, None] == key[None, :]
-    my_len = jnp.sum(jnp.where(mine, branch_len[None, :], 0), axis=1)
-    my_start = jnp.sum(jnp.where(mine, start[None, :], 0), axis=1)
-    slot_here = (block_of == me)[None, :] & (slot_of[None, :] == order[:, None])
-    positions = jnp.sum(jnp.where(slot_here, at[None, :] + 1, 0), axis=1) - 1
-    meta = jnp.concatenate([parent_of, block_of, slot_of, positions, my_start, my_len])
-    at_positions = branches + 2 * bounds
-    at_mine = at_positions + bounds
-    local_at = jnp.where(block_of == me, at + HALO - tail + 1, -HALO * length)
-    parent_at = jnp.sum(jnp.where(parent_of[:, None] == order[None, :], local_at[None, :], 0), axis=1)
-    k = jnp.arange(8, dtype=I32)
-    tail_at = jnp.where(k[None, :] < tail, parent_at[0::2, None], parent_at[1::2, None]) + (k % tail)[None, :]
-    head_of = jnp.arange(n_ctx, dtype=I32) // (n_ctx // heads)
-    log_at = HALO + length + (k[None, :] - 2 * tail) * heads + head_of[:, None]
-    wanted = jnp.where(k[None, :] < 2 * tail, tail_at, log_at).reshape(-1, 1)
-
+
+    at_tails = branches + 2 * bounds
+    at_positions = at_tails + bounds
+    at_mine = at_positions + SLOTS
+    meta, tails, last = call(
+        functools.partial(index_kernel, n_ctx=n_ctx),
+        [((at_mine + 3 * BR_PER,), I32), ((4 * bounds, channels), BF), ((HALO, channels), BF)],
+        [((2 * n_ctx,), I32), ((branches,), I32), ((branches,), I32)],
+        [jnp.full((1,), me, I32), bound_pos, branch_owner, branch_parent, branch_len, prefix_x],
+        smem=5,
+        smem_out=True,
+    )
+    halo = lax.ppermute(last, "ctx", onward)
+    distances = [1 << k for k in range((n_ctx - 1).bit_length())]
+
+    def joined(value, some):
+        for far in some:
+            value = value + lax.ppermute(value, "ctx", [(i, i ^ far) for i in range(n_ctx)])
+        return value
+
+    tails = joined(tails, distances[:EARLY])
+    gathered, tails, halo = lax.optimization_barrier((gathered, tails, halo))
+    bc_halo = lax.ppermute(gathered[length - HALO :, :width], "ctx", onward)
     xc, cumulative, step = call(
         prefix_x_kernel,
         [((length, channels), BF), ((heads, length), F32), ((heads, length), F32)],
@@ -469,13 +528,15 @@
         [prefix_x, halo, prefix_dt, rates, conv_x],
     )
     sent, b_rows, c_rows = call(
-        functools.partial(prefix_state_kernel, base=at_positions),
-        [((n_ctx, MISC + (2 + SLOTS) * rows, n_state), BF), ((length, n_state), BF), ((length, n_state), BF)],
-        [((HALO + length, width), F32), ((HALO + length + 2 * heads, channels + width), F32)],
-        [meta, wanted, prefix_x, halo, gathered, bc_halo, conv_bc, xc, cumulative, step],
+        functools.partial(prefix_state_kernel, base=at_positions, tail_base=at_tails),
+        [((n_ctx, MISC + (1 + SLOTS) * rows, n_state), BF), ((length, n_state), BF), ((length, n_state), BF)],
+        [((HALO + length, width), F32), ((bounds, 8, width), F32)],
+        [meta, gathered, bc_halo, conv_bc, xc, cumulative, step],
         smem=1,
     )
     got = lax.all_to_all(sent, "ctx", 0, 0, tiled=True)
+    tails = joined(tails, distances[EARLY:])
+    got, tails = lax.optimization_barrier((got, tails))
     [y] = call(
         prefix_mix_kernel,
         [((length, channels), F32)],
@@ -485,13 +546,19 @@
 
     scan = functools.partial(scan_kernel, n_branch=branches, bounds=bounds)
     scan_out = [((n_ctx, (1 + BR_PER) * rows, n_state), BF)]
-    scan_scratch = [((n_ctx, rows, n_state), F32), ((bounds, rows, n_state), F32)]
+    scan_scratch = [
+        ((n_ctx, rows, n_state), F32),
+        ((bounds, rows, n_state), F32),
+        ((1 + SLOTS, n_ctx, n_state), F32),
+    ]
 
     def usual():
         return call(scan, scan_out, scan_scratch, [meta, got], smem=1)[0]
 
     def crowded():
-        extra = more_states(xc, b_rows, step, cumulative, positions[SLOTS:], n_ctx)
+        here = (block_of == me)[None, :] & (slot_of[None, :] == order[SLOTS:, None])
+        positions = jnp.sum(jnp.where(here, (bound_pos - block_of * length + 1)[None, :], 0), axis=1) - 1
+        extra = more_states(xc, b_rows, step, cumulative, positions, n_ctx)
         extra = lax.all_to_all(extra, "ctx", 0, 0, tiled=True)
         return call(scan, scan_out, scan_scratch, [meta, got, extra], smem=1)[0]
 
@@ -502,9 +569,9 @@
         functools.partial(branch_kernel, base=at_mine),
         [((length, channels), F32), ((length, n_state), BF), ((heads, length), F32)],
         [((HALO + length, channels + width), F32)],
-        [meta, branch_x, gathered, got, branch_dt, rates, conv_x, conv_bc, skips],
+        [meta, branch_x, gathered, tails, got, branch_dt, rates, conv_x, conv_bc, skips],
         smem=1,
-        blocks={3: (n_ctx, MISC, n_state)},
+        blocks={4: (n_ctx, MISC, n_state)},
     )
     gated, branch_gated, squares = call(
         functools.partial(gate_kernel, base=at_mine),

time: 110 us -> 118 us (1.073)
  starting transfers between devices: 37.2 us -> 57 us
  waiting for transfers between devices: 34.4 us -> 17.7 us
  blocking collectives: 14.9 us -> 22.1 us
  other arithmetic: 6.38 us -> 0.88 us
  Pallas kernels: 12.9 us -> 15.4 us
    ppermute x1 -> x6, starting transfers between devices: 4.02 us -> 25.7 us  [the longest x5 22.5 us: joined(): lax.ppermute(value, 'ctx', [(i, i ^ far) for i in range(n_ctx)])]
    all_to_all x1, waiting for transfers between devices: 20.9 us -> 0.01 us  [body(): got = lax.all_to_all(sent, 'ctx', 0, 0, tiled=True)]
    ppermute x1 -> x6, waiting for transfers between devices: 0.01 us -> 10.9 us  [the longest x5 10.2 us: joined(): lax.ppermute(value, 'ctx', [(i, i ^ far) for i in range(n_ctx)])]
    all_to_all x1, blocking collectives: 14.9 us -> 22.1 us  [body(): squares = lax.all_to_all(squares, 'tp', 0, 0, tiled=True)]
    all_to_all x1, waiting for transfers between devices: 6.13 us -> 0.01 us  [body(): lax.all_to_all(spread, 'tp', 0, 0, tiled=True).reshape(length, 2 * width)]
    reduce_sum x5 -> x0, other arithmetic: 2.75 us -> none  [the longest x1 0.91 us: body(): start = jnp.sum(jnp.where(earlier, branch_len[None, :], 0), axis=1)]
    all_to_all x1, starting transfers between devices: 8.19 us -> 5.71 us  [body(): back = lax.all_to_all(back, 'ctx', 0, 0, tiled=True)]
    pallas_call x7 -> x9, Pallas kernels: 12.9 us -> 15.4 us  [call(): pl.pallas_call(kernel, grid=(1,), in_specs=specs, out_specs=[pl.BlockSpec...]
  transfers between devices with their start and end apart: 5 -> 10, of which waited for: 3 -> 5; matrix products, arithmetic and copies ran while one was open for 7% -> 1% of each run, Pallas kernels for 4% -> 5%
where the time goes in v3:
time: 118 us; the launch traced here: 117 us
  starting transfers between devices  57 us (48%)
  blocking collectives  22.1 us (19%)
  waiting for transfers between devices  17.7 us (15%)
  Pallas kernels  15.4 us (13%)
  local copies, waits for them, and re-layouts  1.92 us (2%)
  between operations  1.57 us (1%)
    ppermute x5, starting transfers between devices, joined(): lax.ppermute(value, 'ctx', [(i, i ^ far) for i in range(n_ctx)])  22.5 us
    all_to_all x1, blocking collectives, body(): squares = lax.all_to_all(squares, 'tp', 0, 0, tiled=True)  22.1 us
    pallas_call x9, Pallas kernels, call(): pl.pallas_call(kernel, grid=(1,), in_specs=specs, out_specs=[pl.BlockSpec...  15.4 us
    all_to_all x1, starting transfers between devices, body(): lax.all_to_all(spread, 'tp', 0, 0, tiled=True).reshape(length, 2 * width)  11.8 us
    ppermute x5, waiting for transfers between devices, joined(): lax.ppermute(value, 'ctx', [(i, i ^ far) for i in range(n_ctx)])  10.2 us
    all_to_all x1, starting transfers between devices, body(): got = lax.all_to_all(sent, 'ctx', 0, 0, tiled=True)  9.93 us
    all_to_all x1, waiting for transfers between devices, body(): back = lax.all_to_all(back, 'ctx', 0, 0, tiled=True)  6.73 us
    all_to_all x1, starting transfers between devices, body(): back = lax.all_to_all(back, 'ctx', 0, 0, tiled=True)  5.71 us
  transfers between devices with their start and end apart: 10, of which 5 were waited for; matrix products, arithmetic and copies ran while one was open for 1% of the time, Pallas kernels for 5%

profile of v3, /device:TPU:1, one launch (start us, length us, event | category | flops | bytes accessed | tf_op | source)
XLA Modules:
  0.0 116.6 jit_solution(12830349521481581760)
XLA Ops:
  0.6 0.0 copy-start
  0.6 0.0 copy-start.4
  0.7 0.7 copy-done.4
  1.4 0.7 copy-done.5
  2.1 0.7 shard_map.177
  2.8 11.8 %all-to-all-start.1 = ((bf16[16,16,512]{2,1,0:T(8,128)(2,1)}), bf16[16,16,512]{2,1,0:T(8,128)(2,1)S(1)}, u32[]{:S(2)}, u32[]{:S(2)}) async-start(bf16[16,16,512]{2,1,0:T(8,128)(2,1)} %shard_map.177), calls=%async_computation.1 | async-start | bytes 524288 | tf_op jit(solution)/shard_map/all_to_all | solution.py:492
  14.7 0.0 copy-start.14
  14.7 0.0 copy-start.6
  14.7 0.0 copy-start.8
  14.7 2.1 %shard_map.176 = (s32[96]{0:T(128)S(1)}, bf16[32,512]{1,0:T(8,128)(2,1)S(1)}, bf16[16,512]{1,0:T(8,128)(2,1)S(1)}) custom-call(s32[1]{0:T(128)} %bitcast.11.me_ref, s32[8]{0:T(128)S(1)} %copy-done.16, s32[64]{0:T(128)S(1)} %copy-done.11, s32[64]{0:T(128)S(1)} %copy-done.12, s32[64]{0:T(128)S(1)} %copy-done.13, bf16[256,512]{1,0:T(8,128)(2,1)S(1)} %copy-done), custom_call_target="tpu_custom_call" | custom-call | flops 2000000000 | bytes 4000000 | tf_op jit(solution)/shard_map/pallas_call | solution.py:429
  16.8 3.2 %collective-permute-start = (bf16[32,512]{1,0:T(8,128)(2,1)S(1)}, bf16[32,512]{1,0:T(8,128)(2,1)S(1)}, u32[]{:S(2)}, u32[]{:S(2)}) collective-permute-start(bf16[32,512]{1,0:T(8,128)(2,1)S(1)} %get-tuple-element.65), channel_id=1, source_target_pairs={{0,16},{16,0},{32,48},{48,32},{64,80},{80,64},{96,112},{112,96},{1... | collective-permute-start | bytes 98312 | tf_op jit(solution)/shard_map/ppermute | solution.py:518
  20.1 1.7 %collective-permute-done = bf16[32,512]{1,0:T(8,128)(2,1)S(1)} collective-permute-done((bf16[32,512]{1,0:T(8,128)(2,1)S(1)}, bf16[32,512]{1,0:T(8,128)(2,1)S(1)}, u32[]{:S(2)}, u32[]{:S(2)}) %collective-permute-start) | collective-permute-done | bytes 32800 | tf_op jit(solution)/shard_map/ppermute | solution.py:518
  21.8 4.2 %collective-permute-start.1 = (bf16[32,512]{1,0:T(8,128)(2,1)S(1)}, bf16[32,512]{1,0:T(8,128)(2,1)S(1)}, u32[]{:S(2)}, u32[]{:S(2)}) collective-permute-start(bf16[32,512]{1,0:T(8,128)(2,1)S(1)} %add.30), channel_id=1, source_target_pairs={{0,32},{16,48},{32,0},{48,16},{64,96},{80,112},{96,64},{112,80},{1... | collective-permute-start | bytes 98312 | tf_op jit(solution)/shard_map/ppermute | solution.py:518
  26.0 3.2 %collective-permute-start.2 = (bf16[16,512]{1,0:T(8,128)(2,1)S(1)}, bf16[16,512]{1,0:T(8,128)(2,1)S(1)}, u32[]{:S(2)}, u32[]{:S(2)}) collective-permute-start(bf16[16,512]{1,0:T(8,128)(2,1)S(1)} %get-tuple-element.66), channel_id=1, source_target_pairs={{0,16},{16,32},{32,48},{48,64},{64,80},{80,96},{96,112},{112,128},... | collective-permute-start | bytes 49160 | tf_op jit(solution)/shard_map/ppermute | solution.py:513
  29.3 0.1 copy.32.rate_ref
  29.3 0.0 collective-permute-done.1
  29.4 0.7 collective-permute-done.2.halo_ref
  30.1 0.0 all-to-all-done.1
  30.1 3.8 %collective-permute-start.3 = (bf16[16,256]{1,0:T(8,128)(2,1)S(1)}, bf16[16,256]{1,0:T(8,128)(2,1)S(1)}, u32[]{:S(2)}, u32[]{:S(2)}) collective-permute-start(bf16[16,256]{1,0:T(8,128)(2,1)S(1)} %slice.6), channel_id=1, source_target_pairs={{0,16},{16,32},{32,48},{48,64},{64,80},{80,96},{96,112},{112,128},... | collective-permute-start | bytes 24584 | tf_op jit(solution)/shard_map/ppermute | solution.py:523
  33.9 0.0 copy-done.6
  33.9 0.0 copy-done.8
  33.9 0.8 shard_map.178
  34.7 0.0 collective-permute-done.3.bchalo_ref
  34.7 3.4 %shard_map.179 = (bf16[32,64,128]{2,1,0:T(8,128)(2,1)}, bf16[256,128]{1,0:T(8,128)(2,1)S(1)}, bf16[256,128]{1,0:T(8,128)(2,1)S(1)}) custom-call(s32[96]{0:T(128)S(1)} %get-tuple-element.64.meta_ref, bf16[256,512]{1,0:T(8,128)(2,1)S(1)} %bitcast.27, bf16[16,256]{1,0:T(8,128)(2,1)S(1)} %collective-permute-done.3.bchalo_ref, bf16[4,256]{1,0:T(4,128)(2,1)S(1)} %copy-done.9, ...), custom_call_target="tpu_custom_call" | custom-call | flops 2000000000 | bytes 4000000 | tf_op jit(solution)/shard_map/pallas_call | solution.py:429
  38.0 9.9 %all-to-all-start.2 = ((bf16[32,64,128]{2,1,0:T(8,128)(2,1)}), bf16[32,64,128]{2,1,0:T(8,128)(2,1)S(1)}, u32[]{:S(2)}, u32[]{:S(2)}) async-start(bf16[32,64,128]{2,1,0:T(8,128)(2,1)} %get-tuple-element.74), calls=%async_computation.2 | async-start | bytes 1048576 | tf_op jit(solution)/shard_map/all_to_all | solution.py:537
  48.0 7.0 %collective-permute-start.4 = (bf16[32,512]{1,0:T(8,128)(2,1)S(1)}, bf16[32,512]{1,0:T(8,128)(2,1)S(1)}, u32[]{:S(2)}, u32[]{:S(2)}) collective-permute-start(bf16[32,512]{1,0:T(8,128)(2,1)S(1)} %add.31), channel_id=1, source_target_pairs={{0,64},{16,80},{32,96},{48,112},{64,0},{80,16},{96,32},{112,48},{1... | collective-permute-start | bytes 98312 | tf_op jit(solution)/shard_map/ppermute | solution.py:518
  55.0 7.1 %collective-permute-done.4 = bf16[32,512]{1,0:T(8,128)(2,1)S(1)} collective-permute-done((bf16[32,512]{1,0:T(8,128)(2,1)S(1)}, bf16[32,512]{1,0:T(8,128)(2,1)S(1)}, u32[]{:S(2)}, u32[]{:S(2)}) %collective-permute-start.4) | collective-permute-done | bytes 32800 | tf_op jit(solution)/shard_map/ppermute | solution.py:518
  62.1 3.3 %collective-permute-start.5 = (bf16[32,512]{1,0:T(8,128)(2,1)S(1)}, bf16[32,512]{1,0:T(8,128)(2,1)S(1)}, u32[]{:S(2)}, u32[]{:S(2)}) collective-permute-start(bf16[32,512]{1,0:T(8,128)(2,1)S(1)} %add.32), channel_id=1, source_target_pairs={{0,128},{16,144},{32,160},{48,176},{64,192},{80,208},{96,224},{112... | collective-permute-start | bytes 98312 | tf_op jit(solution)/shard_map/ppermute | solution.py:518
  65.4 1.4 %collective-permute-done.5 = bf16[32,512]{1,0:T(8,128)(2,1)S(1)} collective-permute-done((bf16[32,512]{1,0:T(8,128)(2,1)S(1)}, bf16[32,512]{1,0:T(8,128)(2,1)S(1)}, u32[]{:S(2)}, u32[]{:S(2)}) %collective-permute-start.5) | collective-permute-done | bytes 32800 | tf_op jit(solution)/shard_map/ppermute | solution.py:518
  66.8 4.8 %collective-permute-start.6 = (bf16[32,512]{1,0:T(8,128)(2,1)S(1)}, bf16[32,512]{1,0:T(8,128)(2,1)S(1)}, u32[]{:S(2)}, u32[]{:S(2)}) collective-permute-start(bf16[32,512]{1,0:T(8,128)(2,1)S(1)} %add.33), channel_id=1, source_target_pairs={{0,256},{16,272},{32,288},{48,304},{64,320},{80,336},{96,352},{112... | collective-permute-start | bytes 98312 | tf_op jit(solution)/shard_map/ppermute | solution.py:518
  71.6 0.2 convert_reduce_fusion
  71.8 0.6 reduce_max.9
  73.1 0.0 collective-permute-done.6
  73.1 0.0 all-to-all-done.2.got_ref
  73.1 0.0 copy-start.15
  73.1 1.7 %conditional.1 = (bf16[32,48,128]{2,1,0:T(8,128)(2,1)}) conditional(s32[]{:T(128)} %convert_element_type.37, (s32[96]{0:T(128)S(1)}, bf16[32,64,128]{2,1,0:T(8,128)(2,1)S(1)}) %tuple.17, (s32[]{:T(128)}, s32[8]{0:T(128)S(1)}, s32[8]{0:T(128)S(1)}, s32[8]{0:T(128)S(1)}, s32[8]{0:T(128)S(1)}, /*index=5*/f32[8,256]{1,0:T(8,128)S(1)}, ...), branch_computations={%region_2.3_spmd, %region_3.6_spmd} | conditional | flops 2207159040 | bytes 12622084 | solution.py:565
  73.1 1.6 %branch_0_fun.1 = bf16[32,48,128]{2,1,0:T(8,128)(2,1)} custom-call(s32[96]{0:T(128)S(1)} %get-tuple-element.14.meta_ref, bf16[32,64,128]{2,1,0:T(8,128)(2,1)S(1)} %get-tuple-element.30.got_ref), custom_call_target="tpu_custom_call" | custom-call | flops 2000000000 | bytes 4000000 | tf_op jit(solution)/shard_map/cond/branch_0_fun/pallas_call | solution.py:429
  74.8 5.7 %all-to-all-start.3 = ((bf16[32,48,128]{2,1,0:T(8,128)(2,1)}), bf16[32,48,128]{2,1,0:T(8,128)(2,1)S(1)}, u32[]{:S(2)}, u32[]{:S(2)}) async-start(bf16[32,48,128]{2,1,0:T(8,128)(2,1)} %get-tuple-element.122), calls=%async_computation.3 | async-start | bytes 786432 | tf_op jit(solution)/shard_map/all_to_all | solution.py:566
  80.5 0.1 broadcast_in_dim.89
  80.6 0.1 broadcast_in_dim_reshape.3.skip_ref
  80.7 0.8 shard_map.180.y_ref
  81.4 0.2 copy-done.1
  81.6 2.4 %shard_map.181 = (f32[256,512]{1,0:T(8,128)S(1)}, bf16[256,128]{1,0:T(8,128)(2,1)S(1)}, f32[8,256]{1,0:T(8,128)S(1)}) custom-call(s32[96]{0:T(128)S(1)} %get-tuple-element.64.meta_ref, bf16[256,512]{1,0:T(8,128)(2,1)S(1)} %copy-done.1, bf16[256,512]{1,0:T(8,128)(2,1)S(1)} %bitcast.28, bf16[32,512]{1,0:T(8,128)(2,1)S(1)} %add.34.xtails_ref, ...), custom_call_target="tpu_custom_call" | custom-call | flops 2000000000 | bytes 4000000 | tf_op jit(solution)/shard_map/pallas_call | solution.py:429
  84.0 6.7 %all-to-all-done.3.back_ref = bf16[32,48,128]{2,1,0:T(8,128)(2,1)S(1)} async-done(((bf16[32,48,128]{2,1,0:T(8,128)(2,1)}), bf16[32,48,128]{2,1,0:T(8,128)(2,1)S(1)}, u32[]{:S(2)}, u32[]{:S(2)}) %all-to-all-start.3) | async-done | bytes 393248 | tf_op jit(solution)/shard_map/all_to_all | solution.py:566
  90.7 0.0 copy-done.2
  90.8 2.0 %shard_map.182 = (f32[256,512]{1,0:T(8,128)S(1)}, f32[256,512]{1,0:T(8,128)S(1)}, f32[16,8,128]{2,1,0:T(8,128)S(1)}) custom-call(s32[96]{0:T(128)S(1)} %get-tuple-element.64.meta_ref, f32[256,512]{1,0:T(8,128)S(1)} %shard_map.180.y_ref, bf16[256,128]{1,0:T(8,128)(2,1)S(1)} %get-tuple-element.73.c_ref, f32[8,256]{1,0:T(8,128)S(1)} %get-tuple-element.70.cum_ref, ...), custom_call_target="tpu_custom_call" | custom-call | flops 2000000000 | bytes 4000000 | tf_op jit(solution)/shard_map/pallas_call | solution.py:429
  92.8 22.1 %all_to_all.25.sq_ref = f32[16,8,128]{2,1,0:T(8,128)S(1)} all-to-all(f32[16,8,128]{2,1,0:T(8,128)S(1)} %get-tuple-element.81), channel_id=1, replica_groups=mesh['ctx'=32,'tp'=16] {'tp'}, dimensions={0} | all-to-all | bytes 131072 | tf_op jit(solution)/shard_map/all_to_all | solution.py:583
  114.9 1.6 %shard_map.183 = (bf16[256,512]{1,0:T(8,128)(2,1)}, bf16[256,512]{1,0:T(8,128)(2,1)}) custom-call(s32[96]{0:T(128)S(1)} %get-tuple-element.64.meta_ref, f32[16,8,128]{2,1,0:T(8,128)S(1)} %all_to_all.25.sq_ref, f32[256,512]{1,0:T(8,128)S(1)} %get-tuple-element.82.g_ref, f32[256,512]{1,0:T(8,128)S(1)} %get-tuple-element.83.bg_ref, f32[1,512]{1,0:T(1,128)S(1)} %bitcast.29), custom_call_target="tpu_custom_call" | custom-call | flops 2000000000 | bytes 4000000 | tf_op jit(solution)/shard_map/pallas_call | solution.py:429
  (30 shorter events, 0.1 us)
Async XLA Ops:
  0.6 14.0 %copy-start = (bf16[256,512]{1,0:T(8,128)(2,1)S(1)}, bf16[256,512]{1,0:T(8,128)(2,1)}, u32[]{:S(2)}) copy-start(bf16[256,512]{1,0:T(8,128)(2,1)} %x_ref.4) | copy-start | bytes 786436
  0.6 0.7 copy-start.4
  1.4 0.7 copy-start.5
  2.1 12.6 %copy-start.11 = (s32[64]{0:T(128)S(1)}, s32[64]{0:T(128)}, u32[]{:S(2)}) copy-start(s32[64]{0:T(128)} %owner_ref.1) | copy-start | bytes 772
  2.1 12.6 %copy-start.12 = (s32[64]{0:T(128)S(1)}, s32[64]{0:T(128)}, u32[]{:S(2)}) copy-start(s32[64]{0:T(128)} %parent_ref.1) | copy-start | bytes 772
  2.1 12.6 %copy-start.13 = (s32[64]{0:T(128)S(1)}, s32[64]{0:T(128)}, u32[]{:S(2)}) copy-start(s32[64]{0:T(128)} %len_ref.1) | copy-start | bytes 772
  2.1 12.6 %copy-start.16 = (s32[8]{0:T(128)S(1)}, s32[8]{0:T(128)}, u32[]{:S(2)}) copy-start(s32[8]{0:T(128)} %bound_ref.1) | copy-start | bytes 100
  2.8 27.3 %all-to-all-start.1 = ((bf16[16,16,512]{2,1,0:T(8,128)(2,1)}), bf16[16,16,512]{2,1,0:T(8,128)(2,1)S(1)}, u32[]{:S(2)}, u32[]{:S(2)}) async-start(bf16[16,16,512]{2,1,0:T(8,128)(2,1)} %shard_map.177), calls=%async_computation.1 | async-start | bytes 524288 | tf_op jit(solution)/shard_map/all_to_all | solution.py:492
  14.7 14.6 %copy-start.14 = (f32[8]{0:T(128)S(1)}, f32[8]{0:T(128)}, u32[]{:S(2)}) copy-start(f32[8]{0:T(128)} %param.29) | copy-start | bytes 100
  14.7 19.2 %copy-start.6 = (f32[8,256]{1,0:T(8,128)S(1)}, f32[8,256]{1,0:T(8,128)}, u32[]{:S(2)}) copy-start(f32[8,256]{1,0:T(8,128)} %dt_ref.2) | copy-start | bytes 24580
  14.7 19.2 %copy-start.8 = (bf16[4,512]{1,0:T(4,128)(2,1)S(1)}, bf16[4,512]{1,0:T(4,128)(2,1)}, u32[]{:S(2)}) copy-start(bf16[4,512]{1,0:T(4,128)(2,1)} %xtaps_ref.1) | copy-start | bytes 12292
  16.8 5.0 %collective-permute-start = (bf16[32,512]{1,0:T(8,128)(2,1)S(1)}, bf16[32,512]{1,0:T(8,128)(2,1)S(1)}, u32[]{:S(2)}, u32[]{:S(2)}) collective-permute-start(bf16[32,512]{1,0:T(8,128)(2,1)S(1)} %get-tuple-element.65), channel_id=1, source_target_pairs={{0,16},{16,0},{32,48},{48,32},{64,80},{80,64},{96,112},{112,96},{1... | collective-permute-start | bytes 98312 | tf_op jit(solution)/shard_map/ppermute | solution.py:518
  21.8 7.5 %collective-permute-start.1 = (bf16[32,512]{1,0:T(8,128)(2,1)S(1)}, bf16[32,512]{1,0:T(8,128)(2,1)S(1)}, u32[]{:S(2)}, u32[]{:S(2)}) collective-permute-start(bf16[32,512]{1,0:T(8,128)(2,1)S(1)} %add.30), channel_id=1, source_target_pairs={{0,32},{16,48},{32,0},{48,16},{64,96},{80,112},{96,64},{112,80},{1... | collective-permute-start | bytes 98312 | tf_op jit(solution)/shard_map/ppermute | solution.py:518
  26.0 4.1 %collective-permute-start.2 = (bf16[16,512]{1,0:T(8,128)(2,1)S(1)}, bf16[16,512]{1,0:T(8,128)(2,1)S(1)}, u32[]{:S(2)}, u32[]{:S(2)}) collective-permute-start(bf16[16,512]{1,0:T(8,128)(2,1)S(1)} %get-tuple-element.66), channel_id=1, source_target_pairs={{0,16},{16,32},{32,48},{48,64},{64,80},{80,96},{96,112},{112,128},... | collective-permute-start | bytes 49160 | tf_op jit(solution)/shard_map/ppermute | solution.py:513
  30.1 4.6 %copy-start.9 = (bf16[4,256]{1,0:T(4,128)(2,1)S(1)}, bf16[4,256]{1,0:T(4,128)(2,1)}, u32[]{:S(2)}) copy-start(bf16[4,256]{1,0:T(4,128)(2,1)} %taps_ref.5) | copy-start | bytes 6148
  30.1 4.5 %collective-permute-start.3 = (bf16[16,256]{1,0:T(8,128)(2,1)S(1)}, bf16[16,256]{1,0:T(8,128)(2,1)S(1)}, u32[]{:S(2)}, u32[]{:S(2)}) collective-permute-start(bf16[16,256]{1,0:T(8,128)(2,1)S(1)} %slice.6), channel_id=1, source_target_pairs={{0,16},{16,32},{32,48},{48,64},{64,80},{80,96},{96,112},{112,128},... | collective-permute-start | bytes 24584 | tf_op jit(solution)/shard_map/ppermute | solution.py:523
  38.0 35.1 %all-to-all-start.2 = ((bf16[32,64,128]{2,1,0:T(8,128)(2,1)}), bf16[32,64,128]{2,1,0:T(8,128)(2,1)S(1)}, u32[]{:S(2)}, u32[]{:S(2)}) async-start(bf16[32,64,128]{2,1,0:T(8,128)(2,1)} %get-tuple-element.74), calls=%async_computation.2 | async-start | bytes 1048576 | tf_op jit(solution)/shard_map/all_to_all | solution.py:537
  48.0 14.1 %collective-permute-start.4 = (bf16[32,512]{1,0:T(8,128)(2,1)S(1)}, bf16[32,512]{1,0:T(8,128)(2,1)S(1)}, u32[]{:S(2)}, u32[]{:S(2)}) collective-permute-start(bf16[32,512]{1,0:T(8,128)(2,1)S(1)} %add.31), channel_id=1, source_target_pairs={{0,64},{16,80},{32,96},{48,112},{64,0},{80,16},{96,32},{112,48},{1... | collective-permute-start | bytes 98312 | tf_op jit(solution)/shard_map/ppermute | solution.py:518
  62.1 4.7 %collective-permute-start.5 = (bf16[32,512]{1,0:T(8,128)(2,1)S(1)}, bf16[32,512]{1,0:T(8,128)(2,1)S(1)}, u32[]{:S(2)}, u32[]{:S(2)}) collective-permute-start(bf16[32,512]{1,0:T(8,128)(2,1)S(1)} %add.32), channel_id=1, source_target_pairs={{0,128},{16,144},{32,160},{48,176},{64,192},{80,208},{96,224},{112... | collective-permute-start | bytes 98312 | tf_op jit(solution)/shard_map/ppermute | solution.py:518
  66.8 6.3 %collective-permute-start.6 = (bf16[32,512]{1,0:T(8,128)(2,1)S(1)}, bf16[32,512]{1,0:T(8,128)(2,1)S(1)}, u32[]{:S(2)}, u32[]{:S(2)}) collective-permute-start(bf16[32,512]{1,0:T(8,128)(2,1)S(1)} %add.33), channel_id=1, source_target_pairs={{0,256},{16,272},{32,288},{48,304},{64,320},{80,336},{96,352},{112... | collective-permute-start | bytes 98312 | tf_op jit(solution)/shard_map/ppermute | solution.py:518
  73.1 7.4 %copy-start.15 = (f32[8]{0:T(128)S(1)}, f32[8]{0:T(128)}, u32[]{:S(2)}) copy-start(f32[8]{0:T(128)} %param.30) | copy-start | bytes 100
  74.8 16.0 %all-to-all-start.3 = ((bf16[32,48,128]{2,1,0:T(8,128)(2,1)}), bf16[32,48,128]{2,1,0:T(8,128)(2,1)S(1)}, u32[]{:S(2)}, u32[]{:S(2)}) async-start(bf16[32,48,128]{2,1,0:T(8,128)(2,1)} %get-tuple-element.122), calls=%async_computation.3 | async-start | bytes 786432 | tf_op jit(solution)/shard_map/all_to_all | solution.py:566
  80.7 1.0 copy-start.1
  80.7 1.0 copy-start.7
  81.6 9.1 %copy-start.2 = (bf16[256,512]{1,0:T(8,128)(2,1)S(1)}, bf16[256,512]{1,0:T(8,128)(2,1)}, u32[]{:S(2)}) copy-start(bf16[256,512]{1,0:T(8,128)(2,1)} %z_ref.1) | copy-start | bytes 786436
  81.6 9.1 %copy-start.3 = (bf16[256,512]{1,0:T(8,128)(2,1)S(1)}, bf16[256,512]{1,0:T(8,128)(2,1)}, u32[]{:S(2)}) copy-start(bf16[256,512]{1,0:T(8,128)(2,1)} %bz_ref.1) | copy-start | bytes 786436
  90.7 24.2 %copy-start.10 = (f32[512]{0:T(512)S(1)}, f32[512]{0:T(512)}, u32[]{:S(2)}) copy-start(f32[512]{0:T(512)} %param.31) | copy-start | bytes 6148

commit v4 on v3

--- a/solution.py
+++ b/solution.py
@@ -10,10 +10,8 @@
 BR_PER = 2
 EPSILON = 1e-05
 SLOTS = 2
-MISC = 16
 LOGS = 3
 HALO = 16
-EARLY = 2
 BF = jnp.bfloat16
 F32 = jnp.float32
 I32 = jnp.int32
@@ -56,7 +54,7 @@
     return value * jax.nn.sigmoid(value)
 
 
-def mixed_rows(values, scores, step, cumulative, mask, out_ref, extra):
+def mixed_rows(values, scores, step, cumulative, mask, out_ref, extra, gate):
     length, channels = values.shape
     heads = step.shape[0]
     size = channels // heads
@@ -74,11 +72,15 @@
                 gap = columns[rows, one : one + 1] - cumulative[one : one + 1, :width]
                 mixing = score * jnp.exp(jnp.where(kept, gap, FAR)) * step[one : one + 1, :width]
                 sums.append(jnp.dot(mixing.astype(BF), values[:width, lanes], preferred_element_type=F32))
-            out_ref[rows, lanes] = jnp.where(low, sums[0], sums[1]) + extra[rows, lanes]
-
-
-def prefix_x_kernel(x_ref, halo_ref, dt_ref, rate_ref, taps_ref, xc_ref, cum_ref, step_ref, ext_ref):
-    length = x_ref.shape[0]
+            out_ref[rows, lanes] = (jnp.where(low, sums[0], sums[1]) + extra[rows, lanes]) * gate[rows, lanes]
+
+
+def prefix_x_kernel(
+    meta_ref, x_ref, halo_ref, dt_ref, rate_ref, taps_ref,
+    xc_ref, cum_ref, step_ref, weighted_ref, logs_ref, ext_ref, *, base,
+):
+    length, channels = x_ref.shape
+    heads = rate_ref.shape[0]
     ext_ref[:HALO] = halo_ref[...].astype(F32)
     ext_ref[HALO:] = x_ref[...].astype(F32)
     taps = taps_ref[...].astype(F32)
@@ -87,25 +89,49 @@
     for i in range(1, count):
         first = HALO - count + 1 + i
         total = total + taps[i : i + 1] * ext_ref[first : first + length]
-    xc_ref[...] = silu(total).astype(BF)
+    values = silu(total).astype(BF)
+    xc_ref[...] = values
     step, _, cumulative = step_and_logs(dt_ref[...], rate_ref[...])
     cum_ref[...] = cumulative
     step_ref[...] = step
-
-
-def tail_tiles(meta_ref, base, bounds, height, rows):
+    lane = iota((heads, length), 1)
+
+    def weigh(at, weight):
+        weighted_ref[at] = (xc_ref[...].astype(F32) * expand(weight.T, channels // heads)).astype(BF)
+
+    ends = [cumulative[:, length - 1 :]]
+    weigh(0, jnp.exp(ends[0] - cumulative) * step)
+    for slot in range(SLOTS):
+        position = meta_ref[base + slot]
+        end = jnp.sum(jnp.where(lane == position, cumulative, 0.0), axis=1, keepdims=True)
+        ends.append(end)
+
+        @pl.when(position >= 0)
+        def _():
+            weigh(1 + slot, jnp.exp(jnp.where(lane <= position, end - cumulative, FAR)) * step)
+
+    spot = iota(logs_ref.shape, 1)
+    logs = jnp.zeros(logs_ref.shape, F32)
+    for at, part in enumerate(part for end in ends for part in parts_of(end, 3)):
+        logs = jnp.where(spot == at, part.astype(F32), logs)
+    logs_ref[...] = logs
+
+
+def tail_tiles(meta_ref, base, rows, out_ref):
+    bounds, height, width = out_ref.shape
     row = iota((bounds * height, 1), 0)
     wanted = jnp.full(row.shape, -1, I32)
     for j in range(bounds):
         wanted = jnp.where(row // height == j, meta_ref[base + j] + row % 4, wanted)
     wanted = jnp.where(row % 4 < 3, wanted, -1)
     picker = (iota((bounds * height, rows.shape[0]), 1) == wanted).astype(BF)
-    return jnp.dot(picker, rows, preferred_element_type=F32)
+    picked = jnp.dot(picker, rows, preferred_element_type=F32)
+    out_ref[...] = picked.reshape(bounds, height, width)
 
 
 def index_kernel(
     me_ref, bound_ref, owner_ref, parent_ref, len_ref, x_ref,
-    meta_ref, tails_ref, last_ref, count_ref, start_ref, size_ref, *, n_ctx,
+    meta_ref, tails_ref, last_ref, count_ref, start_ref, size_ref, tile_ref, *, n_ctx, n_state,
 ):
     me = me_ref[0]
     length = x_ref.shape[0]
@@ -152,9 +178,17 @@
     for k in range(BR_PER):
         meta_ref[at + 3 * bounds + SLOTS + k] = start_ref[me * BR_PER + k]
         meta_ref[at + 3 * bounds + SLOTS + BR_PER + k] = size_ref[me * BR_PER + k]
-        meta_ref[at + 3 * bounds + SLOTS + 2 * BR_PER + k] = meta_ref[me * BR_PER + k]
     last_ref[...] = x_ref[length - HALO :, :]
-    tails_ref[...] = tail_tiles(meta_ref, at + 2 * bounds, bounds, 4, x_ref[...]).astype(BF)
+    tail_tiles(meta_ref, at + 2 * bounds, x_ref[...], tile_ref)
+    upper = iota((8, n_state), 0) < 4
+    groups = x_ref.shape[1] // n_state
+    for o in range(n_ctx):
+        first, second = (meta_ref[o * BR_PER + k] for k in range(BR_PER))
+        tiles = []
+        for g in range(groups):
+            lanes = slice(g * n_state, (g + 1) * n_state)
+            tiles.append(jnp.where(upper, tile_ref[first, :, lanes], tile_ref[second, :, lanes]))
+        tails_ref[o] = jnp.concatenate(tiles, axis=0).astype(BF)
 
 
 def spread_kernel(prefix_ref, branch_ref, out_ref):
@@ -165,14 +199,14 @@
 
 
 def prefix_state_kernel(
-    meta_ref, bc_ref, bchalo_ref, taps_ref, xc_ref, cum_ref, step_ref,
+    meta_ref, bc_ref, bchalo_ref, taps_ref, weighted_ref, logs_ref, xtails_ref,
     sent_ref, b_ref, c_ref, ext_ref, tile_ref, *, base, tail_base,
 ):
-    length, channels = xc_ref.shape
+    _, length, channels = weighted_ref.shape
     width = bchalo_ref.shape[1]
     n_state = width // 2
-    n_ctx = sent_ref.shape[0]
-    heads = cum_ref.shape[0]
+    n_ctx, xrows, _ = xtails_ref.shape
+    heads = logs_ref.shape[0]
     bc = bc_ref[:, :width]
     ext_ref[:HALO] = bchalo_ref[...].astype(F32)
     ext_ref[HALO:] = bc.astype(F32)
@@ -186,72 +220,66 @@
     b_rows = convolved[:, :n_state]
     b_ref[...] = b_rows
     c_ref[...] = convolved[:, n_state:]
-    cumulative = cum_ref[...]
-    step = step_ref[...]
-    values = xc_ref[...].astype(F32)
-    lane = iota((heads, length), 1)
-    size = channels // heads
     rows = channels // n_ctx
-
-    def send(first, weight):
-        weighted = (values * expand(weight.T, size)).astype(BF)
+    misc = xrows + 16
+
+    def send(at):
         state = lax.dot_general(
-            weighted, b_rows, (((0,), (0,)), ((), ())), preferred_element_type=F32
+            weighted_ref[at], b_rows, (((0,), (0,)), ((), ())), preferred_element_type=F32
         )
+        first = misc + at * rows
         sent_ref[:, first : first + rows, :] = state.astype(BF).reshape(n_ctx, rows, n_state)
 
-    ends = [cumulative[:, length - 1 :]]
-    send(MISC, jnp.exp(ends[0] - cumulative) * step)
+    send(0)
     for slot in range(SLOTS):
         position = meta_ref[base + slot]
-        first = MISC + (1 + slot) * rows
-        end = jnp.sum(jnp.where(lane == position, cumulative, 0.0), axis=1, keepdims=True)
-        ends.append(end)
+        first = misc + (1 + slot) * rows
 
         @pl.when(position >= 0)
         def _():
-            send(first, jnp.exp(jnp.where(lane <= position, end - cumulative, FAR)) * step)
+            send(1 + slot)
 
         @pl.when(position < 0)
         def _():
             sent_ref[:, first : first + rows, :] = jnp.zeros((n_ctx, rows, n_state), BF)
 
-    spot = iota((heads, n_state), 1)
-    logs = jnp.zeros((heads, n_state), F32)
-    for at, part in enumerate(part for end in ends for part in parts_of(end, 3)):
-        logs = jnp.where(spot == at, part.astype(F32), logs)
+    sent_ref[:, :xrows, :] = xtails_ref[...]
     bounds = tile_ref.shape[0]
-    tile_ref[...] = tail_tiles(meta_ref, tail_base, bounds, 8, bc).reshape(bounds, 8, width)
+    tail_tiles(meta_ref, tail_base, bc, tile_ref)
     row = iota((8, n_state), 0)
     per_head = n_ctx // heads
     for o in range(n_ctx):
-        pair = [tile_ref[meta_ref[o * BR_PER + k]] for k in range(BR_PER)]
-        tails = [
-            jnp.where(row < 4, pair[0][:, g * n_state : (g + 1) * n_state], pair[1][:, g * n_state : (g + 1) * n_state])
-            for g in range(2)
-        ]
+        first, second = (meta_ref[o * BR_PER + k] for k in range(BR_PER))
+        tails = []
+        for g in range(2):
+            lanes = slice(g * n_state, (g + 1) * n_state)
+            tails.append(jnp.where(row < 4, tile_ref[first, :, lanes], tile_ref[second, :, lanes]))
         h = o // per_head
-        tails[0] = jnp.where(row == LOGS, logs[h : h + 1], tails[0])
-        sent_ref[o, :MISC, :] = jnp.concatenate(tails, axis=0).astype(BF)
-
-
-def prefix_mix_kernel(xc_ref, b_ref, c_ref, cum_ref, step_ref, skip_ref, y_ref):
-    length = xc_ref.shape[0]
+        tails[0] = jnp.where(row == LOGS, logs_ref[h : h + 1], tails[0])
+        sent_ref[o, xrows:misc, :] = jnp.concatenate(tails, axis=0).astype(BF)
+
+
+def prefix_mix_kernel(xc_ref, b_ref, c_ref, cum_ref, step_ref, skip_ref, z_ref, y_ref, scale_ref):
+    length, channels = xc_ref.shape
     scores = lax.dot_general(
         c_ref[...], b_ref[...], (((1,), (1,)), ((), ())), preferred_element_type=F32
     )
     mask = iota((length, length), 1) <= iota((length, length), 0)
     values = xc_ref[...]
+    cumulative = cum_ref[...]
+    gate = silu(z_ref[...].astype(F32))
+    scale_ref[...] = expand(jnp.exp(cumulative).T, channels // cumulative.shape[0]) * gate
     extra = values.astype(F32) * skip_ref[...]
-    mixed_rows(values, scores, step_ref[...], cum_ref[...], mask, y_ref, extra)
+    mixed_rows(values, scores, step_ref[...], cumulative, mask, y_ref, extra, gate)
 
 
 def scan_kernel(meta_ref, got_ref, *rest, n_branch, bounds):
     extra_ref = rest[0] if len(rest) == 5 else None
     back_ref, entering_ref, bound_ref, log_ref = rest[-4:]
-    n_ctx, _, n_state = got_ref.shape
+    n_ctx, sent_rows, n_state = got_ref.shape
     rows = entering_ref.shape[1]
-    parts = got_ref[:, :MISC, :].astype(F32)[:, LOGS, :]
+    misc = sent_rows - (1 + SLOTS) * rows
+    parts = got_ref[:, misc - 16 : misc, :].astype(F32)[:, LOGS, :]
     for v in range(1 + SLOTS):
         log = parts[:, 3 * v : 3 * v + 1] + parts[:, 3 * v + 1 : 3 * v + 2] + parts[:, 3 * v + 2 : 3 * v + 3]
         log_ref[v] = jnp.broadcast_to(log, (n_ctx, n_state))
@@ -260,15 +288,15 @@
         entering_ref[i] = state
         back_ref[i, :rows, :] = state.astype(BF)
         if i < n_ctx - 1:
-            local = got_ref[i, MISC : MISC + rows, :].astype(F32)
+            local = got_ref[i, misc : misc + rows, :].astype(F32)
             state = jnp.exp(log_ref[0, i : i + 1]) * state + local
     for j in range(bounds):
         block = meta_ref[n_branch + j]
         slot = meta_ref[n_branch + bounds + j]
         log = log_ref[1, pl.ds(block, 1)]
-        part = got_ref[block, MISC + rows : MISC + 2 * rows, :].astype(F32)
+        part = got_ref[block, misc + rows : misc + 2 * rows, :].astype(F32)
         for other in range(1, SLOTS):
-            first = MISC + (1 + other) * rows
+            first = misc + (1 + other) * rows
             log = jnp.where(slot == other, log_ref[1 + other, pl.ds(block, 1)], log)
             part = jnp.where(slot == other, got_ref[block, first : first + rows, :].astype(F32), part)
         if extra_ref is not None:
@@ -298,8 +326,8 @@
 
 
 def branch_kernel(
-    meta_ref, x_ref, bc_ref, xtails_ref, got_ref, dt_ref, rate_ref, xtaps_ref, taps_ref, skip_ref,
-    y_ref, c_ref, seed_ref, ext_ref, *, base,
+    meta_ref, x_ref, bc_ref, got_ref, dt_ref, rate_ref, xtaps_ref, taps_ref, skip_ref, z_ref,
+    y_ref, c_ref, scale_ref, ext_ref, *, base,
 ):
     length, channels = x_ref.shape
     n_ctx, _, n_state = got_ref.shape
@@ -307,16 +335,13 @@
     ext_ref[:HALO] = jnp.zeros((HALO, channels + width), F32)
     ext_ref[HALO:, :channels] = x_ref[...].astype(F32)
     ext_ref[HALO:, channels:] = bc_ref[:, width:].astype(F32)
-    misc = got_ref[0].astype(F32)
+    groups = (channels + width) // n_state
+    misc = got_ref[0, : 8 * groups, :].astype(F32)
     for i in range(1, n_ctx):
-        misc = misc + got_ref[i].astype(F32)
-    row = iota((8, 1), 0)
-    parents = [meta_ref[base + 2 * BR_PER + k] for k in range(BR_PER)]
-    wanted = jnp.where(row < 4, parents[0], parents[1]) * 4 + row % 4
-    picker = (iota((8, xtails_ref.shape[0]), 1) == wanted).astype(BF)
-    tails = jnp.dot(picker, xtails_ref[...], preferred_element_type=F32)
-    tails = jnp.concatenate([tails, misc[:8], misc[8:]], axis=1)
-    tails = jnp.where(iota(tails.shape, 0) % 4 == LOGS, 0.0, tails)
+        misc = misc + got_ref[i, : 8 * groups, :].astype(F32)
+    tails = jnp.concatenate([misc[8 * g : 8 * (g + 1)] for g in range(groups)], axis=1)
+    unused = iota(tails.shape, 0) % 4 == LOGS
+    tails = jnp.where(unused, 0.0, tails)
     tails = jnp.concatenate([tails, jnp.zeros_like(tails)], axis=0).astype(BF)
     taps = jnp.concatenate([xtaps_ref[...].astype(F32), taps_ref[...].astype(F32)], axis=1)
     count = taps.shape[0]
@@ -347,21 +372,20 @@
     for k in range(BR_PER):
         first = jnp.sum(jnp.where(lane == meta_ref[base + k], before, 0.0), axis=1, keepdims=True)
         seed = jnp.where(across == k, jnp.exp(jnp.where(across == k, cumulative - first, 0.0)), seed)
-    seed_ref[...] = seed
+    gate = silu(z_ref[...].astype(F32))
+    scale_ref[...] = expand(seed.T, channels // seed.shape[0]) * gate
     scores = lax.dot_general(c_rows, b_rows, (((1,), (1,)), ((), ())), preferred_element_type=F32)
     mask = (segment == across) & (segment < BR_PER)
     mask = mask & (iota((length, length), 1) <= iota((length, length), 0))
     extra = values.astype(F32) * skip_ref[...]
-    mixed_rows(values, scores, step, cumulative, mask, y_ref, extra)
+    mixed_rows(values, scores, step, cumulative, mask, y_ref, extra, gate)
 
 
 def gate_kernel(
-    meta_ref, y_ref, c_ref, cum_ref, z_ref, by_ref, bc_ref, seed_ref, bz_ref, back_ref,
+    meta_ref, y_ref, scale_ref, c_ref, by_ref, bscale_ref, bc_ref, back_ref,
     g_ref, bg_ref, sq_ref, *, base,
 ):
     length, channels = y_ref.shape
-    heads = cum_ref.shape[0]
-    size = channels // heads
     n_ctx, _, n_state = back_ref.shape
     rows = channels // n_ctx
 
@@ -375,8 +399,7 @@
             ones, gated * gated, (((1,), (1,)), ((), ())), precision=HIGH, preferred_element_type=F32
         )
 
-    y = y_ref[...] + expand(jnp.exp(cum_ref[...]).T, size) * from_state(c_ref[...], 0)
-    gated = y * silu(z_ref[...].astype(F32))
+    gated = y_ref[...] + scale_ref[...] * from_state(c_ref[...], 0)
     g_ref[...] = gated
     sums = squares(gated)
     segment, _ = segments(meta_ref, base, (length, 1), 0)
@@ -384,8 +407,7 @@
     seeded = from_state(c_rows, BR_PER)
     for k in range(BR_PER - 1):
         seeded = jnp.where(segment == k, from_state(c_rows, 1 + k), seeded)
-    y = by_ref[...] + expand(seed_ref[...].T, size) * seeded
-    gated = y * silu(bz_ref[...].astype(F32))
+    gated = by_ref[...] + bscale_ref[...] * seeded
     bg_ref[...] = gated
     more = squares(gated)
     half = length // 2
@@ -416,29 +438,17 @@
         bout_ref[rows] = jnp.where(segment[rows] < BR_PER, scaled, 0.0).astype(BF)
 
 
-def call(kernel, outs, scratch, args, smem=0, blocks=None, smem_out=False):
-    blocks = blocks or {}
-    specs = []
-    for i in range(len(args)):
-        if i < smem:
-            specs.append(pl.BlockSpec(memory_space=pltpu.SMEM))
-        elif i in blocks:
-            specs.append(pl.BlockSpec(blocks[i], lambda _, n=len(blocks[i]): (0,) * n))
-        else:
-            specs.append(pl.BlockSpec(args[i].shape, lambda _, n=args[i].ndim: (0,) * n))
+def call(kernel, outs, scratch, args, smem=0, smem_out=False):
+    def where(scalar):
+        return pl.BlockSpec(memory_space=pltpu.SMEM if scalar else pltpu.VMEM)
+
     return pl.pallas_call(
         kernel,
-        grid=(1,),
-        in_specs=specs,
-        out_specs=[
-            pl.BlockSpec(memory_space=pltpu.SMEM)
-            if smem_out and i == 0
-            else pl.BlockSpec(s, lambda _, n=len(s): (0,) * n)
-            for i, (s, _) in enumerate(outs)
-        ],
+        in_specs=[where(i < smem) for i in range(len(args))],
+        out_specs=[where(smem_out and i == 0) for i in range(len(outs))],
         out_shape=[jax.ShapeDtypeStruct(s, t) for s, t in outs],
         scratch_shapes=[(pltpu.SMEM if len(s) == 1 else pltpu.VMEM)(s, t) for s, t in scratch],
-        compiler_params=pltpu.CompilerParams(vmem_limit_bytes=48 * 2**20),
+        compiler_params=pltpu.CompilerParams(vmem_limit_bytes=24 * 2**20),
         cost_estimate=pl.CostEstimate(flops=2 * 10**9, bytes_accessed=4 * 10**6, transcendentals=10**6),
     )(*args)
 
@@ -502,47 +512,46 @@
     at_tails = branches + 2 * bounds
     at_positions = at_tails + bounds
     at_mine = at_positions + SLOTS
-    meta, tails, last = call(
-        functools.partial(index_kernel, n_ctx=n_ctx),
-        [((at_mine + 3 * BR_PER,), I32), ((4 * bounds, channels), BF), ((HALO, channels), BF)],
-        [((2 * n_ctx,), I32), ((branches,), I32), ((branches,), I32)],
+    xrows = 8 * channels // n_state
+    meta, xtails, last = call(
+        functools.partial(index_kernel, n_ctx=n_ctx, n_state=n_state),
+        [((at_mine + 2 * BR_PER,), I32), ((n_ctx, xrows, n_state), BF), ((HALO, channels), BF)],
+        [((2 * n_ctx,), I32), ((branches,), I32), ((branches,), I32), ((bounds, 8, channels), F32)],
         [jnp.full((1,), me, I32), bound_pos, branch_owner, branch_parent, branch_len, prefix_x],
         smem=5,
         smem_out=True,
     )
     halo = lax.ppermute(last, "ctx", onward)
-    distances = [1 << k for k in range((n_ctx - 1).bit_length())]
-
-    def joined(value, some):
-        for far in some:
-            value = value + lax.ppermute(value, "ctx", [(i, i ^ far) for i in range(n_ctx)])
-        return value
-
-    tails = joined(tails, distances[:EARLY])
-    gathered, tails, halo = lax.optimization_barrier((gathered, tails, halo))
+    xc, cumulative, step, weighted, logs = call(
+        functools.partial(prefix_x_kernel, base=at_positions),
+        [
+            ((length, channels), BF),
+            ((heads, length), F32),
+            ((heads, length), F32),
+            ((1 + SLOTS, length, channels), BF),
+            ((heads, n_state), F32),
+        ],
+        [((HALO + length, channels), F32)],
+        [meta, prefix_x, halo, prefix_dt, rates, conv_x],
+        smem=1,
+    )
+    gathered, weighted = lax.optimization_barrier((gathered, weighted))
     bc_halo = lax.ppermute(gathered[length - HALO :, :width], "ctx", onward)
-    xc, cumulative, step = call(
-        prefix_x_kernel,
-        [((length, channels), BF), ((heads, length), F32), ((heads, length), F32)],
-        [((HALO + length, channels), F32)],
-        [prefix_x, halo, prefix_dt, rates, conv_x],
-    )
     sent, b_rows, c_rows = call(
         functools.partial(prefix_state_kernel, base=at_positions, tail_base=at_tails),
-        [((n_ctx, MISC + (1 + SLOTS) * rows, n_state), BF), ((length, n_state), BF), ((length, n_state), BF)],
+        [((n_ctx, xrows + 16 + (1 + SLOTS) * rows, n_state), BF), ((length, n_state), BF), ((length, n_state), BF)],
         [((HALO + length, width), F32), ((bounds, 8, width), F32)],
-        [meta, gathered, bc_halo, conv_bc, xc, cumulative, step],
+        [meta, gathered, bc_halo, conv_bc, weighted, logs, xtails],
         smem=1,
     )
     got = lax.all_to_all(sent, "ctx", 0, 0, tiled=True)
-    tails = joined(tails, distances[EARLY:])
-    got, tails = lax.optimization_barrier((got, tails))
-    [y] = call(
+    y, scale = call(
         prefix_mix_kernel,
-        [((length, channels), F32)],
+        [((length, channels), F32), ((length, channels), F32)],
         [],
-        [xc, b_rows, c_rows, cumulative, step, skips],
-    )
+        [xc, b_rows, c_rows, cumulative, step, skips, prefix_z],
+    )
+    got, y, scale = lax.optimization_barrier((got, y, scale))
 
     scan = functools.partial(scan_kernel, n_branch=branches, bounds=bounds)
     scan_out = [((n_ctx, (1 + BR_PER) * rows, n_state), BF)]
@@ -565,19 +574,18 @@
     back = lax.cond(jnp.max(slot_of) >= SLOTS, crowded, usual)
     back = lax.all_to_all(back, "ctx", 0, 0, tiled=True)
 
-    branch_y, branch_c, seed = call(
+    branch_y, branch_c, branch_scale = call(
         functools.partial(branch_kernel, base=at_mine),
-        [((length, channels), F32), ((length, n_state), BF), ((heads, length), F32)],
+        [((length, channels), F32), ((length, n_state), BF), ((length, channels), F32)],
         [((HALO + length, channels + width), F32)],
-        [meta, branch_x, gathered, tails, got, branch_dt, rates, conv_x, conv_bc, skips],
+        [meta, branch_x, gathered, got, branch_dt, rates, conv_x, conv_bc, skips, branch_z],
         smem=1,
-        blocks={4: (n_ctx, MISC, n_state)},
     )
     gated, branch_gated, squares = call(
         functools.partial(gate_kernel, base=at_mine),
         [((length, channels), F32), ((length, channels), F32), ((n_tp, 8, length // 2), F32)],
         [],
-        [meta, y, c_rows, cumulative, prefix_z, branch_y, branch_c, seed, branch_z, back],
+        [meta, y, scale, c_rows, branch_y, branch_scale, branch_c, back],
         smem=1,
     )
     squares = lax.all_to_all(squares, "tp", 0, 0, tiled=True)

time: 118 us -> 105 us (0.89)
  starting transfers between devices: 57 us -> 38.7 us
  waiting for transfers between devices: 17.7 us -> 28.2 us
  blocking collectives: 22.1 us -> 15.6 us
  Pallas kernels: 15.4 us -> 17.7 us
    ppermute x5 -> x0, starting transfers between devices: 22.5 us -> none  [joined(): lax.ppermute(value, 'ctx', [(i, i ^ far) for i in range(n_ctx)])]
    all_to_all x1, waiting for transfers between devices: 0.01 us -> 16.1 us  [body(): got = lax.all_to_all(sent, 'ctx', 0, 0, tiled=True)]
    ppermute x5 -> x0, waiting for transfers between devices: 10.2 us -> none  [joined(): lax.ppermute(value, 'ctx', [(i, i ^ far) for i in range(n_ctx)])]
    all_to_all x1, blocking collectives: 22.1 us -> 15.6 us  [body(): squares = lax.all_to_all(squares, 'tp', 0, 0, tiled=True)]
    all_to_all x1, waiting for transfers between devices: 0.01 us -> 3.26 us  [body(): lax.all_to_all(spread, 'tp', 0, 0, tiled=True).reshape(length, 2 * width)]
    all_to_all x1, starting transfers between devices: 5.71 us -> 8.81 us  [body(): back = lax.all_to_all(back, 'ctx', 0, 0, tiled=True)]
    pallas_call x9, Pallas kernels: 15.4 us -> 17.7 us  [call(): pl.pallas_call(kernel, in_specs=[where(i < smem) for i in range(len(args)...]
    all_to_all x1, starting transfers between devices: 9.93 us -> 11.7 us  [body(): got = lax.all_to_all(sent, 'ctx', 0, 0, tiled=True)]
  transfers between devices with their start and end apart: 10 -> 5, of which waited for: 5 -> 5; matrix products, arithmetic and copies ran while one was open for 1% -> 1% of each run, Pallas kernels for 5% -> 8%
where the time goes in v4:
time: 105 us; the launch traced here: 104 us
  starting transfers between devices  38.7 us (37%)
  waiting for transfers between devices  28.2 us (27%)
  Pallas kernels  17.7 us (17%)
  blocking collectives  15.6 us (15%)
  local copies, waits for them, and re-layouts  1.73 us (2%)
  between operations  1.48 us (1%)
    pallas_call x9, Pallas kernels, call(): pl.pallas_call(kernel, in_specs=[where(i < smem) for i in range(len(args)...  17.7 us
    all_to_all x1, waiting for transfers between devices, body(): got = lax.all_to_all(sent, 'ctx', 0, 0, tiled=True)  16.1 us
    all_to_all x1, blocking collectives, body(): squares = lax.all_to_all(squares, 'tp', 0, 0, tiled=True)  15.6 us
    all_to_all x1, starting transfers between devices, body(): lax.all_to_all(spread, 'tp', 0, 0, tiled=True).reshape(length, 2 * width)  11.8 us
    all_to_all x1, starting transfers between devices, body(): got = lax.all_to_all(sent, 'ctx', 0, 0, tiled=True)  11.7 us
    all_to_all x1, starting transfers between devices, body(): back = lax.all_to_all(back, 'ctx', 0, 0, tiled=True)  8.81 us
    all_to_all x1, waiting for transfers between devices, body(): back = lax.all_to_all(back, 'ctx', 0, 0, tiled=True)  7.3 us
    all_to_all x1, waiting for transfers between devices, body(): lax.all_to_all(spread, 'tp', 0, 0, tiled=True).reshape(length, 2 * width)  3.26 us
  transfers between devices with their start and end apart: 5, of which 5 were waited for; matrix products, arithmetic and copies ran while one was open for 1% of the time, Pallas kernels for 8%

profile of v4, /device:TPU:1, one launch (start us, length us, event | category | flops | bytes accessed | tf_op | source)
XLA Modules:
  0.0 104.2 jit_solution(5067993593950785315)
XLA Ops:
  0.6 0.0 copy-start
  0.6 0.0 copy-start.4
  0.7 0.7 copy-done.4
  1.4 0.7 copy-done.5
  2.1 0.7 shard_map.177
  2.8 11.8 %all-to-all-start.1 = ((bf16[16,16,512]{2,1,0:T(8,128)(2,1)}), bf16[16,16,512]{2,1,0:T(8,128)(2,1)S(1)}, u32[]{:S(2)}, u32[]{:S(2)}) async-start(bf16[16,16,512]{2,1,0:T(8,128)(2,1)} %shard_map.177), calls=%async_computation.1 | async-start | bytes 524288 | tf_op jit(solution)/shard_map/all_to_all | solution.py:502
  14.6 0.0 copy-done
  14.7 0.0 copy-done.11
  14.7 0.0 copy-done.12
  14.7 0.0 copy-done.13
  14.7 0.0 copy-done.16
  14.7 0.0 copy-start.14
  14.7 0.0 copy-start.6
  14.7 0.0 copy-start.8
  14.7 2.1 %shard_map.176 = (s32[94]{0:T(128)S(1)}, bf16[32,32,128]{2,1,0:T(8,128)(2,1)S(1)}, bf16[16,512]{1,0:T(8,128)(2,1)S(1)}) custom-call(s32[1]{0:T(128)} %bitcast.11.me_ref, s32[8]{0:T(128)S(1)} %copy-done.16, s32[64]{0:T(128)S(1)} %copy-done.11, s32[64]{0:T(128)S(1)} %copy-done.12, s32[64]{0:T(128)S(1)} %copy-done.13, bf16[256,512]{1,0:T(8,128)(2,1)S(1)} %copy-done), custom_call_target="tpu_custom_call" | custom-call | flops 2000000000 | bytes 4000000 | tf_op jit(solution)/shard_map/pallas_call | solution.py:445
  16.8 3.2 %collective-permute-start = (bf16[16,512]{1,0:T(8,128)(2,1)S(1)}, bf16[16,512]{1,0:T(8,128)(2,1)S(1)}, u32[]{:S(2)}, u32[]{:S(2)}) collective-permute-start(bf16[16,512]{1,0:T(8,128)(2,1)S(1)} %get-tuple-element.69), channel_id=1, source_target_pairs={{0,16},{16,32},{32,48},{48,64},{64,80},{80,96},{96,112},{112,128},... | collective-permute-start | bytes 49160 | tf_op jit(solution)/shard_map/ppermute | solution.py:524
  20.1 0.0 copy-done.14
  20.1 0.1 copy.32.rate_ref
  20.1 0.8 collective-permute-done.halo_ref
  20.9 0.0 copy-done.6
  20.9 0.0 copy-done.8
  20.9 2.2 %shard_map.178 = (bf16[256,512]{1,0:T(8,128)(2,1)S(1)}, f32[8,256]{1,0:T(8,128)S(1)}, f32[8,256]{1,0:T(8,128)S(1)}, bf16[3,256,512]{2,1,0:T(8,128)(2,1)S(1)}, f32[8,128]{1,0:T(8,128)S(1)}) custom-call(s32[94]{0:T(128)S(1)} %get-tuple-element.68.meta_ref, bf16[256,512]{1,0:T(8,128)(2,1)S(1)} %copy-done, bf16[16,512]{1,0:T(8,128)(2,1)S(1)} %collective-permute-done.halo_ref, ...), custom_call_target="tpu_custom_call" | custom-call | flops 2000000000 | bytes 4000000 | tf_op jit(solution)/shard_map/pallas_call | solution.py:445
  23.1 3.3 %all-to-all-done.1 = bf16[16,16,512]{2,1,0:T(8,128)(2,1)S(1)} async-done(((bf16[16,16,512]{2,1,0:T(8,128)(2,1)}), bf16[16,16,512]{2,1,0:T(8,128)(2,1)S(1)}, u32[]{:S(2)}, u32[]{:S(2)}) %all-to-all-start.1) | async-done | bytes 262176 | tf_op jit(solution)/shard_map/all_to_all | solution.py:502
  26.4 3.2 %collective-permute-start.1 = (bf16[16,256]{1,0:T(8,128)(2,1)S(1)}, bf16[16,256]{1,0:T(8,128)(2,1)S(1)}, u32[]{:S(2)}, u32[]{:S(2)}) collective-permute-start(bf16[16,256]{1,0:T(8,128)(2,1)S(1)} %slice.6), channel_id=1, source_target_pairs={{0,16},{16,32},{32,48},{48,64},{64,80},{80,96},{96,112},{112,128},... | collective-permute-start | bytes 24584 | tf_op jit(solution)/shard_map/ppermute | solution.py:539
  29.6 0.8 collective-permute-done.1.bchalo_ref
  30.3 0.0 copy-done.9
  30.3 2.4 %shard_map.179 = (bf16[32,96,128]{2,1,0:T(8,128)(2,1)}, bf16[256,128]{1,0:T(8,128)(2,1)S(1)}, bf16[256,128]{1,0:T(8,128)(2,1)S(1)}) custom-call(s32[94]{0:T(128)S(1)} %get-tuple-element.68.meta_ref, bf16[256,512]{1,0:T(8,128)(2,1)S(1)} %bitcast.27, bf16[16,256]{1,0:T(8,128)(2,1)S(1)} %collective-permute-done.1.bchalo_ref, bf16[4,256]{1,0:T(4,128)(2,1)S(1)} %copy-done.9, ...), custom_call_target="tpu_custom_call" | custom-call | flops 2000000000 | bytes 4000000 | tf_op jit(solution)/shard_map/pallas_call | solution.py:445
  32.8 11.7 %all-to-all-start.2 = ((bf16[32,96,128]{2,1,0:T(8,128)(2,1)}), bf16[32,96,128]{2,1,0:T(8,128)(2,1)}, u32[]{:S(2)}, u32[]{:S(2)}) async-start(bf16[32,96,128]{2,1,0:T(8,128)(2,1)} %get-tuple-element.75), calls=%async_computation.2 | async-start | bytes 1572864 | tf_op jit(solution)/shard_map/all_to_all | solution.py:547
  44.4 0.2 convert_reduce_fusion
  44.6 0.6 reduce_max.9
  45.9 0.0 copy-done.15
  45.9 0.1 broadcast_in_dim.89
  46.0 0.1 broadcast_in_dim_reshape.3.skip_ref
  46.1 0.0 copy-done.1
  46.1 1.1 %shard_map.180 = (f32[256,512]{1,0:T(8,128)S(1)}, f32[256,512]{1,0:T(8,128)S(1)}) custom-call(bf16[256,512]{1,0:T(8,128)(2,1)S(1)} %get-tuple-element.76.xc_ref, bf16[256,128]{1,0:T(8,128)(2,1)S(1)} %get-tuple-element.77.b_ref, bf16[256,128]{1,0:T(8,128)(2,1)S(1)} %get-tuple-element.78.c_ref, f32[8,256]{1,0:T(8,128)S(1)} %get-tuple-element.79.cum_ref, ...), custom_call_target="tpu_custom_call" | custom-call | flops 2000000000 | bytes 4000000 | tf_op jit(solution)/shard_map/pallas_call | solution.py:445
  47.2 16.1 %all-to-all-done.2.got_ref = bf16[32,96,128]{2,1,0:T(8,128)(2,1)} async-done(((bf16[32,96,128]{2,1,0:T(8,128)(2,1)}), bf16[32,96,128]{2,1,0:T(8,128)(2,1)}, u32[]{:S(2)}, u32[]{:S(2)}) %all-to-all-start.2) | async-done | bytes 786464 | tf_op jit(solution)/shard_map/all_to_all | solution.py:547
  63.3 2.3 %conditional.1 = (bf16[32,48,128]{2,1,0:T(8,128)(2,1)}) conditional(s32[]{:T(128)} %convert_element_type.37, (s32[94]{0:T(128)S(1)}, bf16[32,96,128]{2,1,0:T(8,128)(2,1)}) %tuple.17, (s32[]{:T(128)}, s32[8]{0:T(128)S(1)}, s32[8]{0:T(128)S(1)}, s32[8]{0:T(128)S(1)}, s32[8]{0:T(128)S(1)}, /*index=5*/f32[8,256]{1,0:T(8,128)S(1)}, ...), branch_computations={%region_2.3_spmd, %region_3.6_spmd} | conditional | flops 2207159040 | bytes 12622084 | solution.py:574
  63.3 2.3 %branch_0_fun.1 = bf16[32,48,128]{2,1,0:T(8,128)(2,1)} custom-call(s32[94]{0:T(128)S(1)} %get-tuple-element.14.meta_ref, bf16[32,96,128]{2,1,0:T(8,128)(2,1)} %get-tuple-element.30.got_ref), custom_call_target="tpu_custom_call" | custom-call | flops 2000000000 | bytes 4000000 | tf_op jit(solution)/shard_map/cond/branch_0_fun/pallas_call | solution.py:445
  65.6 8.8 %all-to-all-start.3 = ((bf16[32,48,128]{2,1,0:T(8,128)(2,1)}), bf16[32,48,128]{2,1,0:T(8,128)(2,1)S(1)}, u32[]{:S(2)}, u32[]{:S(2)}) async-start(bf16[32,48,128]{2,1,0:T(8,128)(2,1)} %get-tuple-element.130), calls=%async_computation.3 | async-start | bytes 786432 | tf_op jit(solution)/shard_map/all_to_all | solution.py:575
  74.5 0.0 copy-done.2
  74.5 0.0 copy-done.3
  74.5 0.0 copy-done.7
  74.5 3.5 %shard_map.181 = (f32[256,512]{1,0:T(8,128)S(1)}, bf16[256,128]{1,0:T(8,128)(2,1)S(1)}, f32[256,512]{1,0:T(8,128)S(1)}) custom-call(s32[94]{0:T(128)S(1)} %get-tuple-element.68.meta_ref, bf16[256,512]{1,0:T(8,128)(2,1)S(1)} %copy-done.2, bf16[256,512]{1,0:T(8,128)(2,1)S(1)} %bitcast.28, bf16[32,96,128]{2,1,0:T(8,128)(2,1)} %all-to-all-done.2.got_ref, ...), custom_call_target="tpu_custom_call" | custom-call | flops 2000000000 | bytes 4000000 | tf_op jit(solution)/shard_map/pallas_call | solution.py:445
  77.9 7.3 %all-to-all-done.3.back_ref = bf16[32,48,128]{2,1,0:T(8,128)(2,1)S(1)} async-done(((bf16[32,48,128]{2,1,0:T(8,128)(2,1)}), bf16[32,48,128]{2,1,0:T(8,128)(2,1)S(1)}, u32[]{:S(2)}, u32[]{:S(2)}) %all-to-all-start.3) | async-done | bytes 393248 | tf_op jit(solution)/shard_map/all_to_all | solution.py:575
  85.3 1.8 %shard_map.182 = (f32[256,512]{1,0:T(8,128)S(1)}, f32[256,512]{1,0:T(8,128)S(1)}, f32[16,8,128]{2,1,0:T(8,128)S(1)}) custom-call(s32[94]{0:T(128)S(1)} %get-tuple-element.68.meta_ref, f32[256,512]{1,0:T(8,128)S(1)} %get-tuple-element.83.y_ref, f32[256,512]{1,0:T(8,128)S(1)} %get-tuple-element.84.scale_ref, bf16[256,128]{1,0:T(8,128)(2,1)S(1)} %get-tuple-element.78.c_ref, ...), custom_call_target="tpu_custom_call" | custom-call | flops 2000000000 | bytes 4000000 | tf_op jit(solution)/shard_map/pallas_call | solution.py:445
  87.0 15.6 %all_to_all.25.sq_ref = f32[16,8,128]{2,1,0:T(8,128)S(1)} all-to-all(f32[16,8,128]{2,1,0:T(8,128)S(1)} %get-tuple-element.89), channel_id=1, replica_groups=mesh['ctx'=32,'tp'=16] {'tp'}, dimensions={0} | all-to-all | bytes 131072 | tf_op jit(solution)/shard_map/all_to_all | solution.py:591
  102.6 0.0 copy-done.10
  102.6 1.6 %shard_map.183 = (bf16[256,512]{1,0:T(8,128)(2,1)}, bf16[256,512]{1,0:T(8,128)(2,1)}) custom-call(s32[94]{0:T(128)S(1)} %get-tuple-element.68.meta_ref, f32[16,8,128]{2,1,0:T(8,128)S(1)} %all_to_all.25.sq_ref, f32[256,512]{1,0:T(8,128)S(1)} %get-tuple-element.90.g_ref, f32[256,512]{1,0:T(8,128)S(1)} %get-tuple-element.91.bg_ref, f32[1,512]{1,0:T(1,128)S(1)} %bitcast.29), custom_call_target="tpu_custom_call" | custom-call | flops 2000000000 | bytes 4000000 | tf_op jit(solution)/shard_map/pallas_call | solution.py:445
  (15 shorter events, 0.0 us)
Async XLA Ops:
  0.6 14.0 %copy-start = (bf16[256,512]{1,0:T(8,128)(2,1)S(1)}, bf16[256,512]{1,0:T(8,128)(2,1)}, u32[]{:S(2)}) copy-start(bf16[256,512]{1,0:T(8,128)(2,1)} %x_ref.4) | copy-start | bytes 786436
  0.6 0.7 copy-start.4
  1.4 0.7 copy-start.5
  2.1 12.6 %copy-start.11 = (s32[64]{0:T(128)S(1)}, s32[64]{0:T(128)}, u32[]{:S(2)}) copy-start(s32[64]{0:T(128)} %owner_ref.1) | copy-start | bytes 772
  2.1 12.6 %copy-start.12 = (s32[64]{0:T(128)S(1)}, s32[64]{0:T(128)}, u32[]{:S(2)}) copy-start(s32[64]{0:T(128)} %parent_ref.1) | copy-start | bytes 772
  2.1 12.6 %copy-start.13 = (s32[64]{0:T(128)S(1)}, s32[64]{0:T(128)}, u32[]{:S(2)}) copy-start(s32[64]{0:T(128)} %len_ref.1) | copy-start | bytes 772
  2.1 12.6 %copy-start.16 = (s32[8]{0:T(128)S(1)}, s32[8]{0:T(128)}, u32[]{:S(2)}) copy-start(s32[8]{0:T(128)} %bound_ref.1) | copy-start | bytes 100
  2.8 23.5 %all-to-all-start.1 = ((bf16[16,16,512]{2,1,0:T(8,128)(2,1)}), bf16[16,16,512]{2,1,0:T(8,128)(2,1)S(1)}, u32[]{:S(2)}, u32[]{:S(2)}) async-start(bf16[16,16,512]{2,1,0:T(8,128)(2,1)} %shard_map.177), calls=%async_computation.1 | async-start | bytes 524288 | tf_op jit(solution)/shard_map/all_to_all | solution.py:502
  14.7 5.4 %copy-start.14 = (f32[8]{0:T(128)S(1)}, f32[8]{0:T(128)}, u32[]{:S(2)}) copy-start(f32[8]{0:T(128)} %param.29) | copy-start | bytes 100
  14.7 6.2 %copy-start.6 = (f32[8,256]{1,0:T(8,128)S(1)}, f32[8,256]{1,0:T(8,128)}, u32[]{:S(2)}) copy-start(f32[8,256]{1,0:T(8,128)} %dt_ref.2) | copy-start | bytes 24580
  14.7 6.2 %copy-start.8 = (bf16[4,512]{1,0:T(4,128)(2,1)S(1)}, bf16[4,512]{1,0:T(4,128)(2,1)}, u32[]{:S(2)}) copy-start(bf16[4,512]{1,0:T(4,128)(2,1)} %xtaps_ref.1) | copy-start | bytes 12292
  16.8 4.1 %collective-permute-start = (bf16[16,512]{1,0:T(8,128)(2,1)S(1)}, bf16[16,512]{1,0:T(8,128)(2,1)S(1)}, u32[]{:S(2)}, u32[]{:S(2)}) collective-permute-start(bf16[16,512]{1,0:T(8,128)(2,1)S(1)} %get-tuple-element.69), channel_id=1, source_target_pairs={{0,16},{16,32},{32,48},{48,64},{64,80},{80,96},{96,112},{112,128},... | collective-permute-start | bytes 49160 | tf_op jit(solution)/shard_map/ppermute | solution.py:524
  20.9 9.4 %copy-start.9 = (bf16[4,256]{1,0:T(4,128)(2,1)S(1)}, bf16[4,256]{1,0:T(4,128)(2,1)}, u32[]{:S(2)}) copy-start(bf16[4,256]{1,0:T(4,128)(2,1)} %taps_ref.5) | copy-start | bytes 6148
  26.4 4.0 %collective-permute-start.1 = (bf16[16,256]{1,0:T(8,128)(2,1)S(1)}, bf16[16,256]{1,0:T(8,128)(2,1)S(1)}, u32[]{:S(2)}, u32[]{:S(2)}) collective-permute-start(bf16[16,256]{1,0:T(8,128)(2,1)S(1)} %slice.6), channel_id=1, source_target_pairs={{0,16},{16,32},{32,48},{48,64},{64,80},{80,96},{96,112},{112,128},... | collective-permute-start | bytes 24584 | tf_op jit(solution)/shard_map/ppermute | solution.py:539
  32.8 13.2 %copy-start.15 = (f32[8]{0:T(128)S(1)}, f32[8]{0:T(128)}, u32[]{:S(2)}) copy-start(f32[8]{0:T(128)} %param.30) | copy-start | bytes 100
  32.8 13.3 %copy-start.1 = (bf16[256,512]{1,0:T(8,128)(2,1)S(1)}, bf16[256,512]{1,0:T(8,128)(2,1)}, u32[]{:S(2)}) copy-start(bf16[256,512]{1,0:T(8,128)(2,1)} %z_ref.2) | copy-start | bytes 786436
  32.8 30.5 %all-to-all-start.2 = ((bf16[32,96,128]{2,1,0:T(8,128)(2,1)}), bf16[32,96,128]{2,1,0:T(8,128)(2,1)}, u32[]{:S(2)}, u32[]{:S(2)}) async-start(bf16[32,96,128]{2,1,0:T(8,128)(2,1)} %get-tuple-element.75), calls=%async_computation.2 | async-start | bytes 1572864 | tf_op jit(solution)/shard_map/all_to_all | solution.py:547
  63.3 11.2 %copy-start.2 = (bf16[256,512]{1,0:T(8,128)(2,1)S(1)}, bf16[256,512]{1,0:T(8,128)(2,1)}, u32[]{:S(2)}) copy-start(bf16[256,512]{1,0:T(8,128)(2,1)} %x_ref.5) | copy-start | bytes 786436
  63.3 11.2 %copy-start.3 = (bf16[256,512]{1,0:T(8,128)(2,1)S(1)}, bf16[256,512]{1,0:T(8,128)(2,1)}, u32[]{:S(2)}) copy-start(bf16[256,512]{1,0:T(8,128)(2,1)} %z_ref.3) | copy-start | bytes 786436
  63.3 11.2 %copy-start.7 = (f32[8,256]{1,0:T(8,128)S(1)}, f32[8,256]{1,0:T(8,128)}, u32[]{:S(2)}) copy-start(f32[8,256]{1,0:T(8,128)} %dt_ref.3) | copy-start | bytes 24580
  65.6 19.6 %all-to-all-start.3 = ((bf16[32,48,128]{2,1,0:T(8,128)(2,1)}), bf16[32,48,128]{2,1,0:T(8,128)(2,1)S(1)}, u32[]{:S(2)}, u32[]{:S(2)}) async-start(bf16[32,48,128]{2,1,0:T(8,128)(2,1)} %get-tuple-element.130), calls=%async_computation.3 | async-start | bytes 786432 | tf_op jit(solution)/shard_map/all_to_all | solution.py:575
  85.2 17.4 %copy-start.10 = (f32[512]{0:T(512)S(1)}, f32[512]{0:T(512)}, u32[]{:S(2)}) copy-start(f32[512]{0:T(512)} %param.31) | copy-start | bytes 6148

commit v5 on v4

--- a/solution.py
+++ b/solution.py
@@ -191,24 +191,30 @@
         tails_ref[o] = jnp.concatenate(tiles, axis=0).astype(BF)
 
 
-def spread_kernel(prefix_ref, branch_ref, out_ref):
-    width = prefix_ref.shape[1]
+def spread_kernel(prefix_ref, branch_ref, halo_ref, out_ref):
+    height, width = prefix_ref.shape
+    n_state = width // 2
+    halo = halo_ref[...].astype(F32)
+    tile = jnp.concatenate([halo[8:, n_state:], halo[8:, :n_state]], axis=0).astype(BF)
     for i in range(out_ref.shape[0]):
         out_ref[i, :, :width] = prefix_ref[...]
-        out_ref[i, :, width:] = branch_ref[...]
+        out_ref[i, :, width : 2 * width] = branch_ref[...]
+        out_ref[i, height - HALO :, 2 * width :] = tile
 
 
 def prefix_state_kernel(
-    meta_ref, bc_ref, bchalo_ref, taps_ref, weighted_ref, logs_ref, xtails_ref,
+    meta_ref, bc_ref, taps_ref, weighted_ref, logs_ref, xtails_ref,
     sent_ref, b_ref, c_ref, ext_ref, tile_ref, *, base, tail_base,
 ):
     _, length, channels = weighted_ref.shape
-    width = bchalo_ref.shape[1]
+    width = taps_ref.shape[1]
     n_state = width // 2
     n_ctx, xrows, _ = xtails_ref.shape
     heads = logs_ref.shape[0]
     bc = bc_ref[:, :width]
-    ext_ref[:HALO] = bchalo_ref[...].astype(F32)
+    halo = bc_ref[length - HALO :, 2 * width :].astype(F32)
+    ext_ref[HALO - 8 : HALO, :n_state] = halo[8:]
+    ext_ref[HALO - 8 : HALO, n_state:] = halo[:8]
     ext_ref[HALO:] = bc.astype(F32)
     taps = taps_ref[...].astype(F32)
     count = taps.shape[0]
@@ -334,7 +340,7 @@
     width = taps_ref.shape[1]
     ext_ref[:HALO] = jnp.zeros((HALO, channels + width), F32)
     ext_ref[HALO:, :channels] = x_ref[...].astype(F32)
-    ext_ref[HALO:, channels:] = bc_ref[:, width:].astype(F32)
+    ext_ref[HALO:, channels:] = bc_ref[:, width : 2 * width].astype(F32)
     groups = (channels + width) // n_state
     misc = got_ref[0, : 8 * groups, :].astype(F32)
     for i in range(1, n_ctx):
@@ -498,8 +504,12 @@
     tail = conv_x.shape[0] - 1
     onward = [(i, i + 1) for i in range(n_ctx - 1)]
 
-    [spread] = call(spread_kernel, [((n_tp, length // n_tp, 2 * width), BF)], [], [prefix_bc, branch_bc])
-    gathered = lax.all_to_all(spread, "tp", 0, 0, tiled=True).reshape(length, 2 * width)
+    height = prefix_bc.shape[0]
+    bc_halo = lax.ppermute(prefix_bc[height - HALO :], "ctx", onward)
+    [spread] = call(
+        spread_kernel, [((n_tp, height, 2 * width + n_state), BF)], [], [prefix_bc, branch_bc, bc_halo]
+    )
+    gathered = lax.all_to_all(spread, "tp", 0, 0, tiled=True).reshape(length, 2 * width + n_state)
     rates = decay_rate[:, None]
     skips = jnp.repeat(skip, channels // heads)[None]
     gain = norm_gain[None]
@@ -536,12 +546,11 @@
         smem=1,
     )
     gathered, weighted = lax.optimization_barrier((gathered, weighted))
-    bc_halo = lax.ppermute(gathered[length - HALO :, :width], "ctx", onward)
     sent, b_rows, c_rows = call(
         functools.partial(prefix_state_kernel, base=at_positions, tail_base=at_tails),
         [((n_ctx, xrows + 16 + (1 + SLOTS) * rows, n_state), BF), ((length, n_state), BF), ((length, n_state), BF)],
         [((HALO + length, width), F32), ((bounds, 8, width), F32)],
-        [meta, gathered, bc_halo, conv_bc, weighted, logs, xtails],
+        [meta, gathered, conv_bc, weighted, logs, xtails],
         smem=1,
     )
     got = lax.all_to_all(sent, "ctx", 0, 0, tiled=True)

time: 105 us -> 107 us (1.019)
  waiting for transfers between devices: 28.2 us -> 33.4 us
  blocking collectives: 15.6 us -> 13.7 us
  starting transfers between devices: 38.7 us -> 37.6 us
    all_to_all x1, waiting for transfers between devices: 16.1 us -> 19.5 us  [body(): got = lax.all_to_all(sent, 'ctx', 0, 0, tiled=True)]
    all_to_all x1, starting transfers between devices: 8.81 us -> 6.01 us  [body(): back = lax.all_to_all(back, 'ctx', 0, 0, tiled=True)]
    all_to_all x1, blocking collectives: 15.6 us -> 13.7 us  [body(): squares = lax.all_to_all(squares, 'tp', 0, 0, tiled=True)]
where the time goes in v5:
time: 107 us; the launch traced here: 106 us
  starting transfers between devices  37.6 us (35%)
  waiting for transfers between devices  33.4 us (31%)
  Pallas kernels  17.7 us (17%)
  blocking collectives  13.7 us (13%)
  local copies, waits for them, and re-layouts  1.69 us (2%)
  between operations  1.47 us (1%)
    all_to_all x1, waiting for transfers between devices, body(): got = lax.all_to_all(sent, 'ctx', 0, 0, tiled=True)  19.5 us
    pallas_call x9, Pallas kernels, call(): pl.pallas_call(kernel, in_specs=[where(i < smem) for i in range(len(args)...  17.7 us
    all_to_all x1, blocking collectives, body(): squares = lax.all_to_all(squares, 'tp', 0, 0, tiled=True)  13.7 us
    all_to_all x1, starting transfers between devices, body(): lax.all_to_all(spread, 'tp', 0, 0, tiled=True)  11.9 us
    all_to_all x1, starting transfers between devices, body(): got = lax.all_to_all(sent, 'ctx', 0, 0, tiled=True)  11.6 us
    all_to_all x1, waiting for transfers between devices, body(): back = lax.all_to_all(back, 'ctx', 0, 0, tiled=True)  8.26 us
    all_to_all x1, starting transfers between devices, body(): back = lax.all_to_all(back, 'ctx', 0, 0, tiled=True)  6.01 us
    ppermute x1, starting transfers between devices, body(): bc_halo = lax.ppermute(prefix_bc[height - HALO:], 'ctx', onward)  4.16 us
  transfers between devices with their start and end apart: 5, of which 5 were waited for; matrix products, arithmetic and copies ran while one was open for 1% of the time, Pallas kernels for 8%

profile of v5, /device:TPU:1, one launch (start us, length us, event | category | flops | bytes accessed | tf_op | source)
XLA Modules:
  0.0 106.4 jit_solution(16900129526045124526)
XLA Ops:
  0.6 0.0 copy-start
  0.6 4.2 %collective-permute-start = (bf16[16,256]{1,0:T(8,128)(2,1)}, bf16[16,256]{1,0:T(8,128)(2,1)S(1)}, u32[]{:S(2)}, u32[]{:S(2)}) collective-permute-start(bf16[16,256]{1,0:T(8,128)(2,1)} %prefix_ref.1), channel_id=1, source_target_pairs={{0,16},{16,32},{32,48},{48,64},{64,80},{80,96},{96,112},{112,128},... | collective-permute-start | bytes 24584 | tf_op jit(solution)/shard_map/ppermute | solution.py:508
  4.8 1.0 collective-permute-done.halo_ref
  5.8 0.0 copy-start.4
  5.8 0.7 copy-done.4
  6.5 0.7 copy-done.5
  7.2 0.8 shard_map.177
  8.0 11.9 %all-to-all-start.1 = ((bf16[16,16,640]{2,1,0:T(8,128)(2,1)}), bf16[16,16,640]{2,1,0:T(8,128)(2,1)S(1)}, u32[]{:S(2)}, u32[]{:S(2)}) async-start(bf16[16,16,640]{2,1,0:T(8,128)(2,1)} %shard_map.177), calls=%async_computation.1 | async-start | bytes 655360 | tf_op jit(solution)/shard_map/all_to_all | solution.py:512
  19.8 0.0 copy-done
  19.8 0.0 copy-done.11
  19.8 0.0 copy-done.12
  19.8 0.0 copy-done.13
  19.9 0.0 copy-done.16
  19.9 0.0 copy-start.14
  19.9 0.0 copy-start.6
  19.9 0.0 copy-start.8
  19.9 2.1 %shard_map.176 = (s32[94]{0:T(128)S(1)}, bf16[32,32,128]{2,1,0:T(8,128)(2,1)S(1)}, bf16[16,512]{1,0:T(8,128)(2,1)S(1)}) custom-call(s32[1]{0:T(128)} %bitcast.11.me_ref, s32[8]{0:T(128)S(1)} %copy-done.16, s32[64]{0:T(128)S(1)} %copy-done.11, s32[64]{0:T(128)S(1)} %copy-done.12, s32[64]{0:T(128)S(1)} %copy-done.13, bf16[256,512]{1,0:T(8,128)(2,1)S(1)} %copy-done), custom_call_target="tpu_custom_call" | custom-call | flops 2000000000 | bytes 4000000 | tf_op jit(solution)/shard_map/pallas_call | solution.py:451
  22.0 3.9 %collective-permute-start.1 = (bf16[16,512]{1,0:T(8,128)(2,1)S(1)}, bf16[16,512]{1,0:T(8,128)(2,1)S(1)}, u32[]{:S(2)}, u32[]{:S(2)}) collective-permute-start(bf16[16,512]{1,0:T(8,128)(2,1)S(1)} %get-tuple-element.69), channel_id=1, source_target_pairs={{0,16},{16,32},{32,48},{48,64},{64,80},{80,96},{96,112},{112,128},... | collective-permute-start | bytes 49160 | tf_op jit(solution)/shard_map/ppermute | solution.py:534
  25.9 0.0 copy-done.14
  25.9 0.1 copy.32.rate_ref
  26.0 0.8 collective-permute-done.1.halo_ref
  26.8 0.0 copy-done.6
  26.8 0.0 copy-done.8
  26.8 2.2 %shard_map.178 = (bf16[256,512]{1,0:T(8,128)(2,1)S(1)}, f32[8,256]{1,0:T(8,128)S(1)}, f32[8,256]{1,0:T(8,128)S(1)}, bf16[3,256,512]{2,1,0:T(8,128)(2,1)S(1)}, f32[8,128]{1,0:T(8,128)S(1)}) custom-call(s32[94]{0:T(128)S(1)} %get-tuple-element.68.meta_ref, bf16[256,512]{1,0:T(8,128)(2,1)S(1)} %copy-done, bf16[16,512]{1,0:T(8,128)(2,1)S(1)} %collective-permute-done.1.halo_ref, ...), custom_call_target="tpu_custom_call" | custom-call | flops 2000000000 | bytes 4000000 | tf_op jit(solution)/shard_map/pallas_call | solution.py:451
  29.0 3.9 %all-to-all-done.1 = bf16[16,16,640]{2,1,0:T(8,128)(2,1)S(1)} async-done(((bf16[16,16,640]{2,1,0:T(8,128)(2,1)}), bf16[16,16,640]{2,1,0:T(8,128)(2,1)S(1)}, u32[]{:S(2)}, u32[]{:S(2)}) %all-to-all-start.1) | async-done | bytes 327712 | tf_op jit(solution)/shard_map/all_to_all | solution.py:512
  32.9 0.0 copy-done.9
  32.9 2.4 %shard_map.179 = (bf16[32,96,128]{2,1,0:T(8,128)(2,1)}, bf16[256,128]{1,0:T(8,128)(2,1)S(1)}, bf16[256,128]{1,0:T(8,128)(2,1)S(1)}) custom-call(s32[94]{0:T(128)S(1)} %get-tuple-element.68.meta_ref, bf16[256,640]{1,0:T(8,128)(2,1)S(1)} %bitcast.26, bf16[4,256]{1,0:T(4,128)(2,1)S(1)} %copy-done.9, bf16[3,256,512]{2,1,0:T(8,128)(2,1)S(1)} %get-tuple-element.72.weighted_ref, ...), custom_call_target="tpu_custom_call" | custom-call | flops 2000000000 | bytes 4000000 | tf_op jit(solution)/shard_map/pallas_call | solution.py:451
  35.3 11.6 %all-to-all-start.2 = ((bf16[32,96,128]{2,1,0:T(8,128)(2,1)}), bf16[32,96,128]{2,1,0:T(8,128)(2,1)}, u32[]{:S(2)}, u32[]{:S(2)}) async-start(bf16[32,96,128]{2,1,0:T(8,128)(2,1)} %get-tuple-element.75), calls=%async_computation.2 | async-start | bytes 1572864 | tf_op jit(solution)/shard_map/all_to_all | solution.py:556
  46.9 0.2 convert_reduce_fusion
  47.1 0.6 reduce_max.9
  48.4 0.0 copy-done.15
  48.4 0.1 broadcast_in_dim.89
  48.5 0.1 broadcast_in_dim_reshape.3.skip_ref
  48.6 0.0 copy-done.1
  48.6 1.1 %shard_map.180 = (f32[256,512]{1,0:T(8,128)S(1)}, f32[256,512]{1,0:T(8,128)S(1)}) custom-call(bf16[256,512]{1,0:T(8,128)(2,1)S(1)} %get-tuple-element.76.xc_ref, bf16[256,128]{1,0:T(8,128)(2,1)S(1)} %get-tuple-element.77.b_ref, bf16[256,128]{1,0:T(8,128)(2,1)S(1)} %get-tuple-element.78.c_ref, f32[8,256]{1,0:T(8,128)S(1)} %get-tuple-element.79.cum_ref, ...), custom_call_target="tpu_custom_call" | custom-call | flops 2000000000 | bytes 4000000 | tf_op jit(solution)/shard_map/pallas_call | solution.py:451
  49.7 19.5 %all-to-all-done.2.got_ref = bf16[32,96,128]{2,1,0:T(8,128)(2,1)} async-done(((bf16[32,96,128]{2,1,0:T(8,128)(2,1)}), bf16[32,96,128]{2,1,0:T(8,128)(2,1)}, u32[]{:S(2)}, u32[]{:S(2)}) %all-to-all-start.2) | async-done | bytes 786464 | tf_op jit(solution)/shard_map/all_to_all | solution.py:556
  69.2 2.3 %conditional.1 = (bf16[32,48,128]{2,1,0:T(8,128)(2,1)}) conditional(s32[]{:T(128)} %convert_element_type.37, (s32[94]{0:T(128)S(1)}, bf16[32,96,128]{2,1,0:T(8,128)(2,1)}) %tuple.17, (s32[]{:T(128)}, s32[8]{0:T(128)S(1)}, s32[8]{0:T(128)S(1)}, s32[8]{0:T(128)S(1)}, s32[8]{0:T(128)S(1)}, /*index=5*/f32[8,256]{1,0:T(8,128)S(1)}, ...), branch_computations={%region_2.3_spmd, %region_3.6_spmd} | conditional | flops 2207159040 | bytes 12622084 | solution.py:583
  69.3 2.3 %branch_0_fun.1 = bf16[32,48,128]{2,1,0:T(8,128)(2,1)} custom-call(s32[94]{0:T(128)S(1)} %get-tuple-element.14.meta_ref, bf16[32,96,128]{2,1,0:T(8,128)(2,1)} %get-tuple-element.30.got_ref), custom_call_target="tpu_custom_call" | custom-call | flops 2000000000 | bytes 4000000 | tf_op jit(solution)/shard_map/cond/branch_0_fun/pallas_call | solution.py:451
  71.6 6.0 %all-to-all-start.3 = ((bf16[32,48,128]{2,1,0:T(8,128)(2,1)}), bf16[32,48,128]{2,1,0:T(8,128)(2,1)S(1)}, u32[]{:S(2)}, u32[]{:S(2)}) async-start(bf16[32,48,128]{2,1,0:T(8,128)(2,1)} %get-tuple-element.130), calls=%async_computation.3 | async-start | bytes 786432 | tf_op jit(solution)/shard_map/all_to_all | solution.py:584
  77.6 0.0 copy-done.2
  77.6 0.0 copy-done.3
  77.6 0.0 copy-done.7
  77.6 3.5 %shard_map.181 = (f32[256,512]{1,0:T(8,128)S(1)}, bf16[256,128]{1,0:T(8,128)(2,1)S(1)}, f32[256,512]{1,0:T(8,128)S(1)}) custom-call(s32[94]{0:T(128)S(1)} %get-tuple-element.68.meta_ref, bf16[256,512]{1,0:T(8,128)(2,1)S(1)} %copy-done.2, bf16[256,640]{1,0:T(8,128)(2,1)S(1)} %bitcast.27, bf16[32,96,128]{2,1,0:T(8,128)(2,1)} %all-to-all-done.2.got_ref, ...), custom_call_target="tpu_custom_call" | custom-call | flops 2000000000 | bytes 4000000 | tf_op jit(solution)/shard_map/pallas_call | solution.py:451
  81.1 8.3 %all-to-all-done.3.back_ref = bf16[32,48,128]{2,1,0:T(8,128)(2,1)S(1)} async-done(((bf16[32,48,128]{2,1,0:T(8,128)(2,1)}), bf16[32,48,128]{2,1,0:T(8,128)(2,1)S(1)}, u32[]{:S(2)}, u32[]{:S(2)}) %all-to-all-start.3) | async-done | bytes 393248 | tf_op jit(solution)/shard_map/all_to_all | solution.py:584
  89.3 1.8 %shard_map.182 = (f32[256,512]{1,0:T(8,128)S(1)}, f32[256,512]{1,0:T(8,128)S(1)}, f32[16,8,128]{2,1,0:T(8,128)S(1)}) custom-call(s32[94]{0:T(128)S(1)} %get-tuple-element.68.meta_ref, f32[256,512]{1,0:T(8,128)S(1)} %get-tuple-element.83.y_ref, f32[256,512]{1,0:T(8,128)S(1)} %get-tuple-element.84.scale_ref, bf16[256,128]{1,0:T(8,128)(2,1)S(1)} %get-tuple-element.78.c_ref, ...), custom_call_target="tpu_custom_call" | custom-call | flops 2000000000 | bytes 4000000 | tf_op jit(solution)/shard_map/pallas_call | solution.py:451
  91.1 13.7 %all_to_all.25.sq_ref = f32[16,8,128]{2,1,0:T(8,128)S(1)} all-to-all(f32[16,8,128]{2,1,0:T(8,128)S(1)} %get-tuple-element.89), channel_id=1, replica_groups=mesh['ctx'=32,'tp'=16] {'tp'}, dimensions={0} | all-to-all | bytes 131072 | tf_op jit(solution)/shard_map/all_to_all | solution.py:600
  104.8 0.0 copy-done.10
  104.8 1.6 %shard_map.183 = (bf16[256,512]{1,0:T(8,128)(2,1)}, bf16[256,512]{1,0:T(8,128)(2,1)}) custom-call(s32[94]{0:T(128)S(1)} %get-tuple-element.68.meta_ref, f32[16,8,128]{2,1,0:T(8,128)S(1)} %all_to_all.25.sq_ref, f32[256,512]{1,0:T(8,128)S(1)} %get-tuple-element.90.g_ref, f32[256,512]{1,0:T(8,128)S(1)} %get-tuple-element.91.bg_ref, f32[1,512]{1,0:T(1,128)S(1)} %bitcast.28), custom_call_target="tpu_custom_call" | custom-call | flops 2000000000 | bytes 4000000 | tf_op jit(solution)/shard_map/pallas_call | solution.py:451
  (14 shorter events, 0.0 us)
Async XLA Ops:
  0.6 19.2 %copy-start = (bf16[256,512]{1,0:T(8,128)(2,1)S(1)}, bf16[256,512]{1,0:T(8,128)(2,1)}, u32[]{:S(2)}) copy-start(bf16[256,512]{1,0:T(8,128)(2,1)} %x_ref.4) | copy-start | bytes 786436
  0.6 5.2 %collective-permute-start = (bf16[16,256]{1,0:T(8,128)(2,1)}, bf16[16,256]{1,0:T(8,128)(2,1)S(1)}, u32[]{:S(2)}, u32[]{:S(2)}) collective-permute-start(bf16[16,256]{1,0:T(8,128)(2,1)} %prefix_ref.1), channel_id=1, source_target_pairs={{0,16},{16,32},{32,48},{48,64},{64,80},{80,96},{96,112},{112,128},... | collective-permute-start | bytes 24584 | tf_op jit(solution)/shard_map/ppermute | solution.py:508
  5.8 0.7 copy-start.4
  6.5 0.7 copy-start.5
  7.2 12.6 %copy-start.11 = (s32[64]{0:T(128)S(1)}, s32[64]{0:T(128)}, u32[]{:S(2)}) copy-start(s32[64]{0:T(128)} %owner_ref.1) | copy-start | bytes 772
  7.2 12.6 %copy-start.12 = (s32[64]{0:T(128)S(1)}, s32[64]{0:T(128)}, u32[]{:S(2)}) copy-start(s32[64]{0:T(128)} %parent_ref.1) | copy-start | bytes 772
  7.2 12.7 %copy-start.13 = (s32[64]{0:T(128)S(1)}, s32[64]{0:T(128)}, u32[]{:S(2)}) copy-start(s32[64]{0:T(128)} %len_ref.1) | copy-start | bytes 772
  7.2 12.7 %copy-start.16 = (s32[8]{0:T(128)S(1)}, s32[8]{0:T(128)}, u32[]{:S(2)}) copy-start(s32[8]{0:T(128)} %bound_ref.1) | copy-start | bytes 100
  8.0 24.9 %all-to-all-start.1 = ((bf16[16,16,640]{2,1,0:T(8,128)(2,1)}), bf16[16,16,640]{2,1,0:T(8,128)(2,1)S(1)}, u32[]{:S(2)}, u32[]{:S(2)}) async-start(bf16[16,16,640]{2,1,0:T(8,128)(2,1)} %shard_map.177), calls=%async_computation.1 | async-start | bytes 655360 | tf_op jit(solution)/shard_map/all_to_all | solution.py:512
  19.9 6.1 %copy-start.14 = (f32[8]{0:T(128)S(1)}, f32[8]{0:T(128)}, u32[]{:S(2)}) copy-start(f32[8]{0:T(128)} %param.29) | copy-start | bytes 100
  19.9 6.9 %copy-start.6 = (f32[8,256]{1,0:T(8,128)S(1)}, f32[8,256]{1,0:T(8,128)}, u32[]{:S(2)}) copy-start(f32[8,256]{1,0:T(8,128)} %dt_ref.2) | copy-start | bytes 24580
  19.9 6.9 %copy-start.8 = (bf16[4,512]{1,0:T(4,128)(2,1)S(1)}, bf16[4,512]{1,0:T(4,128)(2,1)}, u32[]{:S(2)}) copy-start(bf16[4,512]{1,0:T(4,128)(2,1)} %xtaps_ref.1) | copy-start | bytes 12292
  22.0 4.8 %collective-permute-start.1 = (bf16[16,512]{1,0:T(8,128)(2,1)S(1)}, bf16[16,512]{1,0:T(8,128)(2,1)S(1)}, u32[]{:S(2)}, u32[]{:S(2)}) collective-permute-start(bf16[16,512]{1,0:T(8,128)(2,1)S(1)} %get-tuple-element.69), channel_id=1, source_target_pairs={{0,16},{16,32},{32,48},{48,64},{64,80},{80,96},{96,112},{112,128},... | collective-permute-start | bytes 49160 | tf_op jit(solution)/shard_map/ppermute | solution.py:534
  26.8 6.1 %copy-start.9 = (bf16[4,256]{1,0:T(4,128)(2,1)S(1)}, bf16[4,256]{1,0:T(4,128)(2,1)}, u32[]{:S(2)}) copy-start(bf16[4,256]{1,0:T(4,128)(2,1)} %taps_ref.5) | copy-start | bytes 6148
  35.3 13.1 %copy-start.15 = (f32[8]{0:T(128)S(1)}, f32[8]{0:T(128)}, u32[]{:S(2)}) copy-start(f32[8]{0:T(128)} %param.30) | copy-start | bytes 100
  35.3 13.3 %copy-start.1 = (bf16[256,512]{1,0:T(8,128)(2,1)S(1)}, bf16[256,512]{1,0:T(8,128)(2,1)}, u32[]{:S(2)}) copy-start(bf16[256,512]{1,0:T(8,128)(2,1)} %z_ref.2) | copy-start | bytes 786436
  35.3 33.9 %all-to-all-start.2 = ((bf16[32,96,128]{2,1,0:T(8,128)(2,1)}), bf16[32,96,128]{2,1,0:T(8,128)(2,1)}, u32[]{:S(2)}, u32[]{:S(2)}) async-start(bf16[32,96,128]{2,1,0:T(8,128)(2,1)} %get-tuple-element.75), calls=%async_computation.2 | async-start | bytes 1572864 | tf_op jit(solution)/shard_map/all_to_all | solution.py:556
  69.2 8.3 %copy-start.2 = (bf16[256,512]{1,0:T(8,128)(2,1)S(1)}, bf16[256,512]{1,0:T(8,128)(2,1)}, u32[]{:S(2)}) copy-start(bf16[256,512]{1,0:T(8,128)(2,1)} %x_ref.5) | copy-start | bytes 786436
  69.2 8.4 %copy-start.3 = (bf16[256,512]{1,0:T(8,128)(2,1)S(1)}, bf16[256,512]{1,0:T(8,128)(2,1)}, u32[]{:S(2)}) copy-start(bf16[256,512]{1,0:T(8,128)(2,1)} %z_ref.3) | copy-start | bytes 786436
  69.2 8.4 %copy-start.7 = (f32[8,256]{1,0:T(8,128)S(1)}, f32[8,256]{1,0:T(8,128)}, u32[]{:S(2)}) copy-start(f32[8,256]{1,0:T(8,128)} %dt_ref.3) | copy-start | bytes 24580
  71.6 17.8 %all-to-all-start.3 = ((bf16[32,48,128]{2,1,0:T(8,128)(2,1)}), bf16[32,48,128]{2,1,0:T(8,128)(2,1)S(1)}, u32[]{:S(2)}, u32[]{:S(2)}) async-start(bf16[32,48,128]{2,1,0:T(8,128)(2,1)} %get-tuple-element.130), calls=%async_computation.3 | async-start | bytes 786432 | tf_op jit(solution)/shard_map/all_to_all | solution.py:584
  89.3 15.5 %copy-start.10 = (f32[512]{0:T(512)S(1)}, f32[512]{0:T(512)}, u32[]{:S(2)}) copy-start(f32[512]{0:T(512)} %param.31) | copy-start | bytes 6148

commit v6 on v4

--- a/solution.py
+++ b/solution.py
@@ -76,12 +76,12 @@
 
 
 def prefix_x_kernel(
-    meta_ref, x_ref, halo_ref, dt_ref, rate_ref, taps_ref,
-    xc_ref, cum_ref, step_ref, weighted_ref, logs_ref, ext_ref, *, base,
+    meta_ref, x_ref, dt_ref, rate_ref, taps_ref,
+    xc_ref, cum_ref, step_ref, weighted_ref, first_ref, logs_ref, ext_ref, *, base,
 ):
     length, channels = x_ref.shape
     heads = rate_ref.shape[0]
-    ext_ref[:HALO] = halo_ref[...].astype(F32)
+    ext_ref[:HALO] = jnp.zeros((HALO, channels), F32)
     ext_ref[HALO:] = x_ref[...].astype(F32)
     taps = taps_ref[...].astype(F32)
     count = taps.shape[0]
@@ -97,7 +97,9 @@
     lane = iota((heads, length), 1)
 
     def weigh(at, weight):
-        weighted_ref[at] = (xc_ref[...].astype(F32) * expand(weight.T, channels // heads)).astype(BF)
+        wide = expand(weight.T, channels // heads)
+        first_ref[at] = wide[:HALO]
+        weighted_ref[at] = (xc_ref[...].astype(F32) * wide).astype(BF)
 
     ends = [cumulative[:, length - 1 :]]
     weigh(0, jnp.exp(ends[0] - cumulative) * step)
@@ -199,8 +201,8 @@
 
 
 def prefix_state_kernel(
-    meta_ref, bc_ref, bchalo_ref, taps_ref, weighted_ref, logs_ref, xtails_ref,
-    sent_ref, b_ref, c_ref, ext_ref, tile_ref, *, base, tail_base,
+    meta_ref, x_ref, halo_ref, xtaps_ref, bc_ref, bchalo_ref, taps_ref, weighted_ref, first_ref, logs_ref, xtails_ref,
+    sent_ref, b_ref, c_ref, xfirst_ref, ext_ref, tile_ref, edge_ref, *, base, tail_base,
 ):
     _, length, channels = weighted_ref.shape
     width = bchalo_ref.shape[1]
@@ -222,10 +224,21 @@
     c_ref[...] = convolved[:, n_state:]
     rows = channels // n_ctx
     misc = xrows + 16
+    edge_ref[:HALO] = halo_ref[...].astype(F32)
+    edge_ref[HALO:] = x_ref[:HALO].astype(F32)
+    taps = xtaps_ref[...].astype(F32)
+    total = taps[0:1] * edge_ref[HALO - count + 1 : 2 * HALO - count + 1]
+    for i in range(1, count):
+        first = HALO - count + 1 + i
+        total = total + taps[i : i + 1] * edge_ref[first : first + HALO]
+    xfirst = silu(total).astype(BF)
+    xfirst_ref[...] = xfirst
 
     def send(at):
+        edge = (xfirst.astype(F32) * first_ref[at]).astype(BF)
+        weighted = jnp.concatenate([edge, weighted_ref[at, HALO:, :]], axis=0)
         state = lax.dot_general(
-            weighted_ref[at], b_rows, (((0,), (0,)), ((), ())), preferred_element_type=F32
+            weighted, b_rows, (((0,), (0,)), ((), ())), preferred_element_type=F32
         )
         first = misc + at * rows
         sent_ref[:, first : first + rows, :] = state.astype(BF).reshape(n_ctx, rows, n_state)
@@ -259,13 +272,13 @@
         sent_ref[o, xrows:misc, :] = jnp.concatenate(tails, axis=0).astype(BF)
 
 
-def prefix_mix_kernel(xc_ref, b_ref, c_ref, cum_ref, step_ref, skip_ref, z_ref, y_ref, scale_ref):
+def prefix_mix_kernel(xc_ref, xfirst_ref, b_ref, c_ref, cum_ref, step_ref, skip_ref, z_ref, y_ref, scale_ref):
     length, channels = xc_ref.shape
     scores = lax.dot_general(
         c_ref[...], b_ref[...], (((1,), (1,)), ((), ())), preferred_element_type=F32
     )
     mask = iota((length, length), 1) <= iota((length, length), 0)
-    values = xc_ref[...]
+    values = jnp.concatenate([xfirst_ref[...], xc_ref[HALO:]], axis=0)
     cumulative = cum_ref[...]
     gate = silu(z_ref[...].astype(F32))
     scale_ref[...] = expand(jnp.exp(cumulative).T, channels // cumulative.shape[0]) * gate
@@ -438,14 +451,17 @@
         bout_ref[rows] = jnp.where(segment[rows] < BR_PER, scaled, 0.0).astype(BF)
 
 
-def call(kernel, outs, scratch, args, smem=0, smem_out=False):
-    def where(scalar):
+def call(kernel, outs, scratch, args, smem=0, smem_out=False, grid=False):
+    def where(scalar, shape):
+        if grid and not scalar:
+            return pl.BlockSpec(shape, lambda _, n=len(shape): (0,) * n)
         return pl.BlockSpec(memory_space=pltpu.SMEM if scalar else pltpu.VMEM)
 
     return pl.pallas_call(
         kernel,
-        in_specs=[where(i < smem) for i in range(len(args))],
-        out_specs=[where(smem_out and i == 0) for i in range(len(outs))],
+        grid=(1,) if grid else (),
+        in_specs=[where(i < smem, a.shape) for i, a in enumerate(args)],
+        out_specs=[where(smem_out and i == 0, s) for i, (s, _) in enumerate(outs)],
         out_shape=[jax.ShapeDtypeStruct(s, t) for s, t in outs],
         scratch_shapes=[(pltpu.SMEM if len(s) == 1 else pltpu.VMEM)(s, t) for s, t in scratch],
         compiler_params=pltpu.CompilerParams(vmem_limit_bytes=24 * 2**20),
@@ -498,7 +514,7 @@
     tail = conv_x.shape[0] - 1
     onward = [(i, i + 1) for i in range(n_ctx - 1)]
 
-    [spread] = call(spread_kernel, [((n_tp, length // n_tp, 2 * width), BF)], [], [prefix_bc, branch_bc])
+    [spread] = call(spread_kernel, [((n_tp, length // n_tp, 2 * width), BF)], [], [prefix_bc, branch_bc], grid=True)
     gathered = lax.all_to_all(spread, "tp", 0, 0, tiled=True).reshape(length, 2 * width)
     rates = decay_rate[:, None]
     skips = jnp.repeat(skip, channels // heads)[None]
@@ -522,26 +538,27 @@
         smem_out=True,
     )
     halo = lax.ppermute(last, "ctx", onward)
-    xc, cumulative, step, weighted, logs = call(
+    xc, cumulative, step, weighted, first, logs = call(
         functools.partial(prefix_x_kernel, base=at_positions),
         [
             ((length, channels), BF),
             ((heads, length), F32),
             ((heads, length), F32),
             ((1 + SLOTS, length, channels), BF),
+            ((1 + SLOTS, HALO, channels), F32),
             ((heads, n_state), F32),
         ],
         [((HALO + length, channels), F32)],
-        [meta, prefix_x, halo, prefix_dt, rates, conv_x],
+        [meta, prefix_x, prefix_dt, rates, conv_x],
         smem=1,
     )
     gathered, weighted = lax.optimization_barrier((gathered, weighted))
     bc_halo = lax.ppermute(gathered[length - HALO :, :width], "ctx", onward)
-    sent, b_rows, c_rows = call(
+    sent, b_rows, c_rows, xfirst = call(
         functools.partial(prefix_state_kernel, base=at_positions, tail_base=at_tails),
-        [((n_ctx, xrows + 16 + (1 + SLOTS) * rows, n_state), BF), ((length, n_state), BF), ((length, n_state), BF)],
-        [((HALO + length, width), F32), ((bounds, 8, width), F32)],
-        [meta, gathered, bc_halo, conv_bc, weighted, logs, xtails],
+        [((n_ctx, xrows + 16 + (1 + SLOTS) * rows, n_state), BF), ((length, n_state), BF), ((length, n_state), BF), ((HALO, channels), BF)],
+        [((HALO + length, width), F32), ((bounds, 8, width), F32), ((2 * HALO, channels), F32)],
+        [meta, prefix_x, halo, conv_x, gathered, bc_halo, conv_bc, weighted, first, logs, xtails],
         smem=1,
     )
     got = lax.all_to_all(sent, "ctx", 0, 0, tiled=True)
@@ -549,7 +566,7 @@
         prefix_mix_kernel,
         [((length, channels), F32), ((length, channels), F32)],
         [],
-        [xc, b_rows, c_rows, cumulative, step, skips, prefix_z],
+        [xc, xfirst, b_rows, c_rows, cumulative, step, skips, prefix_z],
     )
     got, y, scale = lax.optimization_barrier((got, y, scale))
 
@@ -562,12 +579,13 @@
     ]
 
     def usual():
-        return call(scan, scan_out, scan_scratch, [meta, got], smem=1)[0]
+        return call(scan, scan_out, scan_scratch, [meta, got], smem=1, grid=True)[0]
 
     def crowded():
         here = (block_of == me)[None, :] & (slot_of[None, :] == order[SLOTS:, None])
         positions = jnp.sum(jnp.where(here, (bound_pos - block_of * length + 1)[None, :], 0), axis=1) - 1
-        extra = more_states(xc, b_rows, step, cumulative, positions, n_ctx)
+        whole = jnp.concatenate([xfirst, xc[HALO:]], axis=0)
+        extra = more_states(whole, b_rows, step, cumulative, positions, n_ctx)
         extra = lax.all_to_all(extra, "ctx", 0, 0, tiled=True)
         return call(scan, scan_out, scan_scratch, [meta, got, extra], smem=1)[0]
 
@@ -596,6 +614,7 @@
             [],
             [meta, squares, gated, branch_gated, gain],
             smem=1,
+            grid=True,
         )
     )
 

time: 105 us -> 104 us (level)
  transfers between devices with their start and end apart: 5 -> 5, of which waited for: 5 -> 4; matrix products, arithmetic and copies ran while one was open for 1% -> 1% of each run, Pallas kernels for 8% -> 9%
where the time goes in v6:
time: 104 us
  starting transfers between devices  38.7 us (37%)
  waiting for transfers between devices  28.2 us (27%)
  Pallas kernels  17.7 us (17%)
  blocking collectives  14.9 us (14%)
  local copies, waits for them, and re-layouts  1.73 us (2%)
  between operations  1.49 us (1%)
    pallas_call x9, Pallas kernels, call(): pl.pallas_call(kernel, grid=(1,) if grid else (), in_specs=[where(i < sme...  17.7 us
    all_to_all x1, waiting for transfers between devices, body(): got = lax.all_to_all(sent, 'ctx', 0, 0, tiled=True)  16.1 us
    all_to_all x1, blocking collectives, body(): squares = lax.all_to_all(squares, 'tp', 0, 0, tiled=True)  14.9 us
    all_to_all x1, starting transfers between devices, body(): lax.all_to_all(spread, 'tp', 0, 0, tiled=True).reshape(length, 2 * width)  11.8 us
    all_to_all x1, starting transfers between devices, body(): got = lax.all_to_all(sent, 'ctx', 0, 0, tiled=True)  11.6 us
    all_to_all x1, starting transfers between devices, body(): back = lax.all_to_all(back, 'ctx', 0, 0, tiled=True)  8.81 us
    all_to_all x1, waiting for transfers between devices, body(): back = lax.all_to_all(back, 'ctx', 0, 0, tiled=True)  7.3 us
    all_to_all x1, waiting for transfers between devices, body(): lax.all_to_all(spread, 'tp', 0, 0, tiled=True).reshape(length, 2 * width)  4.02 us
  transfers between devices with their start and end apart: 5, of which 4 were waited for; matrix products, arithmetic and copies ran while one was open for 1% of the time, Pallas kernels for 9%

profile of v6, /device:TPU:1, one launch (start us, length us, event | category | flops | bytes accessed | tf_op | source)
XLA Modules:
  0.0 103.6 jit_solution(2639563327520461712)
XLA Ops:
  0.6 0.0 copy-start
  0.6 0.0 copy-start.4
  0.7 0.7 copy-done.4
  1.4 0.7 copy-done.5
  2.1 0.7 shard_map.177
  2.8 11.8 %all-to-all-start.1 = ((bf16[16,16,512]{2,1,0:T(8,128)(2,1)}), bf16[16,16,512]{2,1,0:T(8,128)(2,1)S(1)}, u32[]{:S(2)}, u32[]{:S(2)}) async-start(bf16[16,16,512]{2,1,0:T(8,128)(2,1)} %shard_map.177), calls=%async_computation.1 | async-start | bytes 524288 | tf_op jit(solution)/shard_map/all_to_all | solution.py:518
  14.6 0.0 copy-done
  14.7 0.0 copy-done.11
  14.7 0.0 copy-done.12
  14.7 0.0 copy-done.13
  14.7 0.0 copy-done.16
  14.7 0.0 copy-start.14
  14.7 0.0 copy-start.6
  14.7 0.0 copy-start.8
  14.7 2.1 %shard_map.176 = (s32[94]{0:T(128)S(1)}, bf16[32,32,128]{2,1,0:T(8,128)(2,1)S(1)}, bf16[16,512]{1,0:T(8,128)(2,1)S(1)}) custom-call(s32[1]{0:T(128)} %bitcast.11.me_ref, s32[8]{0:T(128)S(1)} %copy-done.16, s32[64]{0:T(128)S(1)} %copy-done.11, s32[64]{0:T(128)S(1)} %copy-done.12, s32[64]{0:T(128)S(1)} %copy-done.13, bf16[256,512]{1,0:T(8,128)(2,1)S(1)} %copy-done), custom_call_target="tpu_custom_call" | custom-call | flops 2000000000 | bytes 4000000 | tf_op jit(solution)/shard_map/pallas_call | solution.py:460
  16.8 3.2 %collective-permute-start = (bf16[16,512]{1,0:T(8,128)(2,1)S(1)}, bf16[16,512]{1,0:T(8,128)(2,1)S(1)}, u32[]{:S(2)}, u32[]{:S(2)}) collective-permute-start(bf16[16,512]{1,0:T(8,128)(2,1)S(1)} %get-tuple-element.74), channel_id=1, source_target_pairs={{0,16},{16,32},{32,48},{48,64},{64,80},{80,96},{96,112},{112,128},... | collective-permute-start | bytes 49160 | tf_op jit(solution)/shard_map/ppermute | solution.py:540
  20.1 0.0 copy-done.14
  20.1 0.1 copy.34.rate_ref
  20.1 0.0 copy-done.6
  20.2 0.0 copy-done.8
  20.2 2.2 %shard_map.178 = (bf16[256,512]{1,0:T(8,128)(2,1)S(1)}, f32[8,256]{1,0:T(8,128)S(1)}, f32[8,256]{1,0:T(8,128)S(1)}, bf16[3,256,512]{2,1,0:T(8,128)(2,1)S(1)}, f3...) custom-call(s32[94]{0:T(128)S(1)} %get-tuple-element.73.meta_ref, bf16[256,512]{1,0:T(8,128)(2,1)S(1)} %copy-done, ...), custom_call_target="tpu_custom_call" | custom-call | flops 2000000000 | bytes 4000000 | tf_op jit(solution)/shard_map/pallas_call | solution.py:460
  22.3 4.0 %all-to-all-done.1 = bf16[16,16,512]{2,1,0:T(8,128)(2,1)S(1)} async-done(((bf16[16,16,512]{2,1,0:T(8,128)(2,1)}), bf16[16,16,512]{2,1,0:T(8,128)(2,1)S(1)}, u32[]{:S(2)}, u32[]{:S(2)}) %all-to-all-start.1) | async-done | bytes 262176 | tf_op jit(solution)/shard_map/all_to_all | solution.py:518
  26.4 3.2 %collective-permute-start.1 = (bf16[16,256]{1,0:T(8,128)(2,1)S(1)}, bf16[16,256]{1,0:T(8,128)(2,1)S(1)}, u32[]{:S(2)}, u32[]{:S(2)}) collective-permute-start(bf16[16,256]{1,0:T(8,128)(2,1)S(1)} %slice.9), channel_id=1, source_target_pairs={{0,16},{16,32},{32,48},{48,64},{64,80},{80,96},{96,112},{112,128},... | collective-permute-start | bytes 24584 | tf_op jit(solution)/shard_map/ppermute | solution.py:556
  29.6 0.0 collective-permute-done.halo_ref
  29.6 0.8 collective-permute-done.1.bchalo_ref
  30.3 0.0 copy-done.9
  30.3 2.5 %shard_map.179 = (bf16[32,96,128]{2,1,0:T(8,128)(2,1)}, bf16[256,128]{1,0:T(8,128)(2,1)S(1)}, bf16[256,128]{1,0:T(8,128)(2,1)S(1)}, bf16[16,512]{1,0:T(8,128)(2,1)S(1)}) custom-call(s32[94]{0:T(128)S(1)} %get-tuple-element.73.meta_ref, bf16[256,512]{1,0:T(8,128)(2,1)S(1)} %copy-done, bf16[16,512]{1,0:T(8,128)(2,1)S(1)} %collective-permute-done.halo_ref, ...), custom_call_target="tpu_custom_call" | custom-call | flops 2000000000 | bytes 4000000 | tf_op jit(solution)/shard_map/pallas_call | solution.py:460
  32.8 11.6 %all-to-all-start.2 = ((bf16[32,96,128]{2,1,0:T(8,128)(2,1)}), bf16[32,96,128]{2,1,0:T(8,128)(2,1)}, u32[]{:S(2)}, u32[]{:S(2)}) async-start(bf16[32,96,128]{2,1,0:T(8,128)(2,1)} %get-tuple-element.81), calls=%async_computation.2 | async-start | bytes 1572864 | tf_op jit(solution)/shard_map/all_to_all | solution.py:564
  44.5 0.2 convert_reduce_fusion
  44.7 0.6 reduce_max.9
  46.0 0.0 copy-done.15
  46.0 0.1 broadcast_in_dim.89
  46.0 0.1 broadcast_in_dim_reshape.3.skip_ref
  46.1 0.0 copy-done.1
  46.1 1.1 %shard_map.180 = (f32[256,512]{1,0:T(8,128)S(1)}, f32[256,512]{1,0:T(8,128)S(1)}) custom-call(bf16[256,512]{1,0:T(8,128)(2,1)S(1)} %get-tuple-element.82.xc_ref, bf16[16,512]{1,0:T(8,128)(2,1)S(1)} %get-tuple-element.83.xfirst_ref, bf16[256,128]{1,0:T(8,128)(2,1)S(1)} %get-tuple-element.84.b_ref, bf16[256,128]{1,0:T(8,128)(2,1)S(1)} %get-tuple-element.85.c_ref, ...), custom_call_target="tpu_custom_call" | custom-call | flops 2000000000 | bytes 4000000 | tf_op jit(solution)/shard_map/pallas_call | solution.py:460
  47.2 16.1 %all-to-all-done.2.got_ref = bf16[32,96,128]{2,1,0:T(8,128)(2,1)} async-done(((bf16[32,96,128]{2,1,0:T(8,128)(2,1)}), bf16[32,96,128]{2,1,0:T(8,128)(2,1)}, u32[]{:S(2)}, u32[]{:S(2)}) %all-to-all-start.2) | async-done | bytes 786464 | tf_op jit(solution)/shard_map/all_to_all | solution.py:564
  63.4 2.3 %conditional.1 = (bf16[32,48,128]{2,1,0:T(8,128)(2,1)}) conditional(s32[]{:T(128)} %convert_element_type.37, (s32[94]{0:T(128)S(1)}, bf16[32,96,128]{2,1,0:T(8,128)(2,1)}) %tuple.17, (s32[]{:T(128)}, s32[8]{0:T(128)S(1)}, s32[8]{0:T(128)S(1)}, s32[8]{0:T(128)S(1)}, s32[8]{0:T(128)S(1)}, /*index=5*/f32[8,256]{1,0:T(8,128)S(1)}, ...), branch_computations={%region_2.3_spmd, %region_3.6_spmd} | conditional | flops 2207683328 | bytes 13670660 | solution.py:592
  63.4 2.3 %branch_0_fun.1 = bf16[32,48,128]{2,1,0:T(8,128)(2,1)} custom-call(s32[94]{0:T(128)S(1)} %get-tuple-element.15.meta_ref, bf16[32,96,128]{2,1,0:T(8,128)(2,1)} %get-tuple-element.32.got_ref), custom_call_target="tpu_custom_call" | custom-call | flops 2000000000 | bytes 4000000 | tf_op jit(solution)/shard_map/cond/branch_0_fun/pallas_call | solution.py:460
  65.7 8.8 %all-to-all-start.3 = ((bf16[32,48,128]{2,1,0:T(8,128)(2,1)}), bf16[32,48,128]{2,1,0:T(8,128)(2,1)S(1)}, u32[]{:S(2)}, u32[]{:S(2)}) async-start(bf16[32,48,128]{2,1,0:T(8,128)(2,1)} %get-tuple-element.140), calls=%async_computation.3 | async-start | bytes 786432 | tf_op jit(solution)/shard_map/all_to_all | solution.py:593
  74.5 0.0 copy-done.2
  74.5 0.0 copy-done.3
  74.5 0.0 copy-done.7
  74.5 3.5 %shard_map.181 = (f32[256,512]{1,0:T(8,128)S(1)}, bf16[256,128]{1,0:T(8,128)(2,1)S(1)}, f32[256,512]{1,0:T(8,128)S(1)}) custom-call(s32[94]{0:T(128)S(1)} %get-tuple-element.73.meta_ref, bf16[256,512]{1,0:T(8,128)(2,1)S(1)} %copy-done.2, bf16[256,512]{1,0:T(8,128)(2,1)S(1)} %bitcast.28, bf16[32,96,128]{2,1,0:T(8,128)(2,1)} %all-to-all-done.2.got_ref, ...), custom_call_target="tpu_custom_call" | custom-call | flops 2000000000 | bytes 4000000 | tf_op jit(solution)/shard_map/pallas_call | solution.py:460
  78.0 7.3 %all-to-all-done.3.back_ref = bf16[32,48,128]{2,1,0:T(8,128)(2,1)S(1)} async-done(((bf16[32,48,128]{2,1,0:T(8,128)(2,1)}), bf16[32,48,128]{2,1,0:T(8,128)(2,1)S(1)}, u32[]{:S(2)}, u32[]{:S(2)}) %all-to-all-start.3) | async-done | bytes 393248 | tf_op jit(solution)/shard_map/all_to_all | solution.py:593
  85.3 1.8 %shard_map.182 = (f32[256,512]{1,0:T(8,128)S(1)}, f32[256,512]{1,0:T(8,128)S(1)}, f32[16,8,128]{2,1,0:T(8,128)S(1)}) custom-call(s32[94]{0:T(128)S(1)} %get-tuple-element.73.meta_ref, f32[256,512]{1,0:T(8,128)S(1)} %get-tuple-element.90.y_ref, f32[256,512]{1,0:T(8,128)S(1)} %get-tuple-element.91.scale_ref, bf16[256,128]{1,0:T(8,128)(2,1)S(1)} %get-tuple-element.85.c_ref, ...), custom_call_target="tpu_custom_call" | custom-call | flops 2000000000 | bytes 4000000 | tf_op jit(solution)/shard_map/pallas_call | solution.py:460
  87.1 14.9 %all_to_all.25.sq_ref = f32[16,8,128]{2,1,0:T(8,128)S(1)} all-to-all(f32[16,8,128]{2,1,0:T(8,128)S(1)} %get-tuple-element.96), channel_id=1, replica_groups=mesh['ctx'=32,'tp'=16] {'tp'}, dimensions={0} | all-to-all | bytes 131072 | tf_op jit(solution)/shard_map/all_to_all | solution.py:609
  102.0 0.0 copy-done.10
  102.0 1.6 %shard_map.183 = (bf16[256,512]{1,0:T(8,128)(2,1)}, bf16[256,512]{1,0:T(8,128)(2,1)}) custom-call(s32[94]{0:T(128)S(1)} %get-tuple-element.73.meta_ref, f32[16,8,128]{2,1,0:T(8,128)S(1)} %all_to_all.25.sq_ref, f32[256,512]{1,0:T(8,128)S(1)} %get-tuple-element.97.g_ref, f32[256,512]{1,0:T(8,128)S(1)} %get-tuple-element.98.bg_ref, f32[1,512]{1,0:T(1,128)S(1)} %bitcast.29), custom_call_target="tpu_custom_call" | custom-call | flops 2000000000 | bytes 4000000 | tf_op jit(solution)/shard_map/pallas_call | solution.py:460
  (15 shorter events, 0.0 us)
Async XLA Ops:
  0.6 14.0 %copy-start = (bf16[256,512]{1,0:T(8,128)(2,1)S(1)}, bf16[256,512]{1,0:T(8,128)(2,1)}, u32[]{:S(2)}) copy-start(bf16[256,512]{1,0:T(8,128)(2,1)} %x_ref.6) | copy-start | bytes 786436
  0.6 0.7 copy-start.4
  1.4 0.7 copy-start.5
  2.1 12.6 %copy-start.11 = (s32[64]{0:T(128)S(1)}, s32[64]{0:T(128)}, u32[]{:S(2)}) copy-start(s32[64]{0:T(128)} %owner_ref.1) | copy-start | bytes 772
  2.1 12.6 %copy-start.12 = (s32[64]{0:T(128)S(1)}, s32[64]{0:T(128)}, u32[]{:S(2)}) copy-start(s32[64]{0:T(128)} %parent_ref.1) | copy-start | bytes 772
  2.1 12.6 %copy-start.13 = (s32[64]{0:T(128)S(1)}, s32[64]{0:T(128)}, u32[]{:S(2)}) copy-start(s32[64]{0:T(128)} %len_ref.1) | copy-start | bytes 772
  2.1 12.6 %copy-start.16 = (s32[8]{0:T(128)S(1)}, s32[8]{0:T(128)}, u32[]{:S(2)}) copy-start(s32[8]{0:T(128)} %bound_ref.1) | copy-start | bytes 100
  2.8 23.5 %all-to-all-start.1 = ((bf16[16,16,512]{2,1,0:T(8,128)(2,1)}), bf16[16,16,512]{2,1,0:T(8,128)(2,1)S(1)}, u32[]{:S(2)}, u32[]{:S(2)}) async-start(bf16[16,16,512]{2,1,0:T(8,128)(2,1)} %shard_map.177), calls=%async_computation.1 | async-start | bytes 524288 | tf_op jit(solution)/shard_map/all_to_all | solution.py:518
  14.7 5.4 %copy-start.14 = (f32[8]{0:T(128)S(1)}, f32[8]{0:T(128)}, u32[]{:S(2)}) copy-start(f32[8]{0:T(128)} %param.29) | copy-start | bytes 100
  14.7 5.4 %copy-start.6 = (f32[8,256]{1,0:T(8,128)S(1)}, f32[8,256]{1,0:T(8,128)}, u32[]{:S(2)}) copy-start(f32[8,256]{1,0:T(8,128)} %dt_ref.2) | copy-start | bytes 24580
  14.7 5.4 %copy-start.8 = (bf16[4,512]{1,0:T(4,128)(2,1)S(1)}, bf16[4,512]{1,0:T(4,128)(2,1)}, u32[]{:S(2)}) copy-start(bf16[4,512]{1,0:T(4,128)(2,1)} %xtaps_ref.3) | copy-start | bytes 12292
  16.8 12.7 %collective-permute-start = (bf16[16,512]{1,0:T(8,128)(2,1)S(1)}, bf16[16,512]{1,0:T(8,128)(2,1)S(1)}, u32[]{:S(2)}, u32[]{:S(2)}) collective-permute-start(bf16[16,512]{1,0:T(8,128)(2,1)S(1)} %get-tuple-element.74), channel_id=1, source_target_pairs={{0,16},{16,32},{32,48},{48,64},{64,80},{80,96},{96,112},{112,128},... | collective-permute-start | bytes 49160 | tf_op jit(solution)/shard_map/ppermute | solution.py:540
  20.2 10.2 %copy-start.9 = (bf16[4,256]{1,0:T(4,128)(2,1)S(1)}, bf16[4,256]{1,0:T(4,128)(2,1)}, u32[]{:S(2)}) copy-start(bf16[4,256]{1,0:T(4,128)(2,1)} %taps_ref.5) | copy-start | bytes 6148
  26.4 4.0 %collective-permute-start.1 = (bf16[16,256]{1,0:T(8,128)(2,1)S(1)}, bf16[16,256]{1,0:T(8,128)(2,1)S(1)}, u32[]{:S(2)}, u32[]{:S(2)}) collective-permute-start(bf16[16,256]{1,0:T(8,128)(2,1)S(1)} %slice.9), channel_id=1, source_target_pairs={{0,16},{16,32},{32,48},{48,64},{64,80},{80,96},{96,112},{112,128},... | collective-permute-start | bytes 24584 | tf_op jit(solution)/shard_map/ppermute | solution.py:556
  32.8 13.1 %copy-start.15 = (f32[8]{0:T(128)S(1)}, f32[8]{0:T(128)}, u32[]{:S(2)}) copy-start(f32[8]{0:T(128)} %param.30) | copy-start | bytes 100
  32.8 13.3 %copy-start.1 = (bf16[256,512]{1,0:T(8,128)(2,1)S(1)}, bf16[256,512]{1,0:T(8,128)(2,1)}, u32[]{:S(2)}) copy-start(bf16[256,512]{1,0:T(8,128)(2,1)} %z_ref.2) | copy-start | bytes 786436
  32.8 30.5 %all-to-all-start.2 = ((bf16[32,96,128]{2,1,0:T(8,128)(2,1)}), bf16[32,96,128]{2,1,0:T(8,128)(2,1)}, u32[]{:S(2)}, u32[]{:S(2)}) async-start(bf16[32,96,128]{2,1,0:T(8,128)(2,1)} %get-tuple-element.81), calls=%async_computation.2 | async-start | bytes 1572864 | tf_op jit(solution)/shard_map/all_to_all | solution.py:564
  63.4 11.2 %copy-start.2 = (bf16[256,512]{1,0:T(8,128)(2,1)S(1)}, bf16[256,512]{1,0:T(8,128)(2,1)}, u32[]{:S(2)}) copy-start(bf16[256,512]{1,0:T(8,128)(2,1)} %x_ref.7) | copy-start | bytes 786436
  63.4 11.2 %copy-start.3 = (bf16[256,512]{1,0:T(8,128)(2,1)S(1)}, bf16[256,512]{1,0:T(8,128)(2,1)}, u32[]{:S(2)}) copy-start(bf16[256,512]{1,0:T(8,128)(2,1)} %z_ref.3) | copy-start | bytes 786436
  63.4 11.2 %copy-start.7 = (f32[8,256]{1,0:T(8,128)S(1)}, f32[8,256]{1,0:T(8,128)}, u32[]{:S(2)}) copy-start(f32[8,256]{1,0:T(8,128)} %dt_ref.3) | copy-start | bytes 24580
  65.7 19.6 %all-to-all-start.3 = ((bf16[32,48,128]{2,1,0:T(8,128)(2,1)}), bf16[32,48,128]{2,1,0:T(8,128)(2,1)S(1)}, u32[]{:S(2)}, u32[]{:S(2)}) async-start(bf16[32,48,128]{2,1,0:T(8,128)(2,1)} %get-tuple-element.140), calls=%async_computation.3 | async-start | bytes 786432 | tf_op jit(solution)/shard_map/all_to_all | solution.py:593
  85.3 16.7 %copy-start.10 = (f32[512]{0:T(512)S(1)}, f32[512]{0:T(512)}, u32[]{:S(2)}) copy-start(f32[512]{0:T(512)} %param.31) | copy-start | bytes 6148

commit v7 on v6

--- a/solution.py
+++ b/solution.py
@@ -193,71 +193,41 @@
         tails_ref[o] = jnp.concatenate(tiles, axis=0).astype(BF)
 
 
-def spread_kernel(prefix_ref, branch_ref, out_ref):
-    width = prefix_ref.shape[1]
-    for i in range(out_ref.shape[0]):
-        out_ref[i, :, :width] = prefix_ref[...]
-        out_ref[i, :, width:] = branch_ref[...]
-
-
-def prefix_state_kernel(
-    meta_ref, x_ref, halo_ref, xtaps_ref, bc_ref, bchalo_ref, taps_ref, weighted_ref, first_ref, logs_ref, xtails_ref,
-    sent_ref, b_ref, c_ref, xfirst_ref, ext_ref, tile_ref, edge_ref, *, base, tail_base,
+def convolve(ext_ref, taps_ref, first, height):
+    taps = taps_ref[...].astype(F32)
+    count = taps.shape[0]
+    total = taps[0:1] * ext_ref[first - count + 1 : first - count + 1 + height]
+    for i in range(1, count):
+        start = first - count + 1 + i
+        total = total + taps[i : i + 1] * ext_ref[start : start + height]
+    return silu(total).astype(BF)
+
+
+def over_rows(weighted, b_rows):
+    return lax.dot_general(weighted, b_rows, (((0,), (0,)), ((), ())), preferred_element_type=F32)
+
+
+def prefix_later_kernel(
+    meta_ref, bc_ref, taps_ref, weighted_ref, logs_ref, xtails_ref,
+    part_ref, misc_ref, conv_ref, ext_ref, tile_ref, *, base, tail_base,
 ):
     _, length, channels = weighted_ref.shape
-    width = bchalo_ref.shape[1]
+    width = taps_ref.shape[1]
     n_state = width // 2
     n_ctx, xrows, _ = xtails_ref.shape
     heads = logs_ref.shape[0]
     bc = bc_ref[:, :width]
-    ext_ref[:HALO] = bchalo_ref[...].astype(F32)
-    ext_ref[HALO:] = bc.astype(F32)
-    taps = taps_ref[...].astype(F32)
-    count = taps.shape[0]
-    total = taps[0:1] * ext_ref[HALO - count + 1 : HALO - count + 1 + length]
-    for i in range(1, count):
-        first = HALO - count + 1 + i
-        total = total + taps[i : i + 1] * ext_ref[first : first + length]
-    convolved = silu(total).astype(BF)
-    b_rows = convolved[:, :n_state]
-    b_ref[...] = b_rows
-    c_ref[...] = convolved[:, n_state:]
-    rows = channels // n_ctx
-    misc = xrows + 16
-    edge_ref[:HALO] = halo_ref[...].astype(F32)
-    edge_ref[HALO:] = x_ref[:HALO].astype(F32)
-    taps = xtaps_ref[...].astype(F32)
-    total = taps[0:1] * edge_ref[HALO - count + 1 : 2 * HALO - count + 1]
-    for i in range(1, count):
-        first = HALO - count + 1 + i
-        total = total + taps[i : i + 1] * edge_ref[first : first + HALO]
-    xfirst = silu(total).astype(BF)
-    xfirst_ref[...] = xfirst
-
-    def send(at):
-        edge = (xfirst.astype(F32) * first_ref[at]).astype(BF)
-        weighted = jnp.concatenate([edge, weighted_ref[at, HALO:, :]], axis=0)
-        state = lax.dot_general(
-            weighted, b_rows, (((0,), (0,)), ((), ())), preferred_element_type=F32
-        )
-        first = misc + at * rows
-        sent_ref[:, first : first + rows, :] = state.astype(BF).reshape(n_ctx, rows, n_state)
-
-    send(0)
+    ext_ref[...] = bc.astype(F32)
+    convolved = convolve(ext_ref, taps_ref, HALO, length - HALO)
+    conv_ref[HALO:] = convolved
+    part_ref[0] = over_rows(weighted_ref[0, HALO:, :], convolved[:, :n_state])
     for slot in range(SLOTS):
-        position = meta_ref[base + slot]
-        first = misc + (1 + slot) * rows
-
-        @pl.when(position >= 0)
+
+        @pl.when(meta_ref[base + slot] >= 0)
         def _():
-            send(1 + slot)
-
-        @pl.when(position < 0)
-        def _():
-            sent_ref[:, first : first + rows, :] = jnp.zeros((n_ctx, rows, n_state), BF)
-
-    sent_ref[:, :xrows, :] = xtails_ref[...]
-    bounds = tile_ref.shape[0]
+            part_ref[1 + slot] = over_rows(weighted_ref[1 + slot, HALO:, :], convolved[:, :n_state])
+
+    misc_ref[:, :xrows, :] = xtails_ref[...]
     tail_tiles(meta_ref, tail_base, bc, tile_ref)
     row = iota((8, n_state), 0)
     per_head = n_ctx // heads
@@ -269,7 +239,50 @@
             tails.append(jnp.where(row < 4, tile_ref[first, :, lanes], tile_ref[second, :, lanes]))
         h = o // per_head
         tails[0] = jnp.where(row == LOGS, logs_ref[h : h + 1], tails[0])
-        sent_ref[o, xrows:misc, :] = jnp.concatenate(tails, axis=0).astype(BF)
+        misc_ref[o, xrows:, :] = jnp.concatenate(tails, axis=0).astype(BF)
+
+
+def prefix_state_kernel(
+    meta_ref, x_ref, halo_ref, xtaps_ref, bc_ref, bchalo_ref, taps_ref, first_ref, part_ref, misc_ref, conv_ref,
+    sent_ref, b_ref, c_ref, xfirst_ref, ext_ref, edge_ref, *, base,
+):
+    channels = x_ref.shape[1]
+    width = taps_ref.shape[1]
+    n_state = width // 2
+    n_ctx, misc, _ = misc_ref.shape
+    rows = channels // n_ctx
+    ext_ref[:HALO] = bchalo_ref[...].astype(F32)
+    ext_ref[HALO:] = bc_ref[:HALO, :width].astype(F32)
+    convolved = convolve(ext_ref, taps_ref, HALO, HALO)
+    b_rows = convolved[:, :n_state]
+    b_ref[:HALO] = b_rows
+    b_ref[HALO:] = conv_ref[HALO:, :n_state]
+    c_ref[:HALO] = convolved[:, n_state:]
+    c_ref[HALO:] = conv_ref[HALO:, n_state:]
+    edge_ref[:HALO] = halo_ref[...].astype(F32)
+    edge_ref[HALO:] = x_ref[:HALO].astype(F32)
+    xfirst = convolve(edge_ref, xtaps_ref, HALO, HALO)
+    xfirst_ref[...] = xfirst
+
+    def send(at):
+        weighted = (xfirst.astype(F32) * first_ref[at]).astype(BF)
+        state = part_ref[at] + over_rows(weighted, b_rows)
+        start = misc + at * rows
+        sent_ref[:, start : start + rows, :] = state.astype(BF).reshape(n_ctx, rows, n_state)
+
+    sent_ref[:, :misc, :] = misc_ref[...]
+    send(0)
+    for slot in range(SLOTS):
+        position = meta_ref[base + slot]
+        start = misc + (1 + slot) * rows
+
+        @pl.when(position >= 0)
+        def _():
+            send(1 + slot)
+
+        @pl.when(position < 0)
+        def _():
+            sent_ref[:, start : start + rows, :] = jnp.zeros((n_ctx, rows, n_state), BF)
 
 
 def prefix_mix_kernel(xc_ref, xfirst_ref, b_ref, c_ref, cum_ref, step_ref, skip_ref, z_ref, y_ref, scale_ref):
@@ -407,9 +420,13 @@
         return lax.dot_general(c_rows, state, (((1,), (1,)), ((), ())), preferred_element_type=F32)
 
     def squares(gated):
-        ones = jnp.ones((8, channels), F32)
+        square = gated * gated
+        total = square[:, :n_state]
+        for at in range(n_state, channels, n_state):
+            total = total + square[:, at : at + n_state]
+        ones = jnp.ones((8, n_state), F32)
         return lax.dot_general(
-            ones, gated * gated, (((1,), (1,)), ((), ())), precision=HIGH, preferred_element_type=F32
+            ones, total, (((1,), (1,)), ((), ())), precision=HIGH, preferred_element_type=F32
         )
 
     gated = y_ref[...] + scale_ref[...] * from_state(c_ref[...], 0)
@@ -514,7 +531,8 @@
     tail = conv_x.shape[0] - 1
     onward = [(i, i + 1) for i in range(n_ctx - 1)]
 
-    [spread] = call(spread_kernel, [((n_tp, length // n_tp, 2 * width), BF)], [], [prefix_bc, branch_bc], grid=True)
+    own = jnp.concatenate([prefix_bc, branch_bc], axis=1)
+    spread = jnp.broadcast_to(own[None], (n_tp, *own.shape))
     gathered = lax.all_to_all(spread, "tp", 0, 0, tiled=True).reshape(length, 2 * width)
     rates = decay_rate[:, None]
     skips = jnp.repeat(skip, channels // heads)[None]
@@ -554,11 +572,27 @@
     )
     gathered, weighted = lax.optimization_barrier((gathered, weighted))
     bc_halo = lax.ppermute(gathered[length - HALO :, :width], "ctx", onward)
+    part, misc, convolved = call(
+        functools.partial(prefix_later_kernel, base=at_positions, tail_base=at_tails),
+        [
+            ((1 + SLOTS, channels, n_state), F32),
+            ((n_ctx, xrows + 16, n_state), BF),
+            ((length, width), BF),
+        ],
+        [((length, width), F32), ((bounds, 8, width), F32)],
+        [meta, gathered, conv_bc, weighted, logs, xtails],
+        smem=1,
+    )
     sent, b_rows, c_rows, xfirst = call(
-        functools.partial(prefix_state_kernel, base=at_positions, tail_base=at_tails),
-        [((n_ctx, xrows + 16 + (1 + SLOTS) * rows, n_state), BF), ((length, n_state), BF), ((length, n_state), BF), ((HALO, channels), BF)],
-        [((HALO + length, width), F32), ((bounds, 8, width), F32), ((2 * HALO, channels), F32)],
-        [meta, prefix_x, halo, conv_x, gathered, bc_halo, conv_bc, weighted, first, logs, xtails],
+        functools.partial(prefix_state_kernel, base=at_positions),
+        [
+            ((n_ctx, xrows + 16 + (1 + SLOTS) * rows, n_state), BF),
+            ((length, n_state), BF),
+            ((length, n_state), BF),
+            ((HALO, channels), BF),
+        ],
+        [((2 * HALO, width), F32), ((2 * HALO, channels), F32)],
+        [meta, prefix_x, halo, conv_x, gathered, bc_halo, conv_bc, first, part, misc, convolved],
         smem=1,
     )
     got = lax.all_to_all(sent, "ctx", 0, 0, tiled=True)
@@ -568,7 +602,6 @@
         [],
         [xc, xfirst, b_rows, c_rows, cumulative, step, skips, prefix_z],
     )
-    got, y, scale = lax.optimization_barrier((got, y, scale))
 
     scan = functools.partial(scan_kernel, n_branch=branches, bounds=bounds)
     scan_out = [((n_ctx, (1 + BR_PER) * rows, n_state), BF)]

time: 104 us -> 104 us (level)
  waiting for transfers between devices: 28.2 us -> 23.8 us
  local copies, waits for them, and re-layouts: 1.73 us -> 3.92 us
  starting transfers between devices: 38.7 us -> 37.5 us
  Pallas kernels: 17.7 us -> 18.9 us
    all_to_all x1, waiting for transfers between devices: 4.02 us -> 0.4 us  [body(): lax.all_to_all(spread, 'tp', 0, 0, tiled=True).reshape(length, 2 * width)]
    unnamed x34 -> x32, local copies, waits for them, and re-layouts: 1.49 us -> 2.95 us
    all_to_all x1, waiting for transfers between devices: 7.3 us -> 6.02 us  [body(): back = lax.all_to_all(back, 'ctx', 0, 0, tiled=True)]
    all_to_all x1, waiting for transfers between devices: 16.1 us -> 17.4 us  [body(): got = lax.all_to_all(sent, 'ctx', 0, 0, tiled=True)]
    pallas_call x9, Pallas kernels: 17.7 us -> 18.9 us  [call(): pl.pallas_call(kernel, grid=(1,) if grid else (), in_specs=[where(i < sme...]
    all_to_all x1, starting transfers between devices: 11.6 us -> 10.5 us  [body(): got = lax.all_to_all(sent, 'ctx', 0, 0, tiled=True)]
  transfers between devices with their start and end apart: 5 -> 5, of which waited for: 4 -> 3; matrix products, arithmetic and copies ran while one was open for 1% -> 1% of each run, Pallas kernels for 9% -> 11%
where the time goes in v7:
time: 104 us; the launch traced here: 103 us
  starting transfers between devices  37.5 us (36%)
  waiting for transfers between devices  23.8 us (23%)
  Pallas kernels  18.9 us (18%)
  blocking collectives  15.7 us (15%)
  local copies, waits for them, and re-layouts  3.92 us (4%)
  other arithmetic  1.55 us (1%)
  between operations  1.46 us (1%)
    pallas_call x9, Pallas kernels, call(): pl.pallas_call(kernel, grid=(1,) if grid else (), in_specs=[where(i < sme...  18.9 us
    all_to_all x1, waiting for transfers between devices, body(): got = lax.all_to_all(sent, 'ctx', 0, 0, tiled=True)  17.4 us
    all_to_all x1, blocking collectives, body(): squares = lax.all_to_all(squares, 'tp', 0, 0, tiled=True)  15.7 us
    all_to_all x1, starting transfers between devices, body(): lax.all_to_all(spread, 'tp', 0, 0, tiled=True).reshape(length, 2 * width)  11.8 us
    all_to_all x1, starting transfers between devices, body(): got = lax.all_to_all(sent, 'ctx', 0, 0, tiled=True)  10.5 us
    all_to_all x1, starting transfers between devices, body(): back = lax.all_to_all(back, 'ctx', 0, 0, tiled=True)  8.81 us
    all_to_all x1, waiting for transfers between devices, body(): back = lax.all_to_all(back, 'ctx', 0, 0, tiled=True)  6.02 us
    ppermute x1, starting transfers between devices, body(): halo = lax.ppermute(last, 'ctx', onward)  3.23 us
  transfers between devices with their start and end apart: 5, of which 3 were waited for; matrix products, arithmetic and copies ran while one was open for 1% of the time, Pallas kernels for 11%

profile of v7, /device:TPU:1, one launch (start us, length us, event | category | flops | bytes accessed | tf_op | source)
XLA Modules:
  0.0 102.9 jit_solution(8716397579839576534)
XLA Ops:
  0.6 0.7 pad_maximum_fusion.2
  1.3 0.7 broadcast_in_dim.95
  2.1 11.8 %all-to-all-start.1 = ((bf16[16,16,512]{2,1,0:T(8,128)(2,1)}), bf16[16,16,512]{2,1,0:T(8,128)(2,1)S(1)}, u32[]{:S(2)}, u32[]{:S(2)}) async-start(bf16[16,16,512]{2,1,0:T(8,128)(2,1)} %broadcast_in_dim.95), calls=%async_computation.1 | async-start | bytes 524288 | tf_op jit(solution)/shard_map/all_to_all | solution.py:536
  13.9 0.0 copy-start
  13.9 0.9 copy-done
  14.9 0.0 copy-start.10
  14.9 0.7 copy-done.10
  15.5 0.0 copy-start.11
  15.5 0.7 copy-done.11
  16.2 0.0 copy-start.12
  16.2 0.7 copy-done.12
  16.8 2.3 %shard_map.176 = (s32[94]{0:T(128)S(1)}, bf16[32,32,128]{2,1,0:T(8,128)(2,1)S(1)}, bf16[16,512]{1,0:T(8,128)(2,1)S(1)}) custom-call(s32[1]{0:T(128)} %bitcast.11.me_ref, s32[8]{0:T(128)} %bound_ref.1, s32[64]{0:T(128)S(1)} %copy-done.10, s32[64]{0:T(128)S(1)} %copy-done.11, s32[64]{0:T(128)S(1)} %copy-done.12, bf16[256,512]{1,0:T(8,128)(2,1)S(1)} %copy-done), custom_call_target="tpu_custom_call" | custom-call | flops 2000000000 | bytes 4000000 | tf_op jit(solution)/shard_map/pallas_call | solution.py:477
  19.2 3.2 %collective-permute-start = (bf16[16,512]{1,0:T(8,128)(2,1)S(1)}, bf16[16,512]{1,0:T(8,128)(2,1)S(1)}, u32[]{:S(2)}, u32[]{:S(2)}) collective-permute-start(bf16[16,512]{1,0:T(8,128)(2,1)S(1)} %get-tuple-element.75), channel_id=1, source_target_pairs={{0,16},{16,32},{32,48},{48,64},{64,80},{80,96},{96,112},{112,128},... | collective-permute-start | bytes 49160 | tf_op jit(solution)/shard_map/ppermute | solution.py:558
  22.4 0.0 copy-done.13
  22.4 0.1 copy.34.rate_ref
  22.5 0.0 copy-done.1
  22.5 0.0 copy-done.5
  22.5 0.0 copy-done.7
  22.5 2.7 %shard_map.177 = (bf16[256,512]{1,0:T(8,128)(2,1)S(1)}, f32[8,256]{1,0:T(8,128)S(1)}, f32[8,256]{1,0:T(8,128)S(1)}, bf16[3,256,512]{2,1,0:T(8,128)(2,1)S(1)}, f3...) custom-call(s32[94]{0:T(128)S(1)} %get-tuple-element.73.meta_ref, bf16[256,512]{1,0:T(8,128)(2,1)S(1)} %copy-done.1, ...), custom_call_target="tpu_custom_call" | custom-call | flops 2000000000 | bytes 4000000 | tf_op jit(solution)/shard_map/pallas_call | solution.py:477
  25.2 0.4 all-to-all-done.1
  25.6 3.2 %collective-permute-start.1 = (bf16[16,256]{1,0:T(8,128)(2,1)S(1)}, bf16[16,256]{1,0:T(8,128)(2,1)S(1)}, u32[]{:S(2)}, u32[]{:S(2)}) collective-permute-start(bf16[16,256]{1,0:T(8,128)(2,1)S(1)} %slice.9), channel_id=1, source_target_pairs={{0,16},{16,32},{32,48},{48,64},{64,80},{80,96},{96,112},{112,128},... | collective-permute-start | bytes 24584 | tf_op jit(solution)/shard_map/ppermute | solution.py:574
  28.8 0.0 copy-done.8
  28.8 1.7 %shard_map.178 = (f32[3,512,128]{2,1,0:T(8,128)S(1)}, bf16[32,48,128]{2,1,0:T(8,128)(2,1)S(1)}, bf16[256,256]{1,0:T(8,128)(2,1)S(1)}) custom-call(s32[94]{0:T(128)S(1)} %get-tuple-element.73.meta_ref, bf16[256,512]{1,0:T(8,128)(2,1)S(1)} %bitcast.27, bf16[4,256]{1,0:T(4,128)(2,1)S(1)} %copy-done.8, bf16[3,256,512]{2,1,0:T(8,128)(2,1)S(1)} %get-tuple-element.79.weighted_ref, ...), custom_call_target="tpu_custom_call" | custom-call | flops 2000000000 | bytes 4000000 | tf_op jit(solution)/shard_map/pallas_call | solution.py:477
  30.5 0.0 collective-permute-done.halo_ref
  30.6 0.0 collective-permute-done.1.bchalo_ref
  30.6 2.2 %shard_map.179 = (bf16[32,96,128]{2,1,0:T(8,128)(2,1)}, bf16[256,128]{1,0:T(8,128)(2,1)S(1)}, bf16[256,128]{1,0:T(8,128)(2,1)S(1)}, bf16[16,512]{1,0:T(8,128)(2,1)S(1)}) custom-call(s32[94]{0:T(128)S(1)} %get-tuple-element.73.meta_ref, bf16[256,512]{1,0:T(8,128)(2,1)S(1)} %copy-done.1, bf16[16,512]{1,0:T(8,128)(2,1)S(1)} %collective-permute-done.halo_ref, ...), custom_call_target="tpu_custom_call" | custom-call | flops 2000000000 | bytes 4000000 | tf_op jit(solution)/shard_map/pallas_call | solution.py:477
  32.8 10.5 %all-to-all-start.2 = ((bf16[32,96,128]{2,1,0:T(8,128)(2,1)}), bf16[32,96,128]{2,1,0:T(8,128)(2,1)}, u32[]{:S(2)}, u32[]{:S(2)}) async-start(bf16[32,96,128]{2,1,0:T(8,128)(2,1)} %get-tuple-element.92), calls=%async_computation.2 | async-start | bytes 1572864 | tf_op jit(solution)/shard_map/all_to_all | solution.py:598
  43.3 0.0 copy-done.15
  43.3 0.2 convert_reduce_fusion
  43.5 0.6 reduce_max.9
  44.8 17.4 %all-to-all-done.2.got_ref = bf16[32,96,128]{2,1,0:T(8,128)(2,1)} async-done(((bf16[32,96,128]{2,1,0:T(8,128)(2,1)}), bf16[32,96,128]{2,1,0:T(8,128)(2,1)}, u32[]{:S(2)}, u32[]{:S(2)}) %all-to-all-start.2) | async-done | bytes 786464 | tf_op jit(solution)/shard_map/all_to_all | solution.py:598
  62.2 2.3 %conditional.1 = (bf16[32,48,128]{2,1,0:T(8,128)(2,1)}) conditional(s32[]{:T(128)} %convert_element_type.37, (s32[94]{0:T(128)S(1)}, bf16[32,96,128]{2,1,0:T(8,128)(2,1)}) %tuple.15, (s32[]{:T(128)}, s32[8]{0:T(128)S(1)}, s32[8]{0:T(128)S(1)}, s32[8]{0:T(128)S(1)}, s32[8]{0:T(128)S(1)}, /*index=5*/f32[8,256]{1,0:T(8,128)S(1)}, ...), branch_computations={%region_2.3_spmd, %region_3.6_spmd} | conditional | flops 2207683328 | bytes 13670660 | solution.py:625
  62.2 2.3 %branch_0_fun.1 = bf16[32,48,128]{2,1,0:T(8,128)(2,1)} custom-call(s32[94]{0:T(128)S(1)} %get-tuple-element.15.meta_ref, bf16[32,96,128]{2,1,0:T(8,128)(2,1)} %get-tuple-element.32.got_ref), custom_call_target="tpu_custom_call" | custom-call | flops 2000000000 | bytes 4000000 | tf_op jit(solution)/shard_map/cond/branch_0_fun/pallas_call | solution.py:477
  64.5 8.8 %all-to-all-start.3 = ((bf16[32,48,128]{2,1,0:T(8,128)(2,1)}), bf16[32,48,128]{2,1,0:T(8,128)(2,1)S(1)}, u32[]{:S(2)}, u32[]{:S(2)}) async-start(bf16[32,48,128]{2,1,0:T(8,128)(2,1)} %get-tuple-element.140), calls=%async_computation.3 | async-start | bytes 786432 | tf_op jit(solution)/shard_map/all_to_all | solution.py:626
  73.3 0.0 copy-done.14
  73.3 0.1 broadcast_in_dim.96
  73.4 0.1 broadcast_in_dim_reshape.3.skip_ref
  73.4 0.0 copy-done.2
  73.5 1.1 %shard_map.180 = (f32[256,512]{1,0:T(8,128)S(1)}, f32[256,512]{1,0:T(8,128)S(1)}) custom-call(bf16[256,512]{1,0:T(8,128)(2,1)S(1)} %get-tuple-element.74.xc_ref, bf16[16,512]{1,0:T(8,128)(2,1)S(1)} %get-tuple-element.85.xfirst_ref, bf16[256,128]{1,0:T(8,128)(2,1)S(1)} %get-tuple-element.86.b_ref, bf16[256,128]{1,0:T(8,128)(2,1)S(1)} %get-tuple-element.87.c_ref, ...), custom_call_target="tpu_custom_call" | custom-call | flops 2000000000 | bytes 4000000 | tf_op jit(solution)/shard_map/pallas_call | solution.py:477
  74.6 0.0 copy-done.3
  74.6 0.0 copy-done.4
  74.6 0.0 copy-done.6
  74.6 3.5 %shard_map.181 = (f32[256,512]{1,0:T(8,128)S(1)}, bf16[256,128]{1,0:T(8,128)(2,1)S(1)}, f32[256,512]{1,0:T(8,128)S(1)}) custom-call(s32[94]{0:T(128)S(1)} %get-tuple-element.73.meta_ref, bf16[256,512]{1,0:T(8,128)(2,1)S(1)} %copy-done.3, bf16[256,512]{1,0:T(8,128)(2,1)S(1)} %bitcast.29, bf16[32,96,128]{2,1,0:T(8,128)(2,1)} %all-to-all-done.2.got_ref, ...), custom_call_target="tpu_custom_call" | custom-call | flops 2000000000 | bytes 4000000 | tf_op jit(solution)/shard_map/pallas_call | solution.py:477
  78.1 6.0 %all-to-all-done.3.back_ref = bf16[32,48,128]{2,1,0:T(8,128)(2,1)S(1)} async-done(((bf16[32,48,128]{2,1,0:T(8,128)(2,1)}), bf16[32,48,128]{2,1,0:T(8,128)(2,1)S(1)}, u32[]{:S(2)}, u32[]{:S(2)}) %all-to-all-start.3) | async-done | bytes 393248 | tf_op jit(solution)/shard_map/all_to_all | solution.py:626
  84.1 1.5 %shard_map.182 = (f32[256,512]{1,0:T(8,128)S(1)}, f32[256,512]{1,0:T(8,128)S(1)}, f32[16,8,128]{2,1,0:T(8,128)S(1)}) custom-call(s32[94]{0:T(128)S(1)} %get-tuple-element.73.meta_ref, f32[256,512]{1,0:T(8,128)S(1)} %get-tuple-element.90.y_ref, f32[256,512]{1,0:T(8,128)S(1)} %get-tuple-element.91.scale_ref, bf16[256,128]{1,0:T(8,128)(2,1)S(1)} %get-tuple-element.87.c_ref, ...), custom_call_target="tpu_custom_call" | custom-call | flops 2000000000 | bytes 4000000 | tf_op jit(solution)/shard_map/pallas_call | solution.py:477
  85.6 15.7 %all_to_all.25.sq_ref = f32[16,8,128]{2,1,0:T(8,128)S(1)} all-to-all(f32[16,8,128]{2,1,0:T(8,128)S(1)} %get-tuple-element.96), channel_id=1, replica_groups=mesh['ctx'=32,'tp'=16] {'tp'}, dimensions={0} | all-to-all | bytes 131072 | tf_op jit(solution)/shard_map/all_to_all | solution.py:642
  101.3 0.0 copy-done.9
  101.3 1.6 %shard_map.183 = (bf16[256,512]{1,0:T(8,128)(2,1)}, bf16[256,512]{1,0:T(8,128)(2,1)}) custom-call(s32[94]{0:T(128)S(1)} %get-tuple-element.73.meta_ref, f32[16,8,128]{2,1,0:T(8,128)S(1)} %all_to_all.25.sq_ref, f32[256,512]{1,0:T(8,128)S(1)} %get-tuple-element.97.g_ref, f32[256,512]{1,0:T(8,128)S(1)} %get-tuple-element.98.bg_ref, f32[1,512]{1,0:T(1,128)S(1)} %bitcast.30), custom_call_target="tpu_custom_call" | custom-call | flops 2000000000 | bytes 4000000 | tf_op jit(solution)/shard_map/pallas_call | solution.py:477
  (15 shorter events, 0.0 us)
Async XLA Ops:
  2.1 23.5 %all-to-all-start.1 = ((bf16[16,16,512]{2,1,0:T(8,128)(2,1)}), bf16[16,16,512]{2,1,0:T(8,128)(2,1)S(1)}, u32[]{:S(2)}, u32[]{:S(2)}) async-start(bf16[16,16,512]{2,1,0:T(8,128)(2,1)} %broadcast_in_dim.95), calls=%async_computation.1 | async-start | bytes 524288 | tf_op jit(solution)/shard_map/all_to_all | solution.py:536
  13.9 0.9 copy-start
  14.9 0.7 copy-start.10
  15.5 0.7 copy-start.11
  16.2 0.7 copy-start.12
  16.8 5.6 %copy-start.13 = (f32[8]{0:T(128)S(1)}, f32[8]{0:T(128)}, u32[]{:S(2)}) copy-start(f32[8]{0:T(128)} %param.29) | copy-start | bytes 100
  16.8 5.7 %copy-start.1 = (bf16[256,512]{1,0:T(8,128)(2,1)S(1)}, bf16[256,512]{1,0:T(8,128)(2,1)}, u32[]{:S(2)}) copy-start(bf16[256,512]{1,0:T(8,128)(2,1)} %x_ref.6) | copy-start | bytes 786436
  16.8 5.7 %copy-start.5 = (f32[8,256]{1,0:T(8,128)S(1)}, f32[8,256]{1,0:T(8,128)}, u32[]{:S(2)}) copy-start(f32[8,256]{1,0:T(8,128)} %dt_ref.2) | copy-start | bytes 24580
  16.8 5.7 %copy-start.7 = (bf16[4,512]{1,0:T(4,128)(2,1)S(1)}, bf16[4,512]{1,0:T(4,128)(2,1)}, u32[]{:S(2)}) copy-start(bf16[4,512]{1,0:T(4,128)(2,1)} %xtaps_ref.3) | copy-start | bytes 12292
  19.2 11.4 %collective-permute-start = (bf16[16,512]{1,0:T(8,128)(2,1)S(1)}, bf16[16,512]{1,0:T(8,128)(2,1)S(1)}, u32[]{:S(2)}, u32[]{:S(2)}) collective-permute-start(bf16[16,512]{1,0:T(8,128)(2,1)S(1)} %get-tuple-element.75), channel_id=1, source_target_pairs={{0,16},{16,32},{32,48},{48,64},{64,80},{80,96},{96,112},{112,128},... | collective-permute-start | bytes 49160 | tf_op jit(solution)/shard_map/ppermute | solution.py:558
  22.5 6.3 %copy-start.8 = (bf16[4,256]{1,0:T(4,128)(2,1)S(1)}, bf16[4,256]{1,0:T(4,128)(2,1)}, u32[]{:S(2)}) copy-start(bf16[4,256]{1,0:T(4,128)(2,1)} %taps_ref.7) | copy-start | bytes 6148
  25.6 4.9 %collective-permute-start.1 = (bf16[16,256]{1,0:T(8,128)(2,1)S(1)}, bf16[16,256]{1,0:T(8,128)(2,1)S(1)}, u32[]{:S(2)}, u32[]{:S(2)}) collective-permute-start(bf16[16,256]{1,0:T(8,128)(2,1)S(1)} %slice.9), channel_id=1, source_target_pairs={{0,16},{16,32},{32,48},{48,64},{64,80},{80,96},{96,112},{112,128},... | collective-permute-start | bytes 24584 | tf_op jit(solution)/shard_map/ppermute | solution.py:574
  32.8 10.5 %copy-start.15 = (s32[8]{0:T(128)S(1)}, s32[8]{0:T(128)}, u32[]{:S(2)}) copy-start(s32[8]{0:T(128)} %bound_ref.1) | copy-start | bytes 100
  32.8 29.4 %all-to-all-start.2 = ((bf16[32,96,128]{2,1,0:T(8,128)(2,1)}), bf16[32,96,128]{2,1,0:T(8,128)(2,1)}, u32[]{:S(2)}, u32[]{:S(2)}) async-start(bf16[32,96,128]{2,1,0:T(8,128)(2,1)} %get-tuple-element.92), calls=%async_computation.2 | async-start | bytes 1572864 | tf_op jit(solution)/shard_map/all_to_all | solution.py:598
  62.2 11.1 %copy-start.14 = (f32[8]{0:T(128)S(1)}, f32[8]{0:T(128)}, u32[]{:S(2)}) copy-start(f32[8]{0:T(128)} %param.30) | copy-start | bytes 100
  62.2 11.3 %copy-start.2 = (bf16[256,512]{1,0:T(8,128)(2,1)S(1)}, bf16[256,512]{1,0:T(8,128)(2,1)}, u32[]{:S(2)}) copy-start(bf16[256,512]{1,0:T(8,128)(2,1)} %z_ref.2) | copy-start | bytes 786436
  64.5 19.6 %all-to-all-start.3 = ((bf16[32,48,128]{2,1,0:T(8,128)(2,1)}), bf16[32,48,128]{2,1,0:T(8,128)(2,1)S(1)}, u32[]{:S(2)}, u32[]{:S(2)}) async-start(bf16[32,48,128]{2,1,0:T(8,128)(2,1)} %get-tuple-element.140), calls=%async_computation.3 | async-start | bytes 786432 | tf_op jit(solution)/shard_map/all_to_all | solution.py:626
  73.4 1.1 %copy-start.3 = (bf16[256,512]{1,0:T(8,128)(2,1)S(1)}, bf16[256,512]{1,0:T(8,128)(2,1)}, u32[]{:S(2)}) copy-start(bf16[256,512]{1,0:T(8,128)(2,1)} %x_ref.7) | copy-start | bytes 786436
  73.5 1.1 %copy-start.4 = (bf16[256,512]{1,0:T(8,128)(2,1)S(1)}, bf16[256,512]{1,0:T(8,128)(2,1)}, u32[]{:S(2)}) copy-start(bf16[256,512]{1,0:T(8,128)(2,1)} %z_ref.3) | copy-start | bytes 786436
  73.5 1.1 %copy-start.6 = (f32[8,256]{1,0:T(8,128)S(1)}, f32[8,256]{1,0:T(8,128)}, u32[]{:S(2)}) copy-start(f32[8,256]{1,0:T(8,128)} %dt_ref.3) | copy-start | bytes 24580
  84.1 17.2 %copy-start.9 = (f32[512]{0:T(512)S(1)}, f32[512]{0:T(512)}, u32[]{:S(2)}) copy-start(f32[512]{0:T(512)} %param.31) | copy-start | bytes 6148

commit v8 on v7

--- a/solution.py
+++ b/solution.py
@@ -243,7 +243,7 @@
 
 
 def prefix_state_kernel(
-    meta_ref, x_ref, halo_ref, xtaps_ref, bc_ref, bchalo_ref, taps_ref, first_ref, part_ref, misc_ref, conv_ref,
+    meta_ref, x_ref, halo_ref, xtaps_ref, bc_ref, taps_ref, first_ref, part_ref, misc_ref, conv_ref,
     sent_ref, b_ref, c_ref, xfirst_ref, ext_ref, edge_ref, *, base,
 ):
     channels = x_ref.shape[1]
@@ -251,7 +251,7 @@
     n_state = width // 2
     n_ctx, misc, _ = misc_ref.shape
     rows = channels // n_ctx
-    ext_ref[:HALO] = bchalo_ref[...].astype(F32)
+    ext_ref[:HALO] = halo_ref[:, channels:].astype(F32)
     ext_ref[HALO:] = bc_ref[:HALO, :width].astype(F32)
     convolved = convolve(ext_ref, taps_ref, HALO, HALO)
     b_rows = convolved[:, :n_state]
@@ -259,7 +259,7 @@
     b_ref[HALO:] = conv_ref[HALO:, :n_state]
     c_ref[:HALO] = convolved[:, n_state:]
     c_ref[HALO:] = conv_ref[HALO:, n_state:]
-    edge_ref[:HALO] = halo_ref[...].astype(F32)
+    edge_ref[:HALO] = halo_ref[:, :channels].astype(F32)
     edge_ref[HALO:] = x_ref[:HALO].astype(F32)
     xfirst = convolve(edge_ref, xtaps_ref, HALO, HALO)
     xfirst_ref[...] = xfirst
@@ -555,7 +555,6 @@
         smem=5,
         smem_out=True,
     )
-    halo = lax.ppermute(last, "ctx", onward)
     xc, cumulative, step, weighted, first, logs = call(
         functools.partial(prefix_x_kernel, base=at_positions),
         [
@@ -570,8 +569,10 @@
         [meta, prefix_x, prefix_dt, rates, conv_x],
         smem=1,
     )
-    gathered, weighted = lax.optimization_barrier((gathered, weighted))
-    bc_halo = lax.ppermute(gathered[length - HALO :, :width], "ctx", onward)
+    gathered, weighted, last = lax.optimization_barrier((gathered, weighted, last))
+    halo = lax.ppermute(
+        jnp.concatenate([last, gathered[length - HALO :, :width]], axis=1), "ctx", onward
+    )
     part, misc, convolved = call(
         functools.partial(prefix_later_kernel, base=at_positions, tail_base=at_tails),
         [
@@ -592,7 +593,7 @@
             ((HALO, channels), BF),
         ],
         [((2 * HALO, width), F32), ((2 * HALO, channels), F32)],
-        [meta, prefix_x, halo, conv_x, gathered, bc_halo, conv_bc, first, part, misc, convolved],
+        [meta, prefix_x, halo, conv_x, gathered, conv_bc, first, part, misc, convolved],
         smem=1,
     )
     got = lax.all_to_all(sent, "ctx", 0, 0, tiled=True)

time: 104 us -> 103 us (level)
  waiting for transfers between devices: 23.8 us -> 26.9 us
  starting transfers between devices: 37.5 us -> 35.2 us
    ppermute x2 -> x1, starting transfers between devices: 6.42 us -> 3.19 us  [body(): lax.ppermute(jnp.concatenate([last, gathered[length - HALO:, :width]], ax...]
    all_to_all x1, waiting for transfers between devices: 0.4 us -> 3.5 us  [body(): lax.all_to_all(spread, 'tp', 0, 0, tiled=True).reshape(length, 2 * width)]
    unnamed x32 -> x30, local copies, waits for them, and re-layouts: 2.95 us -> 2.96 us
  transfers between devices with their start and end apart: 5 -> 4, of which waited for: 3 -> 3; matrix products, arithmetic and copies ran while one was open for 1% -> 2% of each run, Pallas kernels for 11% -> 10%
where the time goes in v8:
time: 103 us; the launch traced here: 102 us
  starting transfers between devices  35.2 us (34%)
  waiting for transfers between devices  26.9 us (26%)
  Pallas kernels  17.9 us (17%)
  blocking collectives  14.9 us (14%)
  local copies, waits for them, and re-layouts  4.57 us (4%)
  other arithmetic  1.55 us (2%)
  between operations  1.45 us (1%)
    pallas_call x9, Pallas kernels, call(): pl.pallas_call(kernel, grid=(1,) if grid else (), in_specs=[where(i < sme...  17.9 us
    all_to_all x1, waiting for transfers between devices, body(): got = lax.all_to_all(sent, 'ctx', 0, 0, tiled=True)  17.4 us
    all_to_all x1, blocking collectives, body(): squares = lax.all_to_all(squares, 'tp', 0, 0, tiled=True)  14.9 us
    all_to_all x1, starting transfers between devices, body(): lax.all_to_all(spread, 'tp', 0, 0, tiled=True).reshape(length, 2 * width)  11.8 us
    all_to_all x1, starting transfers between devices, body(): got = lax.all_to_all(sent, 'ctx', 0, 0, tiled=True)  11.3 us
    all_to_all x1, starting transfers between devices, body(): back = lax.all_to_all(back, 'ctx', 0, 0, tiled=True)  8.81 us
    all_to_all x1, waiting for transfers between devices, body(): back = lax.all_to_all(back, 'ctx', 0, 0, tiled=True)  6.02 us
    all_to_all x1, waiting for transfers between devices, body(): lax.all_to_all(spread, 'tp', 0, 0, tiled=True).reshape(length, 2 * width)  3.5 us
  transfers between devices with their start and end apart: 4, of which 3 were waited for; matrix products, arithmetic and copies ran while one was open for 2% of the time, Pallas kernels for 10%

profile of v8, /device:TPU:1, one launch (start us, length us, event | category | flops | bytes accessed | tf_op | source)
XLA Modules:
  0.0 102.4 jit_solution(730384758774650085)
XLA Ops:
  0.6 0.7 pad_maximum_fusion.3
  1.3 0.7 broadcast_in_dim.95
  2.1 11.8 %all-to-all-start.1 = ((bf16[16,16,512]{2,1,0:T(8,128)(2,1)}), bf16[16,16,512]{2,1,0:T(8,128)(2,1)S(1)}, u32[]{:S(2)}, u32[]{:S(2)}) async-start(bf16[16,16,512]{2,1,0:T(8,128)(2,1)} %broadcast_in_dim.95), calls=%async_computation.1 | async-start | bytes 524288 | tf_op jit(solution)/shard_map/all_to_all | solution.py:536
  13.9 0.7 copy.34.rate_ref
  14.6 0.0 copy-start
  14.6 0.9 copy-done
  15.6 0.0 copy-start.10
  15.6 0.7 copy-done.10
  16.2 0.0 copy-start.11
  16.2 0.7 copy-done.11
  16.9 0.0 copy-start.12
  16.9 0.7 copy-done.12
  17.6 0.0 copy-start.1
  17.6 0.0 copy-start.5
  17.6 2.3 %shard_map.176 = (s32[94]{0:T(128)S(1)}, bf16[32,32,128]{2,1,0:T(8,128)(2,1)S(1)}, bf16[16,512]{1,0:T(8,128)(2,1)S(1)}) custom-call(s32[1]{0:T(128)} %bitcast.11.me_ref, s32[8]{0:T(128)} %bound_ref.1, s32[64]{0:T(128)S(1)} %copy-done.10, s32[64]{0:T(128)S(1)} %copy-done.11, s32[64]{0:T(128)S(1)} %copy-done.12, bf16[256,512]{1,0:T(8,128)(2,1)S(1)} %copy-done), custom_call_target="tpu_custom_call" | custom-call | flops 2000000000 | bytes 4000000 | tf_op jit(solution)/shard_map/pallas_call | solution.py:477
  19.9 0.0 copy-done.1
  19.9 0.0 copy-done.5
  19.9 0.0 copy-done.7
  19.9 0.0 copy-start.8
  19.9 2.2 %shard_map.177 = (bf16[256,512]{1,0:T(8,128)(2,1)S(1)}, f32[8,256]{1,0:T(8,128)S(1)}, f32[8,256]{1,0:T(8,128)S(1)}, bf16[3,256,512]{2,1,0:T(8,128)(2,1)S(1)}, f3...) custom-call(s32[94]{0:T(128)S(1)} %get-tuple-element.74.meta_ref, bf16[256,512]{1,0:T(8,128)(2,1)S(1)} %copy-done.1, ...), custom_call_target="tpu_custom_call" | custom-call | flops 2000000000 | bytes 4000000 | tf_op jit(solution)/shard_map/pallas_call | solution.py:477
  22.1 3.5 %all-to-all-done.1 = bf16[16,16,512]{2,1,0:T(8,128)(2,1)S(1)} async-done(((bf16[16,16,512]{2,1,0:T(8,128)(2,1)}), bf16[16,16,512]{2,1,0:T(8,128)(2,1)S(1)}, u32[]{:S(2)}, u32[]{:S(2)}) %all-to-all-start.1) | async-done | bytes 262176 | tf_op jit(solution)/shard_map/all_to_all | solution.py:536
  25.6 3.2 %collective-permute-start = (bf16[16,768]{1,0:T(8,128)(2,1)S(1)}, bf16[16,768]{1,0:T(8,128)(2,1)S(1)}, u32[]{:S(2)}, u32[]{:S(2)}) collective-permute-start(bf16[16,768]{1,0:T(8,128)(2,1)S(1)} %pad_maximum_fusion.2), channel_id=1, source_target_pairs={{0,16},{16,32},{32,48},{48,64},{64,80},{80,96},{96,112},{112,128},... | collective-permute-start | bytes 73736 | tf_op jit(solution)/shard_map/ppermute | solution.py:573
  28.8 0.0 copy-done.8
  28.8 1.4 %shard_map.178 = (f32[3,512,128]{2,1,0:T(8,128)S(1)}, bf16[32,48,128]{2,1,0:T(8,128)(2,1)S(1)}, bf16[256,256]{1,0:T(8,128)(2,1)S(1)}) custom-call(s32[94]{0:T(128)S(1)} %get-tuple-element.74.meta_ref, bf16[256,512]{1,0:T(8,128)(2,1)S(1)} %bitcast.27, bf16[4,256]{1,0:T(4,128)(2,1)S(1)} %copy-done.8, bf16[3,256,512]{2,1,0:T(8,128)(2,1)S(1)} %get-tuple-element.81.weighted_ref, ...), custom_call_target="tpu_custom_call" | custom-call | flops 2000000000 | bytes 4000000 | tf_op jit(solution)/shard_map/pallas_call | solution.py:477
  30.3 0.0 collective-permute-done.halo_ref
  30.3 2.0 %shard_map.179 = (bf16[32,96,128]{2,1,0:T(8,128)(2,1)}, bf16[256,128]{1,0:T(8,128)(2,1)S(1)}, bf16[256,128]{1,0:T(8,128)(2,1)S(1)}, bf16[16,512]{1,0:T(8,128)(2,1)S(1)}) custom-call(s32[94]{0:T(128)S(1)} %get-tuple-element.74.meta_ref, bf16[256,512]{1,0:T(8,128)(2,1)S(1)} %copy-done.1, bf16[16,768]{1,0:T(8,128)(2,1)S(1)} %collective-permute-done.halo_ref, ...), custom_call_target="tpu_custom_call" | custom-call | flops 2000000000 | bytes 4000000 | tf_op jit(solution)/shard_map/pallas_call | solution.py:477
  32.3 11.3 %all-to-all-start.2 = ((bf16[32,96,128]{2,1,0:T(8,128)(2,1)}), bf16[32,96,128]{2,1,0:T(8,128)(2,1)}, u32[]{:S(2)}, u32[]{:S(2)}) async-start(bf16[32,96,128]{2,1,0:T(8,128)(2,1)} %get-tuple-element.94), calls=%async_computation.2 | async-start | bytes 1572864 | tf_op jit(solution)/shard_map/all_to_all | solution.py:599
  43.6 0.0 copy-done.14
  43.7 0.2 convert_reduce_fusion
  43.8 0.6 reduce_max.9
  45.1 17.4 %all-to-all-done.2.got_ref = bf16[32,96,128]{2,1,0:T(8,128)(2,1)} async-done(((bf16[32,96,128]{2,1,0:T(8,128)(2,1)}), bf16[32,96,128]{2,1,0:T(8,128)(2,1)}, u32[]{:S(2)}, u32[]{:S(2)}) %all-to-all-start.2) | async-done | bytes 786464 | tf_op jit(solution)/shard_map/all_to_all | solution.py:599
  62.5 2.3 %conditional.1 = (bf16[32,48,128]{2,1,0:T(8,128)(2,1)}) conditional(s32[]{:T(128)} %convert_element_type.37, (s32[94]{0:T(128)S(1)}, bf16[32,96,128]{2,1,0:T(8,128)(2,1)}) %tuple.15, (s32[]{:T(128)}, s32[8]{0:T(128)S(1)}, s32[8]{0:T(128)S(1)}, s32[8]{0:T(128)S(1)}, s32[8]{0:T(128)S(1)}, /*index=5*/f32[8,256]{1,0:T(8,128)S(1)}, ...), branch_computations={%region_2.3_spmd, %region_3.6_spmd} | conditional | flops 2207683328 | bytes 13670660 | solution.py:626
  62.5 2.3 %branch_0_fun.1 = bf16[32,48,128]{2,1,0:T(8,128)(2,1)} custom-call(s32[94]{0:T(128)S(1)} %get-tuple-element.15.meta_ref, bf16[32,96,128]{2,1,0:T(8,128)(2,1)} %get-tuple-element.32.got_ref), custom_call_target="tpu_custom_call" | custom-call | flops 2000000000 | bytes 4000000 | tf_op jit(solution)/shard_map/cond/branch_0_fun/pallas_call | solution.py:477
  64.8 8.8 %all-to-all-start.3 = ((bf16[32,48,128]{2,1,0:T(8,128)(2,1)}), bf16[32,48,128]{2,1,0:T(8,128)(2,1)S(1)}, u32[]{:S(2)}, u32[]{:S(2)}) async-start(bf16[32,48,128]{2,1,0:T(8,128)(2,1)} %get-tuple-element.142), calls=%async_computation.3 | async-start | bytes 786432 | tf_op jit(solution)/shard_map/all_to_all | solution.py:627
  73.6 0.0 copy-done.13
  73.6 0.1 broadcast_in_dim.96
  73.7 0.1 broadcast_in_dim_reshape.3.skip_ref
  73.8 0.0 copy-done.2
  73.8 1.1 %shard_map.180 = (f32[256,512]{1,0:T(8,128)S(1)}, f32[256,512]{1,0:T(8,128)S(1)}) custom-call(bf16[256,512]{1,0:T(8,128)(2,1)S(1)} %get-tuple-element.75.xc_ref, bf16[16,512]{1,0:T(8,128)(2,1)S(1)} %get-tuple-element.87.xfirst_ref, bf16[256,128]{1,0:T(8,128)(2,1)S(1)} %get-tuple-element.88.b_ref, bf16[256,128]{1,0:T(8,128)(2,1)S(1)} %get-tuple-element.89.c_ref, ...), custom_call_target="tpu_custom_call" | custom-call | flops 2000000000 | bytes 4000000 | tf_op jit(solution)/shard_map/pallas_call | solution.py:477
  74.9 0.0 copy-done.3
  74.9 0.0 copy-done.4
  74.9 0.0 copy-done.6
  74.9 3.5 %shard_map.181 = (f32[256,512]{1,0:T(8,128)S(1)}, bf16[256,128]{1,0:T(8,128)(2,1)S(1)}, f32[256,512]{1,0:T(8,128)S(1)}) custom-call(s32[94]{0:T(128)S(1)} %get-tuple-element.74.meta_ref, bf16[256,512]{1,0:T(8,128)(2,1)S(1)} %copy-done.3, bf16[256,512]{1,0:T(8,128)(2,1)S(1)} %bitcast.29, bf16[32,96,128]{2,1,0:T(8,128)(2,1)} %all-to-all-done.2.got_ref, ...), custom_call_target="tpu_custom_call" | custom-call | flops 2000000000 | bytes 4000000 | tf_op jit(solution)/shard_map/pallas_call | solution.py:477
  78.4 6.0 %all-to-all-done.3.back_ref = bf16[32,48,128]{2,1,0:T(8,128)(2,1)S(1)} async-done(((bf16[32,48,128]{2,1,0:T(8,128)(2,1)}), bf16[32,48,128]{2,1,0:T(8,128)(2,1)S(1)}, u32[]{:S(2)}, u32[]{:S(2)}) %all-to-all-start.3) | async-done | bytes 393248 | tf_op jit(solution)/shard_map/all_to_all | solution.py:627
  84.4 1.5 %shard_map.182 = (f32[256,512]{1,0:T(8,128)S(1)}, f32[256,512]{1,0:T(8,128)S(1)}, f32[16,8,128]{2,1,0:T(8,128)S(1)}) custom-call(s32[94]{0:T(128)S(1)} %get-tuple-element.74.meta_ref, f32[256,512]{1,0:T(8,128)S(1)} %get-tuple-element.92.y_ref, f32[256,512]{1,0:T(8,128)S(1)} %get-tuple-element.93.scale_ref, bf16[256,128]{1,0:T(8,128)(2,1)S(1)} %get-tuple-element.89.c_ref, ...), custom_call_target="tpu_custom_call" | custom-call | flops 2000000000 | bytes 4000000 | tf_op jit(solution)/shard_map/pallas_call | solution.py:477
  85.9 14.9 %all_to_all.25.sq_ref = f32[16,8,128]{2,1,0:T(8,128)S(1)} all-to-all(f32[16,8,128]{2,1,0:T(8,128)S(1)} %get-tuple-element.98), channel_id=1, replica_groups=mesh['ctx'=32,'tp'=16] {'tp'}, dimensions={0} | all-to-all | bytes 131072 | tf_op jit(solution)/shard_map/all_to_all | solution.py:643
  100.8 0.0 copy-done.9
  100.8 1.6 %shard_map.183 = (bf16[256,512]{1,0:T(8,128)(2,1)}, bf16[256,512]{1,0:T(8,128)(2,1)}) custom-call(s32[94]{0:T(128)S(1)} %get-tuple-element.74.meta_ref, f32[16,8,128]{2,1,0:T(8,128)S(1)} %all_to_all.25.sq_ref, f32[256,512]{1,0:T(8,128)S(1)} %get-tuple-element.99.g_ref, f32[256,512]{1,0:T(8,128)S(1)} %get-tuple-element.100.bg_ref, f32[1,512]{1,0:T(1,128)S(1)} %bitcast.30), custom_call_target="tpu_custom_call" | custom-call | flops 2000000000 | bytes 4000000 | tf_op jit(solution)/shard_map/pallas_call | solution.py:477
  (12 shorter events, 0.0 us)
Async XLA Ops:
  2.1 23.5 %all-to-all-start.1 = ((bf16[16,16,512]{2,1,0:T(8,128)(2,1)}), bf16[16,16,512]{2,1,0:T(8,128)(2,1)S(1)}, u32[]{:S(2)}, u32[]{:S(2)}) async-start(bf16[16,16,512]{2,1,0:T(8,128)(2,1)} %broadcast_in_dim.95), calls=%async_computation.1 | async-start | bytes 524288 | tf_op jit(solution)/shard_map/all_to_all | solution.py:536
  14.6 0.9 copy-start
  15.6 0.7 copy-start.10
  16.2 0.7 copy-start.11
  16.9 0.7 copy-start.12
  17.6 2.3 %copy-start.1 = (bf16[256,512]{1,0:T(8,128)(2,1)S(1)}, bf16[256,512]{1,0:T(8,128)(2,1)}, u32[]{:S(2)}) copy-start(bf16[256,512]{1,0:T(8,128)(2,1)} %x_ref.6) | copy-start | bytes 786436
  17.6 2.4 %copy-start.5 = (f32[8,256]{1,0:T(8,128)S(1)}, f32[8,256]{1,0:T(8,128)}, u32[]{:S(2)}) copy-start(f32[8,256]{1,0:T(8,128)} %dt_ref.2) | copy-start | bytes 24580
  17.6 2.4 %copy-start.7 = (bf16[4,512]{1,0:T(4,128)(2,1)S(1)}, bf16[4,512]{1,0:T(4,128)(2,1)}, u32[]{:S(2)}) copy-start(bf16[4,512]{1,0:T(4,128)(2,1)} %xtaps_ref.3) | copy-start | bytes 12292
  19.9 8.9 %copy-start.8 = (bf16[4,256]{1,0:T(4,128)(2,1)S(1)}, bf16[4,256]{1,0:T(4,128)(2,1)}, u32[]{:S(2)}) copy-start(bf16[4,256]{1,0:T(4,128)(2,1)} %taps_ref.7) | copy-start | bytes 6148
  25.6 4.7 %collective-permute-start = (bf16[16,768]{1,0:T(8,128)(2,1)S(1)}, bf16[16,768]{1,0:T(8,128)(2,1)S(1)}, u32[]{:S(2)}, u32[]{:S(2)}) collective-permute-start(bf16[16,768]{1,0:T(8,128)(2,1)S(1)} %pad_maximum_fusion.2), channel_id=1, source_target_pairs={{0,16},{16,32},{32,48},{48,64},{64,80},{80,96},{96,112},{112,128},... | collective-permute-start | bytes 73736 | tf_op jit(solution)/shard_map/ppermute | solution.py:573
  32.3 11.3 %copy-start.14 = (s32[8]{0:T(128)S(1)}, s32[8]{0:T(128)}, u32[]{:S(2)}) copy-start(s32[8]{0:T(128)} %bound_ref.1) | copy-start | bytes 100
  32.3 30.2 %all-to-all-start.2 = ((bf16[32,96,128]{2,1,0:T(8,128)(2,1)}), bf16[32,96,128]{2,1,0:T(8,128)(2,1)}, u32[]{:S(2)}, u32[]{:S(2)}) async-start(bf16[32,96,128]{2,1,0:T(8,128)(2,1)} %get-tuple-element.94), calls=%async_computation.2 | async-start | bytes 1572864 | tf_op jit(solution)/shard_map/all_to_all | solution.py:599
  62.5 11.1 %copy-start.13 = (f32[8]{0:T(128)S(1)}, f32[8]{0:T(128)}, u32[]{:S(2)}) copy-start(f32[8]{0:T(128)} %param.30) | copy-start | bytes 100
  62.5 11.3 %copy-start.2 = (bf16[256,512]{1,0:T(8,128)(2,1)S(1)}, bf16[256,512]{1,0:T(8,128)(2,1)}, u32[]{:S(2)}) copy-start(bf16[256,512]{1,0:T(8,128)(2,1)} %z_ref.2) | copy-start | bytes 786436
  64.8 19.6 %all-to-all-start.3 = ((bf16[32,48,128]{2,1,0:T(8,128)(2,1)}), bf16[32,48,128]{2,1,0:T(8,128)(2,1)S(1)}, u32[]{:S(2)}, u32[]{:S(2)}) async-start(bf16[32,48,128]{2,1,0:T(8,128)(2,1)} %get-tuple-element.142), calls=%async_computation.3 | async-start | bytes 786432 | tf_op jit(solution)/shard_map/all_to_all | solution.py:627
  73.8 1.1 %copy-start.3 = (bf16[256,512]{1,0:T(8,128)(2,1)S(1)}, bf16[256,512]{1,0:T(8,128)(2,1)}, u32[]{:S(2)}) copy-start(bf16[256,512]{1,0:T(8,128)(2,1)} %x_ref.7) | copy-start | bytes 786436
  73.8 1.1 %copy-start.4 = (bf16[256,512]{1,0:T(8,128)(2,1)S(1)}, bf16[256,512]{1,0:T(8,128)(2,1)}, u32[]{:S(2)}) copy-start(bf16[256,512]{1,0:T(8,128)(2,1)} %z_ref.3) | copy-start | bytes 786436
  73.8 1.1 %copy-start.6 = (f32[8,256]{1,0:T(8,128)S(1)}, f32[8,256]{1,0:T(8,128)}, u32[]{:S(2)}) copy-start(f32[8,256]{1,0:T(8,128)} %dt_ref.3) | copy-start | bytes 24580
  84.4 16.4 %copy-start.9 = (f32[512]{0:T(512)S(1)}, f32[512]{0:T(512)}, u32[]{:S(2)}) copy-start(f32[512]{0:T(512)} %param.31) | copy-start | bytes 6148

commit v9 on v8

--- a/solution.py
+++ b/solution.py
@@ -301,38 +301,38 @@
 
 def scan_kernel(meta_ref, got_ref, *rest, n_branch, bounds):
     extra_ref = rest[0] if len(rest) == 5 else None
-    back_ref, entering_ref, bound_ref, log_ref = rest[-4:]
+    back_ref, entering_ref, bound_ref, decay_ref = rest[-4:]
     n_ctx, sent_rows, n_state = got_ref.shape
     rows = entering_ref.shape[1]
     misc = sent_rows - (1 + SLOTS) * rows
     parts = got_ref[:, misc - 16 : misc, :].astype(F32)[:, LOGS, :]
     for v in range(1 + SLOTS):
         log = parts[:, 3 * v : 3 * v + 1] + parts[:, 3 * v + 1 : 3 * v + 2] + parts[:, 3 * v + 2 : 3 * v + 3]
-        log_ref[v] = jnp.broadcast_to(log, (n_ctx, n_state))
+        decay_ref[v] = jnp.broadcast_to(jnp.exp(log), (n_ctx, n_state))
     state = jnp.zeros((rows, n_state), F32)
     for i in range(n_ctx):
         entering_ref[i] = state
         back_ref[i, :rows, :] = state.astype(BF)
         if i < n_ctx - 1:
             local = got_ref[i, misc : misc + rows, :].astype(F32)
-            state = jnp.exp(log_ref[0, i : i + 1]) * state + local
+            state = decay_ref[0, i : i + 1] * state + local
     for j in range(bounds):
         block = meta_ref[n_branch + j]
         slot = meta_ref[n_branch + bounds + j]
-        log = log_ref[1, pl.ds(block, 1)]
+        log = decay_ref[1, pl.ds(block, 1)]
         part = got_ref[block, misc + rows : misc + 2 * rows, :].astype(F32)
         for other in range(1, SLOTS):
             first = misc + (1 + other) * rows
-            log = jnp.where(slot == other, log_ref[1 + other, pl.ds(block, 1)], log)
+            log = jnp.where(slot == other, decay_ref[1 + other, pl.ds(block, 1)], log)
             part = jnp.where(slot == other, got_ref[block, first : first + rows, :].astype(F32), part)
         if extra_ref is not None:
             tail = extra_ref[block, (bounds - SLOTS) * rows :, :].astype(F32)
             for more in range(bounds - SLOTS):
                 here = slot == SLOTS + more
                 three = tail[3 * more : 3 * more + 1] + tail[3 * more + 1 : 3 * more + 2] + tail[3 * more + 2 : 3 * more + 3]
-                log = jnp.where(here, three, log)
+                log = jnp.where(here, jnp.exp(three), log)
                 part = jnp.where(here, extra_ref[block, more * rows : (more + 1) * rows, :].astype(F32), part)
-        bound_ref[j] = jnp.exp(log) * entering_ref[block] + part
+        bound_ref[j] = log * entering_ref[block] + part
     for o in range(n_ctx):
         for k in range(BR_PER):
             first = (1 + k) * rows

time: 103 us -> 103 us (level)
  no operation moved by 1% of the time
where the time goes in v9:
time: 103 us; the launch traced here: 102 us
  starting transfers between devices  35.2 us (34%)
  waiting for transfers between devices  26.9 us (26%)
  Pallas kernels  17.9 us (17%)
  blocking collectives  14.9 us (14%)
  local copies, waits for them, and re-layouts  4.57 us (4%)
  other arithmetic  1.55 us (2%)
  between operations  1.45 us (1%)
    pallas_call x9, Pallas kernels, call(): pl.pallas_call(kernel, grid=(1,) if grid else (), in_specs=[where(i < sme...  17.9 us
    all_to_all x1, waiting for transfers between devices, body(): got = lax.all_to_all(sent, 'ctx', 0, 0, tiled=True)  17.4 us
    all_to_all x1, blocking collectives, body(): squares = lax.all_to_all(squares, 'tp', 0, 0, tiled=True)  14.9 us
    all_to_all x1, starting transfers between devices, body(): lax.all_to_all(spread, 'tp', 0, 0, tiled=True).reshape(length, 2 * width)  11.8 us
    all_to_all x1, starting transfers between devices, body(): got = lax.all_to_all(sent, 'ctx', 0, 0, tiled=True)  11.3 us
    all_to_all x1, starting transfers between devices, body(): back = lax.all_to_all(back, 'ctx', 0, 0, tiled=True)  8.81 us
    all_to_all x1, waiting for transfers between devices, body(): back = lax.all_to_all(back, 'ctx', 0, 0, tiled=True)  6.01 us
    all_to_all x1, waiting for transfers between devices, body(): lax.all_to_all(spread, 'tp', 0, 0, tiled=True).reshape(length, 2 * width)  3.5 us
  transfers between devices with their start and end apart: 4, of which 3 were waited for; matrix products, arithmetic and copies ran while one was open for 2% of the time, Pallas kernels for 10%

profile of v9, /device:TPU:1, one launch (start us, length us, event | category | flops | bytes accessed | tf_op | source)
XLA Modules:
  0.0 102.4 jit_solution(7951376797092788693)
XLA Ops:
  0.6 0.7 pad_maximum_fusion.3
  1.3 0.7 broadcast_in_dim.95
  2.1 11.8 %all-to-all-start.1 = ((bf16[16,16,512]{2,1,0:T(8,128)(2,1)}), bf16[16,16,512]{2,1,0:T(8,128)(2,1)S(1)}, u32[]{:S(2)}, u32[]{:S(2)}) async-start(bf16[16,16,512]{2,1,0:T(8,128)(2,1)} %broadcast_in_dim.95), calls=%async_computation.1 | async-start | bytes 524288 | tf_op jit(solution)/shard_map/all_to_all | solution.py:536
  13.9 0.7 copy.34.rate_ref
  14.6 0.0 copy-start
  14.6 0.9 copy-done
  15.6 0.7 copy-done.10
  16.2 0.0 copy-start.11
  16.2 0.7 copy-done.11
  16.9 0.0 copy-start.12
  16.9 0.7 copy-done.12
  17.6 0.0 copy-start.1
  17.6 0.0 copy-start.5
  17.6 0.0 copy-start.7
  17.6 2.3 %shard_map.176 = (s32[94]{0:T(128)S(1)}, bf16[32,32,128]{2,1,0:T(8,128)(2,1)S(1)}, bf16[16,512]{1,0:T(8,128)(2,1)S(1)}) custom-call(s32[1]{0:T(128)} %bitcast.11.me_ref, s32[8]{0:T(128)} %bound_ref.1, s32[64]{0:T(128)S(1)} %copy-done.10, s32[64]{0:T(128)S(1)} %copy-done.11, s32[64]{0:T(128)S(1)} %copy-done.12, bf16[256,512]{1,0:T(8,128)(2,1)S(1)} %copy-done), custom_call_target="tpu_custom_call" | custom-call | flops 2000000000 | bytes 4000000 | tf_op jit(solution)/shard_map/pallas_call | solution.py:477
  19.9 0.0 copy-done.1
  19.9 0.0 copy-done.5
  19.9 0.0 copy-done.7
  19.9 0.0 copy-start.8
  19.9 2.2 %shard_map.177 = (bf16[256,512]{1,0:T(8,128)(2,1)S(1)}, f32[8,256]{1,0:T(8,128)S(1)}, f32[8,256]{1,0:T(8,128)S(1)}, bf16[3,256,512]{2,1,0:T(8,128)(2,1)S(1)}, f3...) custom-call(s32[94]{0:T(128)S(1)} %get-tuple-element.74.meta_ref, bf16[256,512]{1,0:T(8,128)(2,1)S(1)} %copy-done.1, ...), custom_call_target="tpu_custom_call" | custom-call | flops 2000000000 | bytes 4000000 | tf_op jit(solution)/shard_map/pallas_call | solution.py:477
  22.1 3.5 %all-to-all-done.1 = bf16[16,16,512]{2,1,0:T(8,128)(2,1)S(1)} async-done(((bf16[16,16,512]{2,1,0:T(8,128)(2,1)}), bf16[16,16,512]{2,1,0:T(8,128)(2,1)S(1)}, u32[]{:S(2)}, u32[]{:S(2)}) %all-to-all-start.1) | async-done | bytes 262176 | tf_op jit(solution)/shard_map/all_to_all | solution.py:536
  25.6 3.2 %collective-permute-start = (bf16[16,768]{1,0:T(8,128)(2,1)S(1)}, bf16[16,768]{1,0:T(8,128)(2,1)S(1)}, u32[]{:S(2)}, u32[]{:S(2)}) collective-permute-start(bf16[16,768]{1,0:T(8,128)(2,1)S(1)} %pad_maximum_fusion.2), channel_id=1, source_target_pairs={{0,16},{16,32},{32,48},{48,64},{64,80},{80,96},{96,112},{112,128},... | collective-permute-start | bytes 73736 | tf_op jit(solution)/shard_map/ppermute | solution.py:573
  28.8 0.0 copy-done.8
  28.8 1.4 %shard_map.178 = (f32[3,512,128]{2,1,0:T(8,128)S(1)}, bf16[32,48,128]{2,1,0:T(8,128)(2,1)S(1)}, bf16[256,256]{1,0:T(8,128)(2,1)S(1)}) custom-call(s32[94]{0:T(128)S(1)} %get-tuple-element.74.meta_ref, bf16[256,512]{1,0:T(8,128)(2,1)S(1)} %bitcast.27, bf16[4,256]{1,0:T(4,128)(2,1)S(1)} %copy-done.8, bf16[3,256,512]{2,1,0:T(8,128)(2,1)S(1)} %get-tuple-element.81.weighted_ref, ...), custom_call_target="tpu_custom_call" | custom-call | flops 2000000000 | bytes 4000000 | tf_op jit(solution)/shard_map/pallas_call | solution.py:477
  30.3 0.0 collective-permute-done.halo_ref
  30.3 2.0 %shard_map.179 = (bf16[32,96,128]{2,1,0:T(8,128)(2,1)}, bf16[256,128]{1,0:T(8,128)(2,1)S(1)}, bf16[256,128]{1,0:T(8,128)(2,1)S(1)}, bf16[16,512]{1,0:T(8,128)(2,1)S(1)}) custom-call(s32[94]{0:T(128)S(1)} %get-tuple-element.74.meta_ref, bf16[256,512]{1,0:T(8,128)(2,1)S(1)} %copy-done.1, bf16[16,768]{1,0:T(8,128)(2,1)S(1)} %collective-permute-done.halo_ref, ...), custom_call_target="tpu_custom_call" | custom-call | flops 2000000000 | bytes 4000000 | tf_op jit(solution)/shard_map/pallas_call | solution.py:477
  32.3 11.3 %all-to-all-start.2 = ((bf16[32,96,128]{2,1,0:T(8,128)(2,1)}), bf16[32,96,128]{2,1,0:T(8,128)(2,1)}, u32[]{:S(2)}, u32[]{:S(2)}) async-start(bf16[32,96,128]{2,1,0:T(8,128)(2,1)} %get-tuple-element.94), calls=%async_computation.2 | async-start | bytes 1572864 | tf_op jit(solution)/shard_map/all_to_all | solution.py:599
  43.6 0.0 copy-done.14
  43.7 0.2 convert_reduce_fusion
  43.8 0.6 reduce_max.9
  45.1 17.4 %all-to-all-done.2.got_ref = bf16[32,96,128]{2,1,0:T(8,128)(2,1)} async-done(((bf16[32,96,128]{2,1,0:T(8,128)(2,1)}), bf16[32,96,128]{2,1,0:T(8,128)(2,1)}, u32[]{:S(2)}, u32[]{:S(2)}) %all-to-all-start.2) | async-done | bytes 786464 | tf_op jit(solution)/shard_map/all_to_all | solution.py:599
  62.5 2.3 %conditional.1 = (bf16[32,48,128]{2,1,0:T(8,128)(2,1)}) conditional(s32[]{:T(128)} %convert_element_type.37, (s32[94]{0:T(128)S(1)}, bf16[32,96,128]{2,1,0:T(8,128)(2,1)}) %tuple.15, (s32[]{:T(128)}, s32[8]{0:T(128)S(1)}, s32[8]{0:T(128)S(1)}, s32[8]{0:T(128)S(1)}, s32[8]{0:T(128)S(1)}, /*index=5*/f32[8,256]{1,0:T(8,128)S(1)}, ...), branch_computations={%region_2.3_spmd, %region_3.6_spmd} | conditional | flops 2207683328 | bytes 13670660 | solution.py:626
  62.5 2.3 %branch_0_fun.1 = bf16[32,48,128]{2,1,0:T(8,128)(2,1)} custom-call(s32[94]{0:T(128)S(1)} %get-tuple-element.15.meta_ref, bf16[32,96,128]{2,1,0:T(8,128)(2,1)} %get-tuple-element.32.got_ref), custom_call_target="tpu_custom_call" | custom-call | flops 2000000000 | bytes 4000000 | tf_op jit(solution)/shard_map/cond/branch_0_fun/pallas_call | solution.py:477
  64.8 8.8 %all-to-all-start.3 = ((bf16[32,48,128]{2,1,0:T(8,128)(2,1)}), bf16[32,48,128]{2,1,0:T(8,128)(2,1)S(1)}, u32[]{:S(2)}, u32[]{:S(2)}) async-start(bf16[32,48,128]{2,1,0:T(8,128)(2,1)} %get-tuple-element.142), calls=%async_computation.3 | async-start | bytes 786432 | tf_op jit(solution)/shard_map/all_to_all | solution.py:627
  73.6 0.0 copy-done.13
  73.7 0.1 broadcast_in_dim.96
  73.7 0.1 broadcast_in_dim_reshape.3.skip_ref
  73.8 0.0 copy-done.2
  73.8 1.1 %shard_map.180 = (f32[256,512]{1,0:T(8,128)S(1)}, f32[256,512]{1,0:T(8,128)S(1)}) custom-call(bf16[256,512]{1,0:T(8,128)(2,1)S(1)} %get-tuple-element.75.xc_ref, bf16[16,512]{1,0:T(8,128)(2,1)S(1)} %get-tuple-element.87.xfirst_ref, bf16[256,128]{1,0:T(8,128)(2,1)S(1)} %get-tuple-element.88.b_ref, bf16[256,128]{1,0:T(8,128)(2,1)S(1)} %get-tuple-element.89.c_ref, ...), custom_call_target="tpu_custom_call" | custom-call | flops 2000000000 | bytes 4000000 | tf_op jit(solution)/shard_map/pallas_call | solution.py:477
  74.9 0.0 copy-done.3
  74.9 0.0 copy-done.4
  74.9 0.0 copy-done.6
  74.9 3.5 %shard_map.181 = (f32[256,512]{1,0:T(8,128)S(1)}, bf16[256,128]{1,0:T(8,128)(2,1)S(1)}, f32[256,512]{1,0:T(8,128)S(1)}) custom-call(s32[94]{0:T(128)S(1)} %get-tuple-element.74.meta_ref, bf16[256,512]{1,0:T(8,128)(2,1)S(1)} %copy-done.3, bf16[256,512]{1,0:T(8,128)(2,1)S(1)} %bitcast.29, bf16[32,96,128]{2,1,0:T(8,128)(2,1)} %all-to-all-done.2.got_ref, ...), custom_call_target="tpu_custom_call" | custom-call | flops 2000000000 | bytes 4000000 | tf_op jit(solution)/shard_map/pallas_call | solution.py:477
  78.4 6.0 %all-to-all-done.3.back_ref = bf16[32,48,128]{2,1,0:T(8,128)(2,1)S(1)} async-done(((bf16[32,48,128]{2,1,0:T(8,128)(2,1)}), bf16[32,48,128]{2,1,0:T(8,128)(2,1)S(1)}, u32[]{:S(2)}, u32[]{:S(2)}) %all-to-all-start.3) | async-done | bytes 393248 | tf_op jit(solution)/shard_map/all_to_all | solution.py:627
  84.4 1.5 %shard_map.182 = (f32[256,512]{1,0:T(8,128)S(1)}, f32[256,512]{1,0:T(8,128)S(1)}, f32[16,8,128]{2,1,0:T(8,128)S(1)}) custom-call(s32[94]{0:T(128)S(1)} %get-tuple-element.74.meta_ref, f32[256,512]{1,0:T(8,128)S(1)} %get-tuple-element.92.y_ref, f32[256,512]{1,0:T(8,128)S(1)} %get-tuple-element.93.scale_ref, bf16[256,128]{1,0:T(8,128)(2,1)S(1)} %get-tuple-element.89.c_ref, ...), custom_call_target="tpu_custom_call" | custom-call | flops 2000000000 | bytes 4000000 | tf_op jit(solution)/shard_map/pallas_call | solution.py:477
  85.9 14.9 %all_to_all.25.sq_ref = f32[16,8,128]{2,1,0:T(8,128)S(1)} all-to-all(f32[16,8,128]{2,1,0:T(8,128)S(1)} %get-tuple-element.98), channel_id=1, replica_groups=mesh['ctx'=32,'tp'=16] {'tp'}, dimensions={0} | all-to-all | bytes 131072 | tf_op jit(solution)/shard_map/all_to_all | solution.py:643
  100.8 0.0 copy-done.9
  100.8 1.6 %shard_map.183 = (bf16[256,512]{1,0:T(8,128)(2,1)}, bf16[256,512]{1,0:T(8,128)(2,1)}) custom-call(s32[94]{0:T(128)S(1)} %get-tuple-element.74.meta_ref, f32[16,8,128]{2,1,0:T(8,128)S(1)} %all_to_all.25.sq_ref, f32[256,512]{1,0:T(8,128)S(1)} %get-tuple-element.99.g_ref, f32[256,512]{1,0:T(8,128)S(1)} %get-tuple-element.100.bg_ref, f32[1,512]{1,0:T(1,128)S(1)} %bitcast.30), custom_call_target="tpu_custom_call" | custom-call | flops 2000000000 | bytes 4000000 | tf_op jit(solution)/shard_map/pallas_call | solution.py:477
  (12 shorter events, 0.0 us)
Async XLA Ops:
  2.1 23.5 %all-to-all-start.1 = ((bf16[16,16,512]{2,1,0:T(8,128)(2,1)}), bf16[16,16,512]{2,1,0:T(8,128)(2,1)S(1)}, u32[]{:S(2)}, u32[]{:S(2)}) async-start(bf16[16,16,512]{2,1,0:T(8,128)(2,1)} %broadcast_in_dim.95), calls=%async_computation.1 | async-start | bytes 524288 | tf_op jit(solution)/shard_map/all_to_all | solution.py:536
  14.6 0.9 copy-start
  15.6 0.7 copy-start.10
  16.2 0.7 copy-start.11
  16.9 0.7 copy-start.12
  17.6 2.3 %copy-start.1 = (bf16[256,512]{1,0:T(8,128)(2,1)S(1)}, bf16[256,512]{1,0:T(8,128)(2,1)}, u32[]{:S(2)}) copy-start(bf16[256,512]{1,0:T(8,128)(2,1)} %x_ref.6) | copy-start | bytes 786436
  17.6 2.4 %copy-start.5 = (f32[8,256]{1,0:T(8,128)S(1)}, f32[8,256]{1,0:T(8,128)}, u32[]{:S(2)}) copy-start(f32[8,256]{1,0:T(8,128)} %dt_ref.2) | copy-start | bytes 24580
  17.6 2.4 %copy-start.7 = (bf16[4,512]{1,0:T(4,128)(2,1)S(1)}, bf16[4,512]{1,0:T(4,128)(2,1)}, u32[]{:S(2)}) copy-start(bf16[4,512]{1,0:T(4,128)(2,1)} %xtaps_ref.3) | copy-start | bytes 12292
  19.9 8.9 %copy-start.8 = (bf16[4,256]{1,0:T(4,128)(2,1)S(1)}, bf16[4,256]{1,0:T(4,128)(2,1)}, u32[]{:S(2)}) copy-start(bf16[4,256]{1,0:T(4,128)(2,1)} %taps_ref.7) | copy-start | bytes 6148
  25.6 4.7 %collective-permute-start = (bf16[16,768]{1,0:T(8,128)(2,1)S(1)}, bf16[16,768]{1,0:T(8,128)(2,1)S(1)}, u32[]{:S(2)}, u32[]{:S(2)}) collective-permute-start(bf16[16,768]{1,0:T(8,128)(2,1)S(1)} %pad_maximum_fusion.2), channel_id=1, source_target_pairs={{0,16},{16,32},{32,48},{48,64},{64,80},{80,96},{96,112},{112,128},... | collective-permute-start | bytes 73736 | tf_op jit(solution)/shard_map/ppermute | solution.py:573
  32.3 11.3 %copy-start.14 = (s32[8]{0:T(128)S(1)}, s32[8]{0:T(128)}, u32[]{:S(2)}) copy-start(s32[8]{0:T(128)} %bound_ref.1) | copy-start | bytes 100
  32.3 30.2 %all-to-all-start.2 = ((bf16[32,96,128]{2,1,0:T(8,128)(2,1)}), bf16[32,96,128]{2,1,0:T(8,128)(2,1)}, u32[]{:S(2)}, u32[]{:S(2)}) async-start(bf16[32,96,128]{2,1,0:T(8,128)(2,1)} %get-tuple-element.94), calls=%async_computation.2 | async-start | bytes 1572864 | tf_op jit(solution)/shard_map/all_to_all | solution.py:599
  62.5 11.1 %copy-start.13 = (f32[8]{0:T(128)S(1)}, f32[8]{0:T(128)}, u32[]{:S(2)}) copy-start(f32[8]{0:T(128)} %param.30) | copy-start | bytes 100
  62.5 11.3 %copy-start.2 = (bf16[256,512]{1,0:T(8,128)(2,1)S(1)}, bf16[256,512]{1,0:T(8,128)(2,1)}, u32[]{:S(2)}) copy-start(bf16[256,512]{1,0:T(8,128)(2,1)} %z_ref.2) | copy-start | bytes 786436
  64.8 19.6 %all-to-all-start.3 = ((bf16[32,48,128]{2,1,0:T(8,128)(2,1)}), bf16[32,48,128]{2,1,0:T(8,128)(2,1)S(1)}, u32[]{:S(2)}, u32[]{:S(2)}) async-start(bf16[32,48,128]{2,1,0:T(8,128)(2,1)} %get-tuple-element.142), calls=%async_computation.3 | async-start | bytes 786432 | tf_op jit(solution)/shard_map/all_to_all | solution.py:627
  73.8 1.1 %copy-start.3 = (bf16[256,512]{1,0:T(8,128)(2,1)S(1)}, bf16[256,512]{1,0:T(8,128)(2,1)}, u32[]{:S(2)}) copy-start(bf16[256,512]{1,0:T(8,128)(2,1)} %x_ref.7) | copy-start | bytes 786436
  73.8 1.1 %copy-start.4 = (bf16[256,512]{1,0:T(8,128)(2,1)S(1)}, bf16[256,512]{1,0:T(8,128)(2,1)}, u32[]{:S(2)}) copy-start(bf16[256,512]{1,0:T(8,128)(2,1)} %z_ref.3) | copy-start | bytes 786436
  73.8 1.1 %copy-start.6 = (f32[8,256]{1,0:T(8,128)S(1)}, f32[8,256]{1,0:T(8,128)}, u32[]{:S(2)}) copy-start(f32[8,256]{1,0:T(8,128)} %dt_ref.3) | copy-start | bytes 24580
  84.4 16.4 %copy-start.9 = (f32[512]{0:T(512)S(1)}, f32[512]{0:T(512)}, u32[]{:S(2)}) copy-start(f32[512]{0:T(512)} %param.31) | copy-start | bytes 6148
